TPU v7x, 128 devices: a whole 4x4x4 slice. The times are simulated.
128 devices in a mesh: ctx: 16 (over z, x_hi, core), tp: 8 (over y, x_lo).
Axes of the slice: x: 4 (x_hi: 2, x_lo: 2; x = x_hi * 2 + x_lo), y: 4, z: 4, core: 2. Of those that a mesh axis runs over, the one named last changes fastest.
Arguments:
- att_query: bfloat16 [8192, 6144], P('ctx', 'tp'), may hold values from -8 to 8
- att_key: bfloat16 [8192, 1024], P('ctx', 'tp'), may hold values from -8 to 8
- att_value: bfloat16 [8192, 1024], P('ctx', 'tp'), may hold values from -140 to 140
- lh_query: bfloat16 [8192, 6144], P('ctx', 'tp'), may hold values from -6 to 6
- lh_key: bfloat16 [8192, 6144], P('ctx', 'tp'), may hold values from -36 to 36
- lh_value: bfloat16 [8192, 6144], P('ctx', 'tp'), may hold values from -36 to 36
- lh_step: float32 [8192, 48], P('ctx', 'tp'), may hold values from 0 to 1
- att_gain: float32 [6144], P('tp'), may hold values from 0.1 to 1.9
- lh_gain: float32 [6144], P('tp'), may hold values from 0.1 to 1.9
Outputs:
- mixed: bfloat16 [8192, 6144], P('ctx', 'tp')
All inputs are finite; a program needn't handle non-finite values.
Results may differ from a plain program's by a relative error of at most 0.012.
Values may be sent and summed in bfloat16 or wider, within the bound.
No kernel may reach another device: no remote copies, remote signals or barrier semaphores. Data moves between devices by JAX's collectives and lax.ppermute only.
A program may use at most 64 MiB of HBM per device.

v0:
```python
import math

import jax
import jax.numpy as jnp
from jax import lax
from jax.sharding import PartitionSpec as P

HD = 128


norm_eps = 1e-06
masked_score = -1e30
highest = lax.Precision.HIGHEST


def prefix(value, axis, join, neutral):
    count, mine = (lax.axis_size(axis), lax.axis_index(axis))
    pieces = jax.tree.map(lambda part: lax.all_gather(part, axis), value)
    running = jax.tree.map(
        lambda part, zero: jnp.full_like(part, 0) + jnp.asarray(zero, part.dtype), value, neutral
    )

    def lap(position, running):
        longer = join(running, jax.tree.map(lambda part: part[position], pieces))
        return jax.tree.map(lambda new, old: jnp.where(position < mine, new, old), longer, running)

    return lax.fori_loop(0, count - 1, lap, running)


def attend(queries, positions, key_shard, value_shard, kv_count):
    query_rows = queries.shape[0]
    group_size = queries.shape[1] // (kv_count * HD)
    grouped = queries.reshape(query_rows, kv_count, group_size, HD)
    last_position = jnp.max(positions)
    scale = 1.0 / math.sqrt(HD)
    initial = (
        jnp.full((kv_count, group_size, query_rows), masked_score, jnp.float32),
        jnp.zeros((kv_count, group_size, query_rows), jnp.float32),
        jnp.zeros((kv_count, group_size, query_rows, HD), jnp.float32),
    )
    key_piece = lax.all_gather(key_shard, "ctx", axis=0, tiled=True)
    value_piece = lax.all_gather(value_shard, "ctx", axis=0, tiled=True)
    piece_rows = key_piece.shape[0]
    block_rows = math.gcd(piece_rows, 512)

    def block_step(block_index, running):
        first_row = block_index * block_rows

        def visit_block(current):
            running_max, totals, numerator = current
            key_block = lax.dynamic_slice_in_dim(key_piece, first_row, block_rows, 0).reshape(
                block_rows, kv_count, HD
            )
            value_block = lax.dynamic_slice_in_dim(value_piece, first_row, block_rows, 0).reshape(
                block_rows, kv_count, HD
            )
            scores = (
                jnp.einsum("rkgd,skd->kgrs", grouped, key_block, preferred_element_type=jnp.float32)
                * scale
            )
            key_positions = first_row + jnp.arange(block_rows, dtype=jnp.int32)
            visible = key_positions[None, :] <= positions[:, None]
            scores = jnp.where(visible, scores, masked_score)
            new_max = jnp.maximum(running_max, jnp.max(scores, -1))
            rescale = jnp.exp(running_max - new_max)
            exponent = jnp.where(visible, jnp.exp(scores - new_max[..., None]), 0.0)
            weights = exponent.astype(jnp.bfloat16)
            numerator = numerator * rescale[..., None] + jnp.einsum(
                "kgrs,skd->kgrd", weights, value_block, preferred_element_type=jnp.float32
            )
            totals = totals * rescale + jnp.sum(exponent, -1)
            return (new_max, totals, numerator)

        def skip_block(current):
            return current

        return lax.cond(first_row <= last_position, visit_block, skip_block, running)

    running_max, totals, numerator = lax.fori_loop(0, piece_rows // block_rows, block_step, initial)
    result = numerator / totals[..., None]
    return (
        jnp.transpose(result, (2, 0, 1, 3))
        .reshape(query_rows, kv_count * group_size * HD)
        .astype(jnp.bfloat16)
    )


def scan_local(lh_query, lh_key, lh_value, lh_step):
    row_count = lh_query.shape[0]
    heads = lh_step.shape[1]
    query_bf16 = lh_query.reshape(row_count, heads, HD)
    query_f32 = query_bf16.astype(jnp.float32)
    key_rows = lh_key.astype(jnp.float32).reshape(row_count, heads, HD)
    key_rows = key_rows * lax.rsqrt(jnp.sum(key_rows * key_rows, -1, keepdims=True) + norm_eps)
    key_bf16 = key_rows.astype(jnp.bfloat16)
    value_rows = lh_value.astype(jnp.float32).reshape(row_count, heads, HD)
    log_decay = -jnp.log1p(lh_step)
    rates = lh_step / (1.0 + lh_step)
    span_rows = math.gcd(row_count, 512)
    causal = jnp.arange(span_rows)[:, None] >= jnp.arange(span_rows)[None, :]
    carried = jnp.zeros((heads, HD, HD), jnp.float32)
    cumulated = jnp.cumsum(log_decay, 0)
    log_gap = cumulated.T[:, :, None] - cumulated.T[:, None, :]
    decays = jnp.exp(jnp.where(causal[None], log_gap, masked_score))
    scores = jnp.einsum("thd,shd->hts", query_bf16, key_bf16, preferred_element_type=jnp.float32)
    weights = scores * decays * rates.T[:, None, :]
    local_part = jnp.einsum("hts,shd->thd", weights, value_rows, precision=highest)
    carried_part = (
        jnp.einsum("hvk,thk->thv", carried, query_f32, precision=highest)
        * jnp.exp(cumulated)[..., None]
    )
    outputs = local_part + carried_part
    end_log = cumulated[-1]
    tail_weight = jnp.exp(end_log[None, :] - cumulated) * rates
    carried = jnp.exp(end_log)[:, None, None] * carried + jnp.einsum(
        "shv,shk->hvk",
        value_rows * tail_weight[..., None],
        key_bf16.astype(jnp.float32),
        precision=highest,
    )
    return (outputs, carried, jnp.cumsum(log_decay, 0), query_f32)


def body(att_query, att_key, att_value, lh_query, lh_key, lh_value, lh_step, att_gain, lh_gain):
    row_count = att_query.shape[0]
    my_index = lax.axis_index("ctx")
    kv_count = att_key.shape[1] // HD
    own_rows = my_index * row_count + jnp.arange(row_count, dtype=jnp.int32)
    attention_out = attend(att_query, own_rows, att_key, att_value, kv_count)
    local_out, local_state, log_cumul, query_f32 = scan_local(lh_query, lh_key, lh_value, lh_step)
    end_log = log_cumul[-1]

    def combine(earlier, later):
        return (earlier[0] * later[0], later[0][:, None, None] * earlier[1] + later[1])

    carried = prefix(
        (jnp.exp(end_log), local_state),
        "ctx",
        combine,
        (jnp.ones_like(end_log), jnp.zeros_like(local_state)),
    )
    state_in = carried[1]
    lh_out = local_out + jnp.exp(log_cumul)[..., None] * jnp.einsum(
        "hvk,thk->thv", state_in, query_f32, precision=highest
    )
    attention_f32 = attention_out.astype(jnp.float32)
    squares = jnp.sum(attention_f32 * attention_f32, -1)
    squares = lax.psum(squares, "tp")
    feature_count = attention_out.shape[1] * lax.axis_size("tp")
    att_part = attention_f32 * lax.rsqrt(squares / feature_count + norm_eps)[:, None] * att_gain
    head_square = jnp.mean(lh_out * lh_out, -1, keepdims=True)
    lh_part = (lh_out * lax.rsqrt(head_square + norm_eps)).reshape(row_count, -1) * lh_gain
    return (att_part + lh_part).astype(jnp.bfloat16)


def solution(mesh):
    placed = (
        P("ctx", "tp"),
        P("ctx", "tp"),
        P("ctx", "tp"),
        P("ctx", "tp"),
        P("ctx", "tp"),
        P("ctx", "tp"),
        P("ctx", "tp"),
        P("tp"),
        P("tp"),
    )
    return jax.shard_map(
        body, mesh=mesh, in_specs=placed, out_specs=P("ctx", "tp"), check_vma=False
    )
```

profile of v0, /device:TPU:101, one launch (start us, length us, event | category | flops | bytes accessed | tf_op | source)
XLA Modules:
  0.0 303.0 jit_solution(16502241933013335860)
XLA Ops:
  8.8 1.8 reduce-window.6
  14.4 1.8 fusion.47
  18.2 18.9 %all-gather.1 = f32[16,1,6]{2,1,0:T(1,128)S(1)} all-gather(f32[1,1,6]{2,1,0:T(1,128)} %bitcast.143), channel_id=1, replica_groups=mesh['ctx'=16,'tp'=8] {'ctx'}, dimensions={0}, use_global_device_ids=true | all-gather | bytes 408 | tf_op jit(solution)/shard_map/all_gather | solution.py:18
  37.2 1.9 fusion.55
  39.1 3.7 %fusion.53 = f32[6,512,512]{2,1,0:T(8,128)} fusion(bf16[512,6,128]{0,2,1:T(8,128)(2,1)S(1)} %bitcast.127, bf16[512,6,128]{0,2,1:T(8,128)(2,1)S(1)} %bitcast.131, f32[512,6]{0,1:T(8,128)S(1)} %add_rsqrt_fusion.1), kind=kOutput, calls=%fused_computation.66 | convolution fusion | flops 403832832 | bytes 7876608 | tf_op jit(solution)/shard_map/thd,shd->hts/dot_general | solution.py:105
  42.8 13.5 %all-gather.6.cloned.1.call-done = bf16[8192,128]{1,0:T(8,128)(2,1)} async-done(((bf16[512,128]{1,0:T(8,128)(2,1)}), bf16[8192,128]{1,0:T(8,128)(2,1)}) %all-gather.6.cloned.1.call-update) | async-done | bytes 2097168 | tf_op jit(solution)/shard_map/all_gather | solution.py:41
  56.3 48.9 %all-gather.8.cloned.1.call-done = bf16[8192,128]{1,0:T(8,128)(2,1)} async-done(((bf16[512,128]{1,0:T(8,128)(2,1)}), bf16[8192,128]{1,0:T(8,128)(2,1)}) %all-gather.8.cloned.1.call-update) | async-done | bytes 2097168 | tf_op jit(solution)/shard_map/all_gather | solution.py:42
  106.4 141.8 %while.32 = (s32[]{:T(128)}, f32[1,6,512]{2,1,0:T(8,128)S(1)}, f32[1,6,512]{2,1,0:T(8,128)S(1)}, f32[1,6,512,128]{3,2,1,0:T(8,128)}, s32[]{:T(128)}, /*index=5*/...) while((s32[]{:T(128)}, f32[1,6,512]{2,1,0:T(8,128)S(1)}, ...), condition=%wide.region_6.7_spmd.clone, body=%wide.region_1.6_spmd.clone.sunk | while | flops 826812416 | bytes 24326464 | solution.py:79
  107.0 8.3 %conditional.3 = ((f32[1,6,512]{2,1,0:T(8,128)S(1)}, f32[1,6,512]{2,1,0:T(8,128)S(1)}, f32[1,6,512,128]{3,2,1,0:T(8,128)})) conditional(s32[]{:T(128)} %convert_element_type.67, (f32[1,6,512]{2,1,0:T(8,128)S(1)}, f32[1,6,512]{2,1,0:T(8,128)S(1)}, f32[1,6,512,128]{3,2,1,0:T(8,128)}) %tuple.83, (s32[]{:T(128)}, s32[]{:T(128)}, ...), branch_computations={%region_2.0_spmd, %region_3.5_spmd} | conditional | flops 826812416 | bytes 24324178 | solution.py:77
  107.3 2.1 fusion.2
  109.4 1.5 fusion.4
  111.0 4.4 %bitcast_add_fusion = f32[1,6,512,128]{3,2,1,0:T(8,128)} fusion(f32[1,6,512,128]{3,2,1,0:T(8,128)} %get-tuple-element.269, f32[512,512,6]{1,0,2:T(8,128)S(1)} %get-tuple-element.409, f32[6,512]{1,0:T(8,128)S(1)} %bitcast.133, pred[512,512]{0,1:T(8,128)(4,1)S(1)} %broadcast_compare_fusion, f32[6,512]{1,0:T(8,128)S(1)} %get-tuple-element.404, ...), kind=kOutput, calls=%fused_computation.9 | convolution fusion | flops 411303936 | bytes 9854980 | tf_op jit(solution)/shard_map/while/body/eval_jaxpr/cond/branch_1_fun/kgrs,skd->kgrd/dot_general | solution.py:68
  115.9 8.4 %conditional.3 = ((f32[1,6,512]{2,1,0:T(8,128)S(1)}, f32[1,6,512]{2,1,0:T(8,128)S(1)}, f32[1,6,512,128]{3,2,1,0:T(8,128)})) conditional(s32[]{:T(128)} %convert_element_type.67, (f32[1,6,512]{2,1,0:T(8,128)S(1)}, f32[1,6,512]{2,1,0:T(8,128)S(1)}, f32[1,6,512,128]{3,2,1,0:T(8,128)}) %tuple.83, (s32[]{:T(128)}, s32[]{:T(128)}, ...), branch_computations={%region_2.0_spmd, %region_3.5_spmd} | conditional | flops 826812416 | bytes 24324178 | solution.py:77
  116.1 2.1 fusion.2
  118.3 1.5 fusion.4
  119.8 4.4 %bitcast_add_fusion = f32[1,6,512,128]{3,2,1,0:T(8,128)} fusion(f32[1,6,512,128]{3,2,1,0:T(8,128)} %get-tuple-element.269, f32[512,512,6]{1,0,2:T(8,128)S(1)} %get-tuple-element.409, f32[6,512]{1,0:T(8,128)S(1)} %bitcast.133, pred[512,512]{0,1:T(8,128)(4,1)S(1)} %broadcast_compare_fusion, f32[6,512]{1,0:T(8,128)S(1)} %get-tuple-element.404, ...), kind=kOutput, calls=%fused_computation.9 | convolution fusion | flops 411303936 | bytes 9854980 | tf_op jit(solution)/shard_map/while/body/eval_jaxpr/cond/branch_1_fun/kgrs,skd->kgrd/dot_general | solution.py:68
  124.8 8.3 %conditional.3 = ((f32[1,6,512]{2,1,0:T(8,128)S(1)}, f32[1,6,512]{2,1,0:T(8,128)S(1)}, f32[1,6,512,128]{3,2,1,0:T(8,128)})) conditional(s32[]{:T(128)} %convert_element_type.67, (f32[1,6,512]{2,1,0:T(8,128)S(1)}, f32[1,6,512]{2,1,0:T(8,128)S(1)}, f32[1,6,512,128]{3,2,1,0:T(8,128)}) %tuple.83, (s32[]{:T(128)}, s32[]{:T(128)}, ...), branch_computations={%region_2.0_spmd, %region_3.5_spmd} | conditional | flops 826812416 | bytes 24324178 | solution.py:77
  125.1 2.1 fusion.2
  127.2 1.5 fusion.4
  128.8 4.3 %bitcast_add_fusion = f32[1,6,512,128]{3,2,1,0:T(8,128)} fusion(f32[1,6,512,128]{3,2,1,0:T(8,128)} %get-tuple-element.269, f32[512,512,6]{1,0,2:T(8,128)S(1)} %get-tuple-element.409, f32[6,512]{1,0:T(8,128)S(1)} %bitcast.133, pred[512,512]{0,1:T(8,128)(4,1)S(1)} %broadcast_compare_fusion, f32[6,512]{1,0:T(8,128)S(1)} %get-tuple-element.404, ...), kind=kOutput, calls=%fused_computation.9 | convolution fusion | flops 411303936 | bytes 9854980 | tf_op jit(solution)/shard_map/while/body/eval_jaxpr/cond/branch_1_fun/kgrs,skd->kgrd/dot_general | solution.py:68
  133.7 8.3 %conditional.3 = ((f32[1,6,512]{2,1,0:T(8,128)S(1)}, f32[1,6,512]{2,1,0:T(8,128)S(1)}, f32[1,6,512,128]{3,2,1,0:T(8,128)})) conditional(s32[]{:T(128)} %convert_element_type.67, (f32[1,6,512]{2,1,0:T(8,128)S(1)}, f32[1,6,512]{2,1,0:T(8,128)S(1)}, f32[1,6,512,128]{3,2,1,0:T(8,128)}) %tuple.83, (s32[]{:T(128)}, s32[]{:T(128)}, ...), branch_computations={%region_2.0_spmd, %region_3.5_spmd} | conditional | flops 826812416 | bytes 24324178 | solution.py:77
  133.9 2.1 fusion.2
  136.1 1.5 fusion.4
  137.6 4.3 %bitcast_add_fusion = f32[1,6,512,128]{3,2,1,0:T(8,128)} fusion(f32[1,6,512,128]{3,2,1,0:T(8,128)} %get-tuple-element.269, f32[512,512,6]{1,0,2:T(8,128)S(1)} %get-tuple-element.409, f32[6,512]{1,0:T(8,128)S(1)} %bitcast.133, pred[512,512]{0,1:T(8,128)(4,1)S(1)} %broadcast_compare_fusion, f32[6,512]{1,0:T(8,128)S(1)} %get-tuple-element.404, ...), kind=kOutput, calls=%fused_computation.9 | convolution fusion | flops 411303936 | bytes 9854980 | tf_op jit(solution)/shard_map/while/body/eval_jaxpr/cond/branch_1_fun/kgrs,skd->kgrd/dot_general | solution.py:68
  142.5 8.3 %conditional.3 = ((f32[1,6,512]{2,1,0:T(8,128)S(1)}, f32[1,6,512]{2,1,0:T(8,128)S(1)}, f32[1,6,512,128]{3,2,1,0:T(8,128)})) conditional(s32[]{:T(128)} %convert_element_type.67, (f32[1,6,512]{2,1,0:T(8,128)S(1)}, f32[1,6,512]{2,1,0:T(8,128)S(1)}, f32[1,6,512,128]{3,2,1,0:T(8,128)}) %tuple.83, (s32[]{:T(128)}, s32[]{:T(128)}, ...), branch_computations={%region_2.0_spmd, %region_3.5_spmd} | conditional | flops 826812416 | bytes 24324178 | solution.py:77
  142.8 2.1 fusion.2
  146.5 4.4 %bitcast_add_fusion = f32[1,6,512,128]{3,2,1,0:T(8,128)} fusion(f32[1,6,512,128]{3,2,1,0:T(8,128)} %get-tuple-element.269, f32[512,512,6]{1,0,2:T(8,128)S(1)} %get-tuple-element.409, f32[6,512]{1,0:T(8,128)S(1)} %bitcast.133, pred[512,512]{0,1:T(8,128)(4,1)S(1)} %broadcast_compare_fusion, f32[6,512]{1,0:T(8,128)S(1)} %get-tuple-element.404, ...), kind=kOutput, calls=%fused_computation.9 | convolution fusion | flops 411303936 | bytes 9854980 | tf_op jit(solution)/shard_map/while/body/eval_jaxpr/cond/branch_1_fun/kgrs,skd->kgrd/dot_general | solution.py:68
  151.5 8.3 %conditional.3 = ((f32[1,6,512]{2,1,0:T(8,128)S(1)}, f32[1,6,512]{2,1,0:T(8,128)S(1)}, f32[1,6,512,128]{3,2,1,0:T(8,128)})) conditional(s32[]{:T(128)} %convert_element_type.67, (f32[1,6,512]{2,1,0:T(8,128)S(1)}, f32[1,6,512]{2,1,0:T(8,128)S(1)}, f32[1,6,512,128]{3,2,1,0:T(8,128)}) %tuple.83, (s32[]{:T(128)}, s32[]{:T(128)}, ...), branch_computations={%region_2.0_spmd, %region_3.5_spmd} | conditional | flops 826812416 | bytes 24324178 | solution.py:77
  151.7 2.1 fusion.2
  155.4 4.3 %bitcast_add_fusion = f32[1,6,512,128]{3,2,1,0:T(8,128)} fusion(f32[1,6,512,128]{3,2,1,0:T(8,128)} %get-tuple-element.269, f32[512,512,6]{1,0,2:T(8,128)S(1)} %get-tuple-element.409, f32[6,512]{1,0:T(8,128)S(1)} %bitcast.133, pred[512,512]{0,1:T(8,128)(4,1)S(1)} %broadcast_compare_fusion, f32[6,512]{1,0:T(8,128)S(1)} %get-tuple-element.404, ...), kind=kOutput, calls=%fused_computation.9 | convolution fusion | flops 411303936 | bytes 9854980 | tf_op jit(solution)/shard_map/while/body/eval_jaxpr/cond/branch_1_fun/kgrs,skd->kgrd/dot_general | solution.py:68
  160.3 8.3 %conditional.3 = ((f32[1,6,512]{2,1,0:T(8,128)S(1)}, f32[1,6,512]{2,1,0:T(8,128)S(1)}, f32[1,6,512,128]{3,2,1,0:T(8,128)})) conditional(s32[]{:T(128)} %convert_element_type.67, (f32[1,6,512]{2,1,0:T(8,128)S(1)}, f32[1,6,512]{2,1,0:T(8,128)S(1)}, f32[1,6,512,128]{3,2,1,0:T(8,128)}) %tuple.83, (s32[]{:T(128)}, s32[]{:T(128)}, ...), branch_computations={%region_2.0_spmd, %region_3.5_spmd} | conditional | flops 826812416 | bytes 24324178 | solution.py:77
  160.6 2.1 fusion.2
  164.2 4.3 %bitcast_add_fusion = f32[1,6,512,128]{3,2,1,0:T(8,128)} fusion(f32[1,6,512,128]{3,2,1,0:T(8,128)} %get-tuple-element.269, f32[512,512,6]{1,0,2:T(8,128)S(1)} %get-tuple-element.409, f32[6,512]{1,0:T(8,128)S(1)} %bitcast.133, pred[512,512]{0,1:T(8,128)(4,1)S(1)} %broadcast_compare_fusion, f32[6,512]{1,0:T(8,128)S(1)} %get-tuple-element.404, ...), kind=kOutput, calls=%fused_computation.9 | convolution fusion | flops 411303936 | bytes 9854980 | tf_op jit(solution)/shard_map/while/body/eval_jaxpr/cond/branch_1_fun/kgrs,skd->kgrd/dot_general | solution.py:68
  169.2 8.3 %conditional.3 = ((f32[1,6,512]{2,1,0:T(8,128)S(1)}, f32[1,6,512]{2,1,0:T(8,128)S(1)}, f32[1,6,512,128]{3,2,1,0:T(8,128)})) conditional(s32[]{:T(128)} %convert_element_type.67, (f32[1,6,512]{2,1,0:T(8,128)S(1)}, f32[1,6,512]{2,1,0:T(8,128)S(1)}, f32[1,6,512,128]{3,2,1,0:T(8,128)}) %tuple.83, (s32[]{:T(128)}, s32[]{:T(128)}, ...), branch_computations={%region_2.0_spmd, %region_3.5_spmd} | conditional | flops 826812416 | bytes 24324178 | solution.py:77
  169.4 2.1 fusion.2
  173.1 4.3 %bitcast_add_fusion = f32[1,6,512,128]{3,2,1,0:T(8,128)} fusion(f32[1,6,512,128]{3,2,1,0:T(8,128)} %get-tuple-element.269, f32[512,512,6]{1,0,2:T(8,128)S(1)} %get-tuple-element.409, f32[6,512]{1,0:T(8,128)S(1)} %bitcast.133, pred[512,512]{0,1:T(8,128)(4,1)S(1)} %broadcast_compare_fusion, f32[6,512]{1,0:T(8,128)S(1)} %get-tuple-element.404, ...), kind=kOutput, calls=%fused_computation.9 | convolution fusion | flops 411303936 | bytes 9854980 | tf_op jit(solution)/shard_map/while/body/eval_jaxpr/cond/branch_1_fun/kgrs,skd->kgrd/dot_general | solution.py:68
  178.0 8.3 %conditional.3 = ((f32[1,6,512]{2,1,0:T(8,128)S(1)}, f32[1,6,512]{2,1,0:T(8,128)S(1)}, f32[1,6,512,128]{3,2,1,0:T(8,128)})) conditional(s32[]{:T(128)} %convert_element_type.67, (f32[1,6,512]{2,1,0:T(8,128)S(1)}, f32[1,6,512]{2,1,0:T(8,128)S(1)}, f32[1,6,512,128]{3,2,1,0:T(8,128)}) %tuple.83, (s32[]{:T(128)}, s32[]{:T(128)}, ...), branch_computations={%region_2.0_spmd, %region_3.5_spmd} | conditional | flops 826812416 | bytes 24324178 | solution.py:77
  178.3 2.1 fusion.2
  181.9 4.3 %bitcast_add_fusion = f32[1,6,512,128]{3,2,1,0:T(8,128)} fusion(f32[1,6,512,128]{3,2,1,0:T(8,128)} %get-tuple-element.269, f32[512,512,6]{1,0,2:T(8,128)S(1)} %get-tuple-element.409, f32[6,512]{1,0:T(8,128)S(1)} %bitcast.133, pred[512,512]{0,1:T(8,128)(4,1)S(1)} %broadcast_compare_fusion, f32[6,512]{1,0:T(8,128)S(1)} %get-tuple-element.404, ...), kind=kOutput, calls=%fused_computation.9 | convolution fusion | flops 411303936 | bytes 9854980 | tf_op jit(solution)/shard_map/while/body/eval_jaxpr/cond/branch_1_fun/kgrs,skd->kgrd/dot_general | solution.py:68
  186.9 8.3 %conditional.3 = ((f32[1,6,512]{2,1,0:T(8,128)S(1)}, f32[1,6,512]{2,1,0:T(8,128)S(1)}, f32[1,6,512,128]{3,2,1,0:T(8,128)})) conditional(s32[]{:T(128)} %convert_element_type.67, (f32[1,6,512]{2,1,0:T(8,128)S(1)}, f32[1,6,512]{2,1,0:T(8,128)S(1)}, f32[1,6,512,128]{3,2,1,0:T(8,128)}) %tuple.83, (s32[]{:T(128)}, s32[]{:T(128)}, ...), branch_computations={%region_2.0_spmd, %region_3.5_spmd} | conditional | flops 826812416 | bytes 24324178 | solution.py:77
  187.1 2.1 fusion.2
  190.8 4.3 %bitcast_add_fusion = f32[1,6,512,128]{3,2,1,0:T(8,128)} fusion(f32[1,6,512,128]{3,2,1,0:T(8,128)} %get-tuple-element.269, f32[512,512,6]{1,0,2:T(8,128)S(1)} %get-tuple-element.409, f32[6,512]{1,0:T(8,128)S(1)} %bitcast.133, pred[512,512]{0,1:T(8,128)(4,1)S(1)} %broadcast_compare_fusion, f32[6,512]{1,0:T(8,128)S(1)} %get-tuple-element.404, ...), kind=kOutput, calls=%fused_computation.9 | convolution fusion | flops 411303936 | bytes 9854980 | tf_op jit(solution)/shard_map/while/body/eval_jaxpr/cond/branch_1_fun/kgrs,skd->kgrd/dot_general | solution.py:68
  195.7 8.3 %conditional.3 = ((f32[1,6,512]{2,1,0:T(8,128)S(1)}, f32[1,6,512]{2,1,0:T(8,128)S(1)}, f32[1,6,512,128]{3,2,1,0:T(8,128)})) conditional(s32[]{:T(128)} %convert_element_type.67, (f32[1,6,512]{2,1,0:T(8,128)S(1)}, f32[1,6,512]{2,1,0:T(8,128)S(1)}, f32[1,6,512,128]{3,2,1,0:T(8,128)}) %tuple.83, (s32[]{:T(128)}, s32[]{:T(128)}, ...), branch_computations={%region_2.0_spmd, %region_3.5_spmd} | conditional | flops 826812416 | bytes 24324178 | solution.py:77
  196.0 2.1 fusion.2
  199.6 4.3 %bitcast_add_fusion = f32[1,6,512,128]{3,2,1,0:T(8,128)} fusion(f32[1,6,512,128]{3,2,1,0:T(8,128)} %get-tuple-element.269, f32[512,512,6]{1,0,2:T(8,128)S(1)} %get-tuple-element.409, f32[6,512]{1,0:T(8,128)S(1)} %bitcast.133, pred[512,512]{0,1:T(8,128)(4,1)S(1)} %broadcast_compare_fusion, f32[6,512]{1,0:T(8,128)S(1)} %get-tuple-element.404, ...), kind=kOutput, calls=%fused_computation.9 | convolution fusion | flops 411303936 | bytes 9854980 | tf_op jit(solution)/shard_map/while/body/eval_jaxpr/cond/branch_1_fun/kgrs,skd->kgrd/dot_general | solution.py:68
  204.6 8.3 %conditional.3 = ((f32[1,6,512]{2,1,0:T(8,128)S(1)}, f32[1,6,512]{2,1,0:T(8,128)S(1)}, f32[1,6,512,128]{3,2,1,0:T(8,128)})) conditional(s32[]{:T(128)} %convert_element_type.67, (f32[1,6,512]{2,1,0:T(8,128)S(1)}, f32[1,6,512]{2,1,0:T(8,128)S(1)}, f32[1,6,512,128]{3,2,1,0:T(8,128)}) %tuple.83, (s32[]{:T(128)}, s32[]{:T(128)}, ...), branch_computations={%region_2.0_spmd, %region_3.5_spmd} | conditional | flops 826812416 | bytes 24324178 | solution.py:77
  204.8 2.1 fusion.2
  208.5 4.3 %bitcast_add_fusion = f32[1,6,512,128]{3,2,1,0:T(8,128)} fusion(f32[1,6,512,128]{3,2,1,0:T(8,128)} %get-tuple-element.269, f32[512,512,6]{1,0,2:T(8,128)S(1)} %get-tuple-element.409, f32[6,512]{1,0:T(8,128)S(1)} %bitcast.133, pred[512,512]{0,1:T(8,128)(4,1)S(1)} %broadcast_compare_fusion, f32[6,512]{1,0:T(8,128)S(1)} %get-tuple-element.404, ...), kind=kOutput, calls=%fused_computation.9 | convolution fusion | flops 411303936 | bytes 9854980 | tf_op jit(solution)/shard_map/while/body/eval_jaxpr/cond/branch_1_fun/kgrs,skd->kgrd/dot_general | solution.py:68
  213.4 8.3 %conditional.3 = ((f32[1,6,512]{2,1,0:T(8,128)S(1)}, f32[1,6,512]{2,1,0:T(8,128)S(1)}, f32[1,6,512,128]{3,2,1,0:T(8,128)})) conditional(s32[]{:T(128)} %convert_element_type.67, (f32[1,6,512]{2,1,0:T(8,128)S(1)}, f32[1,6,512]{2,1,0:T(8,128)S(1)}, f32[1,6,512,128]{3,2,1,0:T(8,128)}) %tuple.83, (s32[]{:T(128)}, s32[]{:T(128)}, ...), branch_computations={%region_2.0_spmd, %region_3.5_spmd} | conditional | flops 826812416 | bytes 24324178 | solution.py:77
  213.7 2.1 fusion.2
  217.3 4.3 %bitcast_add_fusion = f32[1,6,512,128]{3,2,1,0:T(8,128)} fusion(f32[1,6,512,128]{3,2,1,0:T(8,128)} %get-tuple-element.269, f32[512,512,6]{1,0,2:T(8,128)S(1)} %get-tuple-element.409, f32[6,512]{1,0:T(8,128)S(1)} %bitcast.133, pred[512,512]{0,1:T(8,128)(4,1)S(1)} %broadcast_compare_fusion, f32[6,512]{1,0:T(8,128)S(1)} %get-tuple-element.404, ...), kind=kOutput, calls=%fused_computation.9 | convolution fusion | flops 411303936 | bytes 9854980 | tf_op jit(solution)/shard_map/while/body/eval_jaxpr/cond/branch_1_fun/kgrs,skd->kgrd/dot_general | solution.py:68
  222.3 8.3 %conditional.3 = ((f32[1,6,512]{2,1,0:T(8,128)S(1)}, f32[1,6,512]{2,1,0:T(8,128)S(1)}, f32[1,6,512,128]{3,2,1,0:T(8,128)})) conditional(s32[]{:T(128)} %convert_element_type.67, (f32[1,6,512]{2,1,0:T(8,128)S(1)}, f32[1,6,512]{2,1,0:T(8,128)S(1)}, f32[1,6,512,128]{3,2,1,0:T(8,128)}) %tuple.83, (s32[]{:T(128)}, s32[]{:T(128)}, ...), branch_computations={%region_2.0_spmd, %region_3.5_spmd} | conditional | flops 826812416 | bytes 24324178 | solution.py:77
  222.5 2.1 fusion.2
  226.2 4.3 %bitcast_add_fusion = f32[1,6,512,128]{3,2,1,0:T(8,128)} fusion(f32[1,6,512,128]{3,2,1,0:T(8,128)} %get-tuple-element.269, f32[512,512,6]{1,0,2:T(8,128)S(1)} %get-tuple-element.409, f32[6,512]{1,0:T(8,128)S(1)} %bitcast.133, pred[512,512]{0,1:T(8,128)(4,1)S(1)} %broadcast_compare_fusion, f32[6,512]{1,0:T(8,128)S(1)} %get-tuple-element.404, ...), kind=kOutput, calls=%fused_computation.9 | convolution fusion | flops 411303936 | bytes 9854980 | tf_op jit(solution)/shard_map/while/body/eval_jaxpr/cond/branch_1_fun/kgrs,skd->kgrd/dot_general | solution.py:68
  231.1 8.3 %conditional.3 = ((f32[1,6,512]{2,1,0:T(8,128)S(1)}, f32[1,6,512]{2,1,0:T(8,128)S(1)}, f32[1,6,512,128]{3,2,1,0:T(8,128)})) conditional(s32[]{:T(128)} %convert_element_type.67, (f32[1,6,512]{2,1,0:T(8,128)S(1)}, f32[1,6,512]{2,1,0:T(8,128)S(1)}, f32[1,6,512,128]{3,2,1,0:T(8,128)}) %tuple.83, (s32[]{:T(128)}, s32[]{:T(128)}, ...), branch_computations={%region_2.0_spmd, %region_3.5_spmd} | conditional | flops 826812416 | bytes 24324178 | solution.py:77
  231.4 2.1 fusion.2
  235.0 4.3 %bitcast_add_fusion = f32[1,6,512,128]{3,2,1,0:T(8,128)} fusion(f32[1,6,512,128]{3,2,1,0:T(8,128)} %get-tuple-element.269, f32[512,512,6]{1,0,2:T(8,128)S(1)} %get-tuple-element.409, f32[6,512]{1,0:T(8,128)S(1)} %bitcast.133, pred[512,512]{0,1:T(8,128)(4,1)S(1)} %broadcast_compare_fusion, f32[6,512]{1,0:T(8,128)S(1)} %get-tuple-element.404, ...), kind=kOutput, calls=%fused_computation.9 | convolution fusion | flops 411303936 | bytes 9854980 | tf_op jit(solution)/shard_map/while/body/eval_jaxpr/cond/branch_1_fun/kgrs,skd->kgrd/dot_general | solution.py:68
  240.0 8.3 %conditional.3 = ((f32[1,6,512]{2,1,0:T(8,128)S(1)}, f32[1,6,512]{2,1,0:T(8,128)S(1)}, f32[1,6,512,128]{3,2,1,0:T(8,128)})) conditional(s32[]{:T(128)} %convert_element_type.67, (f32[1,6,512]{2,1,0:T(8,128)S(1)}, f32[1,6,512]{2,1,0:T(8,128)S(1)}, f32[1,6,512,128]{3,2,1,0:T(8,128)}) %tuple.83, (s32[]{:T(128)}, s32[]{:T(128)}, ...), branch_computations={%region_2.0_spmd, %region_3.5_spmd} | conditional | flops 826812416 | bytes 24324178 | solution.py:77
  240.2 2.1 fusion.2
  243.9 4.3 %bitcast_add_fusion = f32[1,6,512,128]{3,2,1,0:T(8,128)} fusion(f32[1,6,512,128]{3,2,1,0:T(8,128)} %get-tuple-element.269, f32[512,512,6]{1,0,2:T(8,128)S(1)} %get-tuple-element.409, f32[6,512]{1,0:T(8,128)S(1)} %bitcast.133, pred[512,512]{0,1:T(8,128)(4,1)S(1)} %broadcast_compare_fusion, f32[6,512]{1,0:T(8,128)S(1)} %get-tuple-element.404, ...), kind=kOutput, calls=%fused_computation.9 | convolution fusion | flops 411303936 | bytes 9854980 | tf_op jit(solution)/shard_map/while/body/eval_jaxpr/cond/branch_1_fun/kgrs,skd->kgrd/dot_general | solution.py:68
  248.2 1.9 copy.40
  251.6 16.7 %psum.7 = f32[512]{0:T(512)S(1)} all-reduce(f32[512]{0:T(512)S(1)} %get-tuple-element.406), channel_id=1, replica_groups=mesh['ctx'=16,'tp'=8] {'tp'}, use_global_device_ids=true, to_apply=%region_8.9 | all-reduce | flops 512 | bytes 4096 | tf_op jit(solution)/shard_map/psum | solution.py:148
  268.2 17.4 %while.33 = (s32[]{:T(128)}, f32[6,128,128]{2,1,0:T(8,128)S(1)}, s32[]{:T(128)}, f32[16,6]{1,0:T(8,128)S(1)}, f32[16,6,128,128]{3,2,1,0:T(8,128)}, /*index=5*/s32[]{:T(128)}, s32[]{:T(128)}) while((s32[]{:T(128)}, f32[6,128,128]{2,1,0:T(8,128)S(1)}, s32[]{:T(128)}, f32[16,6]{1,0:T(8,128)S(1)}, f32[16,6,128,128]{3,2,1,0:T(8,128)}, ...), condition=%wide.region_13.14_spmd.clone, body=%wide.region_12.13_spmd.clone.sunk | while | flops 393220 | bytes 1179833 | solution.py:27
  287.2 6.3 %multiply_reduce_fusion = (f32[512,6]{0,1:T(8,128)S(1)}, f32[512,6,128]{0,2,1:T(8,128)S(1)}) fusion(f32[6,128,512]{2,1,0:T(8,128)S(1)} %fusion.63, f32[512,6]{0,1:T(8,128)S(1)} %copy-done.11, f32[6,128,512]{2,1,0:T(8,128)S(1)} %copy-done.1, bf16[512,6,128]{0,2,1:T(8,128)(2,1)S(1)} %bitcast.137, f32[6,512,512]{2,1,0:T(8,128)} %fusion.53, ...), kind=kOutput, calls=%fused_computation.55 | convolution fusion | flops 2424566784 | bytes 12107776 | tf_op jit(solution)/shard_map/hts,shd->thd/dot_general | solution.py:107
  (205 shorter events, 54.3 us)
Async XLA Ops:
  6.5 5.9 %copy-start.2 = (bf16[512,768]{1,0:T(8,128)(2,1)S(1)}, bf16[512,768]{1,0:T(8,128)(2,1)}, u32[]{:S(2)}) copy-start(bf16[512,768]{1,0:T(8,128)(2,1)} %param.19) | copy-start | bytes 2359300
  6.5 49.8 %all-gather.6.cloned.1.call-start = ((), (), s32[]{:S(2)}) async-start(), calls=%async_computation | async-start | bytes 2228224 | tf_op jit(solution)/shard_map/all_gather | solution.py:41
  7.3 97.9 %all-gather.8.cloned.1.call-start = ((), (), s32[]{:S(2)}) async-start(), calls=%async_computation.1 | async-start | bytes 2228224 | tf_op jit(solution)/shard_map/all_gather | solution.py:42
  8.0 260.2 %all-gather.10.cloned.1.call-start = ((), (), s32[]{:S(2)}) async-start(), calls=%async_computation.2 | async-start | bytes 6684672 | tf_op jit(solution)/shard_map/all_gather | solution.py:18
  11.0 1.7 copy-start.8
  12.5 3.7 %copy-start.5 = (bf16[512,768]{0,1:T(8,128)(2,1)}, bf16[512,768]{0,1:T(8,128)(2,1)S(1)}, u32[]{:S(2)}) copy-start(bf16[512,768]{0,1:T(8,128)(2,1)S(1)} %copy.47) | copy-start | bytes 2359300
  12.5 1.2 copy-start.7
  13.5 3.3 %copy-start.3 = (bf16[512,768]{1,0:T(8,128)(2,1)S(1)}, bf16[512,768]{1,0:T(8,128)(2,1)}, u32[]{:S(2)}) copy-start(bf16[512,768]{1,0:T(8,128)(2,1)} %param.15) | copy-start | bytes 2359300
  16.8 1.1 copy-start.4
  285.6 1.4 copy-start.1
  285.6 1.6 copy-start.6
  285.6 1.6 copy-start.9
  285.6 1.6 copy-start.10
  285.6 1.6 copy-start.11
  293.5 1.4 copy-start
  293.6 1.4 copy-start.12
  293.6 1.4 copy-start.13
Sparse Core Ops, SparseCore 0:
  9.8 46.4 all-gather.5
  58.8 46.3 all-gather.7
  107.6 61.3 all-gather.9
where the time goes:
time: 305 us; the launch traced here: 303 us
  matrix products  118 us (39%)
  waiting for transfers between devices  63.8 us (21%)
  other arithmetic  51.1 us (17%)
  blocking collectives  35.5 us (12%)
  between operations  13.4 us (4%)
  loops' own time  10.9 us (4%)
  local copies, waits for them, and re-layouts  10.7 us (4%)
    dot_general x16, matrix products, visit_block(): jnp.einsum('kgrs,skd->kgrd', weights, value_block, preferred_element_type...  69.7 us
    all_gather x1, waiting for transfers between devices, attend(): value_piece = lax.all_gather(value_shard, 'ctx', axis=0, tiled=True)  48.9 us
    dot_general x16, matrix products, visit_block(): jnp.einsum('rkgd,skd->kgrs', grouped, key_block, preferred_element_type=j...  33.4 us
    reduce_sum x16, other arithmetic, visit_block(): totals = totals * rescale + jnp.sum(exponent, -1)  24.3 us
    all_gather x1, blocking collectives, prefix(): pieces = jax.tree.map(lambda part: lax.all_gather(part, axis), value)  18.9 us
    select_n x15, other arithmetic, lap(): jnp.where(position < mine, new, old)  16.7 us
    psum x1, blocking collectives, body(): squares = lax.psum(squares, 'tp')  16.7 us
    all_gather x1, waiting for transfers between devices, attend(): key_piece = lax.all_gather(key_shard, 'ctx', axis=0, tiled=True)  13.5 us
  transfers between devices with their start and end apart: 3, of which 2 were waited for; matrix products, arithmetic and copies ran while one was open for 50% of the time, Pallas kernels for 0%

commit v1 on v0

v1 whole, which is shorter than its diff:
```python
import functools
import math

import jax
import jax.numpy as jnp
from jax import lax
from jax.experimental import pallas as pl
from jax.experimental.pallas import tpu as pltpu
from jax.sharding import PartitionSpec as P

HD = 128
ROWS = 512
HEADS = 6
TILE = 256
EPS = 1e-06
MASKED = -1e30
LOG2E = math.log2(math.e)
SCORE_SCALE = LOG2E / math.sqrt(HD)
SAFE_EXPONENT = 100.0
STATE_ROWS = HEADS * HD + 8
NEVER = 1 << 20

VMEM = pl.BlockSpec(memory_space=pltpu.VMEM)
SMEM = pl.BlockSpec(memory_space=pltpu.SMEM)
f32 = jnp.float32
bf16 = jnp.bfloat16
highest = lax.Precision.HIGHEST


def dot(a, b, contract=((1,), (0,)), precision=None):
    return lax.dot_general(a, b, (contract, ((), ())), precision=precision, preferred_element_type=f32)


def params():
    return pltpu.CompilerParams(vmem_limit_bytes=56 << 20)


def head(h):
    return slice(h * HD, (h + 1) * HD)


def recur_kernel(q_ref, k_ref, v_ref, step_ref, local_ref, grow_ref, message_ref):
    step = step_ref[...]
    rate = step / (1.0 + step)
    log_decay = -jnp.log(1.0 + step) * LOG2E
    earlier = lax.broadcasted_iota(jnp.int32, (ROWS, ROWS), 0)
    later = lax.broadcasted_iota(jnp.int32, (ROWS, ROWS), 1)
    upper = jnp.where(earlier <= later, 1.0, 0.0).astype(f32)
    total = dot(log_decay, upper, precision=highest)
    source = jnp.log(rate) * LOG2E - total
    end = total[:, ROWS - 1 : ROWS]
    tail = jnp.exp2(end + source)
    rows16 = jnp.concatenate([total, tail], 0)
    eye = jnp.where(
        lax.broadcasted_iota(jnp.int32, (16, HD), 0) == lax.broadcasted_iota(jnp.int32, (16, HD), 1), 1.0, 0.0
    ).astype(f32)
    columns = dot(rows16, eye, ((0,), (0,)), highest)
    grow_ref[...] = jnp.exp2(columns)
    message_ref[HEADS * HD :, :] = jnp.broadcast_to(end, (8, HD))
    at_row = lax.broadcasted_iota(jnp.int32, (TILE, TILE), 0)
    at_column = lax.broadcasted_iota(jnp.int32, (TILE, TILE), 1)
    seen = at_column <= at_row
    for h in range(HEADS):
        keys = k_ref[:, head(h)].astype(f32)
        keys = keys * lax.rsqrt(jnp.sum(keys * keys, -1, keepdims=True) + EPS)
        unit = keys.astype(bf16)
        values = v_ref[:, head(h)]
        for a in range(0, ROWS, TILE):
            result = None
            for b in range(0, a + TILE, TILE):
                scores = dot(q_ref[a : a + TILE, head(h)], unit[b : b + TILE], ((1,), (1,)))
                decay = jnp.exp2(columns[a : a + TILE, h : h + 1] + source[h : h + 1, b : b + TILE])
                weights = scores * decay
                if a == b:
                    weights = jnp.where(seen, weights, 0.0)
                part = dot(weights.astype(bf16), values[b : b + TILE])
                result = part if result is None else result + part
            local_ref[a : a + TILE, head(h)] = result
        tailed = (values.astype(f32) * columns[:, 8 + h : 9 + h]).astype(bf16)
        message_ref[head(h), :] = dot(unit, tailed, ((0,), (0,)))


def recur(lh_query, lh_key, lh_value, lh_step):
    step = jnp.pad(lh_step.T, ((0, 2), (0, 0)), constant_values=0.5)
    return pl.pallas_call(
        recur_kernel,
        out_shape=(
            jax.ShapeDtypeStruct((ROWS, HEADS * HD), f32),
            jax.ShapeDtypeStruct((ROWS, HD), f32),
            jax.ShapeDtypeStruct((STATE_ROWS, HD), f32),
        ),
        in_specs=[VMEM] * 4,
        out_specs=(VMEM,) * 3,
        compiler_params=params(),
        name="recur",
    )(lh_query, lh_key, lh_value, step)


def join_kernel(flag_ref, *refs):
    *messages, out_ref = refs
    decay = jnp.zeros((8, HD), f32)
    parts = [jnp.zeros((HD, HD), f32) for _ in range(HEADS)]
    for n, message in enumerate(messages):
        on = flag_ref[n] > 0
        logs = jnp.where(on, message[HEADS * HD :, :], 0.0)
        for h in range(HEADS):
            state = jnp.where(on, message[head(h), :], 0.0)
            parts[h] = jnp.exp2(logs[h : h + 1, :]) * parts[h] + state
        decay = decay + logs
    for h in range(HEADS):
        out_ref[head(h), :] = parts[h]
    out_ref[HEADS * HD :, :] = decay


def join(flags, *messages):
    return pl.pallas_call(
        join_kernel,
        out_shape=jax.ShapeDtypeStruct((STATE_ROWS, HD), f32),
        in_specs=[SMEM] + [VMEM] * len(messages),
        out_specs=VMEM,
        compiler_params=params(),
        name="join",
    )(jnp.stack([jnp.asarray(flag, jnp.int32) for flag in flags]), *messages)


def attend_kernel(first, last, buffers, meta_ref, *refs):
    mine = meta_ref[0]
    refs = list(refs)
    query_ref = refs.pop(0)
    own_ref = refs.pop(0) if first else None
    carry_ref, top_in_ref = (None, None) if first else (refs.pop(0), refs.pop(0))
    block_refs = [refs.pop(0) for _ in range(buffers)]
    if last:
        out_ref, square_ref, top_ref, sums, scaled, keys, values = refs
    else:
        sums, top_ref, scaled, keys, values = refs
    ones = jnp.ones((HD, HD), bf16)

    def norm(part):
        part = part.astype(f32)
        lengths = dot((part * part).astype(bf16), ones)
        return jnp.max(lengths.reshape(-1, 8, HD), 0)

    for h in range(HEADS):
        scaled[h * ROWS : (h + 1) * ROWS, :] = (query_ref[:, head(h)].astype(f32) * SCORE_SCALE).astype(bf16)
    if first:
        sums[...] = jnp.zeros_like(sums)
        top_ref[0:8, :] = norm(scaled[...])
        top_ref[8:16, :] = norm(own_ref[:, :HD])
    else:
        sums[...] = carry_ref[...]
        top_ref[...] = top_in_ref[...]
    values[:, HD:] = jnp.ones((values.shape[0], HD), bf16)

    filled = jnp.int32(0)
    for n, block in enumerate(block_refs):
        rows = block.shape[0]
        number = meta_ref[1 + n]
        takes = number < mine
        place = filled

        @pl.when(takes)
        def _():
            at = pl.ds(pl.multiple_of(place * ROWS, ROWS), rows)
            keys[at, :] = block[:, :HD]
            values[at, :HD] = block[:, HD:]
            top_ref[8:16, :] = jnp.maximum(top_ref[8:16, :], norm(block[:, :HD]))

        filled = filled + jnp.where(takes, rows // ROWS, 0)

    def visit(start, count):
        at = pl.ds(pl.multiple_of(start, ROWS), count)
        block_keys = keys[at, :]
        block_values = values[at, :]
        for h in range(HEADS):
            for a in range(0, ROWS, TILE):
                query = scaled[h * ROWS + a : h * ROWS + a + TILE, :]
                weights = jnp.exp2(dot(query, block_keys, ((1,), (1,)))).astype(bf16)
                sums[h, a : a + TILE, :] += dot(weights, block_values)

    if first:

        @pl.when(filled > 0)
        def _():
            visit(0, ROWS)

        at_row = lax.broadcasted_iota(jnp.int32, (TILE, TILE), 0)
        at_column = lax.broadcasted_iota(jnp.int32, (TILE, TILE), 1)
        seen = at_column <= at_row
        values[:ROWS, :HD] = own_ref[:, HD:]
        for h in range(HEADS):
            for a in range(0, ROWS, TILE):
                query = scaled[h * ROWS + a : h * ROWS + a + TILE, :]
                for b in range(0, a + TILE, TILE):
                    weights = jnp.exp2(dot(query, own_ref[b : b + TILE, :HD], ((1,), (1,))))
                    if a == b:
                        weights = jnp.where(seen, weights, 0.0)
                    sums[h, a : a + TILE, :] += dot(weights.astype(bf16), values[b : b + TILE, :])
    else:

        def pair(n, _):
            visit(n * 2 * ROWS, 2 * ROWS)
            return 0

        lax.fori_loop(0, filled // 2, pair, 0)

    if last:
        squares = jnp.zeros((8, ROWS), f32)
        for h in range(HEADS):
            result = (sums[h, :, :HD] / sums[h, :, HD:]).astype(bf16)
            out_ref[:, head(h)] = result
            result = result.astype(f32)
            squares = squares + dot(jnp.ones((8, HD), bf16), (result * result).astype(bf16), ((1,), (1,)))
        square_ref[...] = squares


def attend(mine, query, own, carry, blocks, numbers, last=False):
    first = carry is None
    meta = jnp.stack([mine] + list(numbers)).astype(jnp.int32)
    size = max(sum(block.shape[0] for block in blocks), ROWS)
    operands = [query] + ([own] if first else list(carry)) + list(blocks)
    sums = ((HEADS, ROWS, 2 * HD), f32)
    top = jax.ShapeDtypeStruct((16, HD), f32)
    scratch = [
        pltpu.VMEM((HEADS * ROWS, HD), bf16),
        pltpu.VMEM((size, HD), bf16),
        pltpu.VMEM((size, 2 * HD), bf16),
    ]
    if last:
        out_shape = (
            jax.ShapeDtypeStruct((ROWS, HEADS * HD), bf16),
            jax.ShapeDtypeStruct((8, ROWS), f32),
            top,
        )
        scratch = [pltpu.VMEM(*sums)] + scratch
    else:
        out_shape = (jax.ShapeDtypeStruct(*sums), top)
    return pl.pallas_call(
        functools.partial(attend_kernel, first, last, len(blocks)),
        out_shape=out_shape,
        in_specs=[SMEM] + [VMEM] * len(operands),
        out_specs=(VMEM,) * len(out_shape),
        scratch_shapes=scratch,
        compiler_params=params(),
        name="attend_last" if last else "attend",
    )(meta, *operands)


def attend_shifted(mine, query, pieces, numbers):
    grouped = query.reshape(ROWS, HEADS, HD)
    stacked = jnp.concatenate(pieces, 0)
    count = stacked.shape[0] // ROWS
    table = jnp.stack(numbers).astype(jnp.int32)
    scale = 1.0 / math.sqrt(HD)
    positions = mine * ROWS + jnp.arange(ROWS, dtype=jnp.int32)
    initial = (
        jnp.full((HEADS, ROWS), MASKED, f32),
        jnp.zeros((HEADS, ROWS), f32),
        jnp.zeros((HEADS, ROWS, HD), f32),
    )

    def step(n, running):
        def visit(current):
            top, totals, numerator = current
            block = lax.dynamic_slice_in_dim(stacked, n * ROWS, ROWS, 0)
            scores = jnp.einsum("rgd,sd->grs", grouped, block[:, :HD], preferred_element_type=f32) * scale
            places = table[n] * ROWS + jnp.arange(ROWS, dtype=jnp.int32)
            visible = places[None, :] <= positions[:, None]
            scores = jnp.where(visible, scores, MASKED)
            new_top = jnp.maximum(top, jnp.max(scores, -1))
            rescale = jnp.exp(top - new_top)
            weights = jnp.where(visible, jnp.exp(scores - new_top[..., None]), 0.0)
            numerator = numerator * rescale[..., None] + jnp.einsum(
                "grs,sd->grd", weights.astype(bf16), block[:, HD:], preferred_element_type=f32
            )
            return (new_top, totals * rescale + jnp.sum(weights, -1), numerator)

        return lax.cond(table[n] <= mine, visit, lambda current: current, running)

    _, totals, numerator = lax.fori_loop(0, count, step, initial)
    result = (numerator / totals[..., None]).astype(bf16)
    result = jnp.transpose(result, (1, 0, 2)).reshape(ROWS, HEADS * HD)
    wide = result.astype(f32)
    return result, jnp.broadcast_to(jnp.sum(wide * wide, -1)[None], (8, ROWS))


def carry_kernel(query_ref, local_ref, grow_ref, state_ref, gain_ref, out_ref):
    grow = grow_ref[...]
    for h in range(HEADS):
        state = state_ref[head(h), :]
        upper = state.astype(bf16)
        lower = (state - upper.astype(f32)).astype(bf16)
        both = dot(query_ref[:, head(h)], jnp.concatenate([upper, lower], 1))
        entered = both[:, :HD] + both[:, HD:]
        result = local_ref[:, head(h)] + entered * grow[:, h : h + 1]
        square = jnp.mean(result * result, -1, keepdims=True)
        out_ref[:, head(h)] = result * lax.rsqrt(square + EPS) * gain_ref[:, head(h)]


def finish_kernel(features, attention_ref, square_ref, linear_ref, gain_ref, out_ref):
    factor = lax.rsqrt(square_ref[...] / features + EPS)
    factor = dot(factor, jnp.full((8, HD), 0.125, f32), ((0,), (0,)), highest)
    for h in range(HEADS):
        part = attention_ref[:, head(h)].astype(f32) * factor * gain_ref[:, head(h)]
        out_ref[:, head(h)] = (part + linear_ref[:, head(h)]).astype(bf16)


def simple(kernel, dtype, name, *operands):
    return pl.pallas_call(
        kernel,
        out_shape=jax.ShapeDtypeStruct((ROWS, HEADS * HD), dtype),
        in_specs=[VMEM] * len(operands),
        out_specs=VMEM,
        compiler_params=params(),
        name=name,
    )(*operands)


def body(att_query, att_key, att_value, lh_query, lh_key, lh_value, lh_step, att_gain, lh_gain):
    mine = lax.axis_index("ctx")
    plane, side, core = mine // 4, (mine // 2) % 2, mine % 2
    partner = mine ^ 2

    def move(value, pairs):
        return lax.ppermute(value, "ctx", pairs)

    every = range(16)
    sibling = [(i, i ^ 1) for i in every]
    down = [(i, i ^ 1) for i in every if i % 2 == 0]

    own = jnp.concatenate([att_key, att_value], 1)
    across = move(own, [(i, i ^ 2) for i in every if i < 4 or i % 4 < 2])
    near = move(own, sibling)
    chip = jnp.concatenate([own, near], 0)
    onward = [(i, i + 4) for i in every if i % 2 == 0 and i < 12]
    wrapped = [(i, i + 12) for i in (1, 3)]
    behind = move(chip, onward + wrapped)
    local, grow, message = recur(lh_query, lh_key, lh_value, lh_step)

    def before(number, wanted):
        return jnp.where(wanted, number, NEVER)

    numbers = []
    pieces = []

    carry = attend(mine, att_query, own, None, [near], [before(mine ^ 1, core == 1)])
    pieces += [own, near]
    numbers += [mine, mine ^ 1]

    across_near = move(across, sibling)
    behind_near = move(behind, sibling)
    there = side == 1
    blocks = [across, across_near, behind, behind_near]
    got = [
        before(partner, there),
        before(partner ^ 1, there),
        before(jnp.where(core == 0, mine - 4, mine - 12), jnp.where(core == 0, plane >= 1, plane == 3)),
        before(jnp.where(core == 0, mine - 12 + 1, mine - 4 - 1), jnp.where(core == 0, plane == 3, plane >= 1)),
    ]
    carry = attend(mine, att_query, None, carry, blocks, got)
    pieces += blocks
    numbers += [
        got[0],
        got[1],
        got[2],
        jnp.where(got[2] < NEVER, got[2] ^ 1, NEVER),
        got[3],
        jnp.where(got[3] < NEVER, got[3] ^ 1, NEVER),
    ]

    far_message = jnp.where(core == 0, behind, jnp.concatenate([across, across_near], 0))
    far = move(far_message, [(i, i + 4) for i in every if i % 2 == 0 and 4 <= i < 12] + wrapped)
    level = move(behind, [(i, i ^ 2) for i in every if i % 2 == 0 and i >= 4])
    far_near = move(far, sibling)
    level_near = move(level, down)
    blocks = [level, level_near, far, far_near]
    got = [
        before(partner - 4, (core == 0) & (plane >= 1)),
        before(partner - 4 - 1, (core == 1) & (plane >= 1)),
        before(
            jnp.where(core == 0, mine - 8, partner - 12), jnp.where(core == 0, plane >= 2, plane == 3)
        ),
        before(
            jnp.where(core == 0, partner - 12 + 1, mine - 8 - 1),
            jnp.where(core == 0, plane == 3, plane >= 2),
        ),
    ]
    carry = attend(mine, att_query, None, carry, blocks, got)
    pieces += blocks
    for number in got:
        numbers += [number, jnp.where(number < NEVER, number ^ 1, NEVER)]

    level_far = move(far, [(i, i ^ 2) for i in every if i % 2 == 0 and i >= 8])
    level_far_near = move(level_far, down)
    blocks = [level_far, level_far_near]
    got = [
        before(partner - 8, (core == 0) & (plane >= 2)),
        before(partner - 8 - 1, (core == 1) & (plane >= 2)),
    ]
    attention, squares, top = attend(mine, att_query, None, carry, blocks, got, last=True)
    pieces += blocks
    for number in got:
        numbers += [number, jnp.where(number < NEVER, number ^ 1, NEVER)]
    bound = jnp.max(top[:8]) * jnp.max(top[8:])
    attention, squares = lax.cond(
        bound * 1.05 <= SAFE_EXPONENT * SAFE_EXPONENT,
        lambda: (attention, squares),
        lambda: attend_shifted(mine, att_query, pieces, numbers),
    )

    other = move(message, sibling)
    first_core = jnp.asarray(1, jnp.int32)
    of_chip = join(
        [first_core, first_core],
        jnp.where(core == 0, message, other),
        jnp.where(core == 0, other, message),
    )
    other_chip = move(of_chip, [(i, i ^ 2) for i in every])
    of_plane = join(
        [first_core, first_core],
        jnp.where(side == 0, of_chip, other_chip),
        jnp.where(side == 0, other_chip, of_chip),
    )
    one_back = move(of_plane, onward + wrapped)
    two_back = move(one_back, [(i, i + 4) for i in every if i % 2 == 0 and 4 <= i < 12])
    swapped = move(jnp.where(core == 0, two_back, one_back), sibling)
    swapped_one = move(one_back, down)
    entering = join(
        [
            plane == 3,
            plane >= 2,
            plane >= 1,
            side == 1,
            core == 1,
        ],
        jnp.where(core == 0, swapped, one_back),
        jnp.where(core == 0, two_back, swapped),
        jnp.where(core == 0, one_back, swapped_one),
        other_chip,
        other,
    )
    linear = simple(
        carry_kernel, f32, "carry", lh_query, local, grow, entering, lh_gain.reshape(1, HEADS * HD)
    )

    for bit in (1, 2, 4):
        squares = squares + lax.ppermute(squares, "tp", [(i, i ^ bit) for i in range(8)])
    features = HEADS * HD * lax.axis_size("tp")
    return simple(
        functools.partial(finish_kernel, float(features)),
        bf16,
        "finish",
        attention,
        squares,
        linear,
        att_gain.reshape(1, HEADS * HD),
    )


def solution(mesh):
    placed = (P("ctx", "tp"),) * 7 + (P("tp"), P("tp"))
    return jax.shard_map(body, mesh=mesh, in_specs=placed, out_specs=P("ctx", "tp"), check_vma=False)
```

time: 305 us -> 372 us (1.22)
  starting transfers between devices: 0.08 us -> 255 us
  matrix products: 118 us -> 0 us
  Pallas kernels: 0 us -> 67 us
  waiting for transfers between devices: 63.8 us -> 25.6 us
  other arithmetic: 51.1 us -> 13.9 us
  blocking collectives: 35.5 us -> 0 us
  between operations: 13.4 us -> 1.54 us
  loops' own time: 10.9 us -> 0.02 us
    ppermute x0 -> x20, starting transfers between devices: none -> 255 us  [the longest x3 232 us: body(): lax.ppermute(squares, 'tp', [(i, i ^ bit) for i in range(8)])]
    dot_general x37 -> x0, matrix products: 118 us -> none  [the longest x16 69.7 us: visit_block(): jnp.einsum('kgrs,skd->kgrd', weights, value_block, preferred_element_type...]
    pallas_call x0 -> x10, Pallas kernels: none -> 67 us  [the longest x4 46.7 us: attend(): pl.pallas_call(functools.partial(attend_kernel, first, last, len(blocks))...]
    all_gather x3 -> x0, waiting for transfers between devices: 62.4 us -> none  [the longest x1 48.9 us: attend(): value_piece = lax.all_gather(value_shard, 'ctx', axis=0, tiled=True)]
    reduce_sum x18 -> x0, other arithmetic: 25.9 us -> none  [the longest x16 24.3 us: visit_block(): totals = totals * rescale + jnp.sum(exponent, -1)]
    ppermute x0 -> x20, waiting for transfers between devices: none -> 25.6 us  [the longest x17 24.5 us: move(): return lax.ppermute(value, 'ctx', pairs)]
    all_gather x1 -> x0, blocking collectives: 18.9 us -> none  [prefix(): pieces = jax.tree.map(lambda part: lax.all_gather(part, axis), value)]
    psum x1 -> x0, blocking collectives: 16.7 us -> none  [body(): squares = lax.psum(squares, 'tp')]
  transfers between devices with their start and end apart: 3 -> 20, of which waited for: 2 -> 4; matrix products, arithmetic and copies ran while one was open for 50% -> 5% of each run, Pallas kernels for 0% -> 17%
where the time goes in v1:
time: 372 us; the launch traced here: 370 us
  starting transfers between devices  255 us (69%)
  Pallas kernels  67 us (18%)
  waiting for transfers between devices  25.6 us (7%)
  other arithmetic  13.9 us (4%)
  local copies, waits for them, and re-layouts  7.07 us (2%)
    ppermute x3, starting transfers between devices, body(): lax.ppermute(squares, 'tp', [(i, i ^ bit) for i in range(8)])  232 us
    pallas_call x4, Pallas kernels, attend(): pl.pallas_call(functools.partial(attend_kernel, first, last, len(blocks))...  46.7 us
    ppermute x17, waiting for transfers between devices, move(): return lax.ppermute(value, 'ctx', pairs)  24.5 us
    ppermute x17, starting transfers between devices, move(): return lax.ppermute(value, 'ctx', pairs)  22.7 us
  transfers between devices with their start and end apart: 20, of which 4 were waited for; matrix products, arithmetic and copies ran while one was open for 5% of the time, Pallas kernels for 17%

profile of v1, /device:TPU:101, one launch (start us, length us, event | category | flops | bytes accessed | tf_op | source)
XLA Modules:
  0.0 370.0 jit_solution(10956432057053450331)
XLA Ops:
  0.0 0.9 constant_dynamic-update-slice_fusion.13
  0.9 0.9 constant_dynamic-update-slice_fusion.12.refs_1_
  1.9 0.8 collective-permute-start
  2.6 1.3 pad.4.step_ref
  4.0 6.7 %recur.1 = (f32[512,768]{1,0:T(8,128)}, f32[512,128]{1,0:T(8,128)}, f32[776,128]{1,0:T(8,128)}) custom-call(bf16[512,768]{1,0:T(8,128)(2,1)} %query_ref.1, bf16[512,768]{1,0:T(8,128)(2,1)} %k_ref.1, bf16[512,768]{1,0:T(8,128)(2,1)} %v_ref.1, f32[8,512]{1,0:T(8,128)} %pad.4.step_ref), custom_call_target="tpu_custom_call" | custom-call | tf_op jit(solution)/shard_map/recur/pallas_call | solution.py:85
  10.7 0.0 collective-permute-start.14
  10.7 1.4 collective-permute-start.1
  12.1 0.0 collective-permute-done.refs_2_
  12.1 0.8 pad_maximum_fusion
  13.0 1.3 collective-permute-start.3
  14.3 7.5 %collective-permute-done.1.refs_3_ = bf16[512,256]{1,0:T(8,128)(2,1)S(1)} collective-permute-done((bf16[512,256]{1,0:T(8,128)(2,1)S(1)}, bf16[512,256]{1,0:T(8,128)(2,1)S(1)}, u32[]{:S(2)}, u32[]{:S(2)}) %collective-permute-start.1) | collective-permute-done | bytes 262176 | tf_op jit(solution)/shard_map/ppermute | solution.py:325
  21.8 1.2 collective-permute-start.2
  22.9 0.0 collective-permute-done.14.refs_4_
  23.0 2.1 broadcast_select_fusion.6
  25.0 0.5 broadcast_9_flag_ref.2.flag_ref
  25.6 1.9 join.3
  27.5 0.0 collective-permute-start.15
  27.5 0.9 maximum_select_fusion
  28.4 1.3 collective-permute-start.7
  29.8 10.3 %collective-permute-done.15.refs_3_ = f32[776,128]{1,0:T(8,128)S(1)} collective-permute-done((f32[776,128]{1,0:T(8,128)}, f32[776,128]{1,0:T(8,128)S(1)}, u32[]{:S(2)}, u32[]{:S(2)}) %collective-permute-start.15) | collective-permute-done | bytes 397344 | tf_op jit(solution)/shard_map/ppermute | solution.py:325
  40.0 2.1 broadcast_select_fusion
  42.2 1.9 join.4
  44.1 1.3 collective-permute-start.16
  45.4 0.7 collective-permute-start.5
  46.1 0.0 collective-permute-done.7.refs_5_
  46.1 1.4 collective-permute-start.9
  47.5 6.7 %collective-permute-done.16 = f32[776,128]{1,0:T(8,128)} collective-permute-done((f32[776,128]{1,0:T(8,128)}, f32[776,128]{1,0:T(8,128)}, u32[]{:S(2)}, u32[]{:S(2)}) %collective-permute-start.16) | collective-permute-done | bytes 397344 | tf_op jit(solution)/shard_map/ppermute | solution.py:325
  54.2 0.7 collective-permute-start.17
  54.9 1.4 collective-permute-start.4
  56.3 1.3 collective-permute-start.6
  57.5 3.3 collective-permute-start.8
  60.8 1.3 collective-permute-start.10
  62.1 0.0 collective-permute-done.17
  62.1 1.3 collective-permute-start.19
  63.4 1.8 broadcast_select_fusion.5
  65.2 0.8 copy-done.2
  66.0 4.2 %collective-permute-start.18 = (f32[776,128]{1,0:T(8,128)}, f32[776,128]{1,0:T(8,128)}, u32[]{:S(2)}, u32[]{:S(2)}) collective-permute-start(f32[776,128]{1,0:T(8,128)} %broadcast_select_fusion.5), channel_id=1, source_target_pairs={{0,8},{8,0},{16,24},{24,16},{32,40},{40,32},{48,56},{56,48},{64,72... | collective-permute-start | bytes 1191944 | tf_op jit(solution)/shard_map/ppermute | solution.py:325
  70.2 0.6 stack.147.meta_ref
  70.9 0.6 stack.152.meta_ref
  71.5 0.6 pad_add_fusion.1.meta_ref
  72.0 0.6 pad_add_fusion.meta_ref
  72.7 6.8 %attend.3 = (f32[6,512,256]{2,1,0:T(8,128)}, f32[16,128]{1,0:T(8,128)}) custom-call(s32[2]{0:T(128)} %pad_add_fusion.1.meta_ref, bf16[512,768]{1,0:T(8,128)(2,1)S(1)} %copy-done.1, bf16[512,256]{1,0:T(8,128)(2,1)S(1)} %constant_dynamic-update-slice_fusion.12.refs_1_, bf16[512,256]{1,0:T(8,128)(2,1)S(1)} %collective-permute-done.refs_2_), custom_call_target="tpu_custom_call" | custom-call | tf_op jit(solution)/shard_map/attend/pallas_call | solution.py:238
  79.5 16.0 %attend.4 = (f32[6,512,256]{2,1,0:T(8,128)}, f32[16,128]{1,0:T(8,128)}) custom-call(s32[5]{0:T(128)} %stack.152.meta_ref, bf16[512,768]{1,0:T(8,128)(2,1)S(1)} %copy-done.1, f32[6,512,256]{2,1,0:T(8,128)} %get-tuple-element.316.refs_1_, f32[16,128]{1,0:T(8,128)} %get-tuple-element.317.refs_2_, bf16[512,256]{1,0:T(8,128)(2,1)S(1)} %collective-permute-done.1.refs_3_, ...), custom_call_target="tpu_custom_call" | custom-call | tf_op jit(solution)/shard_map/attend/pallas_call | solution.py:238
  95.5 0.0 collective-permute-done.8.refs_6_
  95.5 16.0 %attend.5 = (f32[6,512,256]{2,1,0:T(8,128)}, f32[16,128]{1,0:T(8,128)}) custom-call(s32[5]{0:T(128)} %stack.147.meta_ref, bf16[512,768]{1,0:T(8,128)(2,1)S(1)} %copy-done.1, f32[6,512,256]{2,1,0:T(8,128)} %get-tuple-element.318.refs_1_, f32[16,128]{1,0:T(8,128)} %get-tuple-element.319.refs_2_, bf16[1024,256]{1,0:T(8,128)(2,1)S(1)} %collective-permute-done.5.refs_3_, ...), custom_call_target="tpu_custom_call" | custom-call | tf_op jit(solution)/shard_map/attend/pallas_call | solution.py:238
  111.5 0.0 collective-permute-done.10.refs_4_
  111.5 7.9 %attend_last.1 = (bf16[512,768]{1,0:T(8,128)(2,1)}, f32[8,512]{1,0:T(8,128)S(1)}, f32[16,128]{1,0:T(8,128)}) custom-call(s32[3]{0:T(128)} %pad_add_fusion.meta_ref, bf16[512,768]{1,0:T(8,128)(2,1)S(1)} %copy-done.1, f32[6,512,256]{2,1,0:T(8,128)} %get-tuple-element.320.refs_1_, f32[16,128]{1,0:T(8,128)} %get-tuple-element.321.refs_2_, ...), custom_call_target="tpu_custom_call" | custom-call | tf_op jit(solution)/shard_map/attend_last/pallas_call | solution.py:238
  119.4 1.4 slice_reduce_fusion
  122.1 0.0 copy-start.8
  122.1 0.0 copy-start.9
  122.1 0.0 copy-start.6
  122.1 228.0 %collective-permute-start.11 = (f32[8,512]{1,0:T(8,128)S(1)}, f32[8,512]{1,0:T(8,128)S(1)}, u32[]{:S(2)}, u32[]{:S(2)}) collective-permute-start(f32[8,512]{1,0:T(8,128)S(1)} %get-tuple-element.326), channel_id=1, source_target_pairs={{0,1},{1,0},{2,3},{3,2},{4,5},{5,4},{6,7},{7,6},{8,9},{9,8},{10,11... | collective-permute-start | bytes 49160 | tf_op jit(solution)/shard_map/ppermute | solution.py:447
  350.2 1.1 collective-permute-done.11
  351.3 1.8 collective-permute-start.12
  353.1 0.1 stack.160
  353.2 0.6 stack.161.flag_ref
  353.8 0.6 reshape.23.gain_ref
  354.4 0.6 reshape.24.gain_ref
  355.0 2.3 collective-permute-start.13
  357.3 2.3 broadcast_select_fusion.2
  359.7 2.4 join.5.state_ref
  362.1 4.4 %carry.1.linear_ref = f32[512,768]{1,0:T(8,128)} custom-call(bf16[512,768]{1,0:T(8,128)(2,1)} %query_ref.1, f32[512,768]{1,0:T(8,128)} %get-tuple-element.327.local_ref, f32[512,128]{1,0:T(8,128)} %get-tuple-element.328.grow_ref, f32[776,128]{1,0:T(8,128)} %join.5.state_ref, f32[1,768]{1,0:T(1,128)} %reshape.23.gain_ref), custom_call_target="tpu_custom_call" | custom-call | tf_op jit(solution)/shard_map/carry/pallas_call | solution.py:309
  366.5 0.6 add.103.square_ref
  367.1 2.9 finish.1
  (26 shorter events, 0.1 us)
Async XLA Ops:
  1.9 10.3 %collective-permute-start = (bf16[512,256]{1,0:T(8,128)(2,1)S(1)}, bf16[512,256]{1,0:T(8,128)(2,1)S(1)}, u32[]{:S(2)}, u32[]{:S(2)}) collective-permute-start(bf16[512,256]{1,0:T(8,128)(2,1)S(1)} %constant_dynamic-update-slice_fusion.12.refs_1_), channel_id=1, source_target_pairs={{0,8},{8,0},{16,24},{24,16},{32,40},{40,32},{48,56},{56,48},{64,72... | collective-permute-start | bytes 786440 | tf_op jit(solution)/shard_map/ppermute | solution.py:325
  10.7 62.0 %copy-start.1 = (bf16[512,768]{1,0:T(8,128)(2,1)S(1)}, bf16[512,768]{1,0:T(8,128)(2,1)}, u32[]{:S(2)}) copy-start(bf16[512,768]{1,0:T(8,128)(2,1)} %refs_0_.7) | copy-start | bytes 2359300
  10.7 12.3 %collective-permute-start.14 = (f32[776,128]{1,0:T(8,128)}, f32[776,128]{1,0:T(8,128)S(1)}, u32[]{:S(2)}, u32[]{:S(2)}) collective-permute-start(f32[776,128]{1,0:T(8,128)} %get-tuple-element.329), channel_id=1, source_target_pairs={{0,8},{8,0},{16,24},{24,16},{32,40},{40,32},{48,56},{56,48},{64,72... | collective-permute-start | bytes 1191944 | tf_op jit(solution)/shard_map/ppermute | solution.py:325
  10.7 11.0 %collective-permute-start.1 = (bf16[512,256]{1,0:T(8,128)(2,1)S(1)}, bf16[512,256]{1,0:T(8,128)(2,1)S(1)}, u32[]{:S(2)}, u32[]{:S(2)}) collective-permute-start(bf16[512,256]{1,0:T(8,128)(2,1)S(1)} %constant_dynamic-update-slice_fusion.12.refs_1_), channel_id=1, source_target_pairs={{0,16},{8,24},{16,0},{24,8},{32,48},{40,56},{64,80},{72,88},{96,11... | collective-permute-start | bytes 786440 | tf_op jit(solution)/shard_map/ppermute | solution.py:325
  13.0 14.5 %collective-permute-start.3 = (bf16[1024,256]{1,0:T(8,128)(2,1)}, bf16[1024,256]{1,0:T(8,128)(2,1)S(1)}, u32[]{:S(2)}, u32[]{:S(2)}) collective-permute-start(bf16[1024,256]{1,0:T(8,128)(2,1)} %pad_maximum_fusion), channel_id=1, source_target_pairs={{0,32},{16,48},{32,64},{48,80},{64,96},{80,112},{8,104},{24,120},{... | collective-permute-start | bytes 1572872 | tf_op jit(solution)/shard_map/ppermute | solution.py:325
  21.8 5.8 %collective-permute-start.2 = (bf16[512,256]{1,0:T(8,128)(2,1)S(1)}, bf16[512,256]{1,0:T(8,128)(2,1)S(1)}, u32[]{:S(2)}, u32[]{:S(2)}) collective-permute-start(bf16[512,256]{1,0:T(8,128)(2,1)S(1)} %collective-permute-done.1.refs_3_), channel_id=1, source_target_pairs={{0,8},{8,0},{16,24},{24,16},{32,40},{40,32},{48,56},{56,48},{64,72... | collective-permute-start | bytes 786440 | tf_op jit(solution)/shard_map/ppermute | solution.py:325
  23.0 4.6 %copy-start.4 = (f32[776,128]{1,0:T(8,128)}, f32[776,128]{1,0:T(8,128)S(1)}, u32[]{:S(2)}) copy-start(f32[776,128]{1,0:T(8,128)S(1)} %collective-permute-done.14.refs_4_) | copy-start | bytes 1191940
  27.5 12.5 %collective-permute-start.15 = (f32[776,128]{1,0:T(8,128)}, f32[776,128]{1,0:T(8,128)S(1)}, u32[]{:S(2)}, u32[]{:S(2)}) collective-permute-start(f32[776,128]{1,0:T(8,128)} %join.3), channel_id=1, source_target_pairs={{0,16},{8,24},{16,0},{24,8},{32,48},{40,56},{48,32},{56,40},{64,80... | collective-permute-start | bytes 1191944 | tf_op jit(solution)/shard_map/ppermute | solution.py:325
  28.4 17.6 %collective-permute-start.7 = (bf16[1024,256]{1,0:T(8,128)(2,1)}, bf16[1024,256]{1,0:T(8,128)(2,1)S(1)}, u32[]{:S(2)}, u32[]{:S(2)}) collective-permute-start(bf16[1024,256]{1,0:T(8,128)(2,1)} %maximum_select_fusion), channel_id=1, source_target_pairs={{32,64},{48,80},{64,96},{80,112},{8,104},{24,120},{33,65},{49,81},... | collective-permute-start | bytes 1572872 | tf_op jit(solution)/shard_map/ppermute | solution.py:325
  40.0 4.0 %copy-start.5 = (f32[776,128]{1,0:T(8,128)}, f32[776,128]{1,0:T(8,128)S(1)}, u32[]{:S(2)}) copy-start(f32[776,128]{1,0:T(8,128)S(1)} %collective-permute-done.15.refs_3_) | copy-start | bytes 1191940
  44.1 10.1 %collective-permute-start.16 = (f32[776,128]{1,0:T(8,128)}, f32[776,128]{1,0:T(8,128)}, u32[]{:S(2)}, u32[]{:S(2)}) collective-permute-start(f32[776,128]{1,0:T(8,128)} %join.4), channel_id=1, source_target_pairs={{0,32},{16,48},{32,64},{48,80},{64,96},{80,112},{8,104},{24,120},{... | collective-permute-start | bytes 1191944 | tf_op jit(solution)/shard_map/ppermute | solution.py:325
  45.4 10.9 %collective-permute-start.5 = (bf16[1024,256]{1,0:T(8,128)(2,1)S(1)}, bf16[1024,256]{1,0:T(8,128)(2,1)S(1)}, u32[]{:S(2)}, u32[]{:S(2)}) collective-permute-start(bf16[1024,256]{1,0:T(8,128)(2,1)S(1)} %collective-permute-done.3.refs_5_), channel_id=1, source_target_pairs={{32,48},{48,32},{64,80},{80,64},{96,112},{112,96},{33,49},{49,33},... | collective-permute-start | bytes 1572872 | tf_op jit(solution)/shard_map/ppermute | solution.py:325
  46.1 14.7 %collective-permute-start.9 = (bf16[1024,256]{1,0:T(8,128)(2,1)S(1)}, bf16[1024,256]{1,0:T(8,128)(2,1)}, u32[]{:S(2)}, u32[]{:S(2)}) collective-permute-start(bf16[1024,256]{1,0:T(8,128)(2,1)S(1)} %collective-permute-done.7.refs_5_), channel_id=1, source_target_pairs={{64,80},{80,64},{96,112},{112,96},{65,81},{81,65},{97,113},{113,97... | collective-permute-start | bytes 1572872 | tf_op jit(solution)/shard_map/ppermute | solution.py:325
  54.2 7.9 %collective-permute-start.17 = (f32[776,128]{1,0:T(8,128)}, f32[776,128]{1,0:T(8,128)S(1)}, u32[]{:S(2)}, u32[]{:S(2)}) collective-permute-start(f32[776,128]{1,0:T(8,128)} %collective-permute-done.16), channel_id=1, source_target_pairs={{32,64},{48,80},{64,96},{80,112},{33,65},{49,81},{65,97},{81,113},... | collective-permute-start | bytes 1191944 | tf_op jit(solution)/shard_map/ppermute | solution.py:325
  54.9 10.4 %collective-permute-start.4 = (bf16[1024,256]{1,0:T(8,128)(2,1)S(1)}, bf16[1024,256]{1,0:T(8,128)(2,1)S(1)}, u32[]{:S(2)}, u32[]{:S(2)}) collective-permute-start(bf16[1024,256]{1,0:T(8,128)(2,1)S(1)} %collective-permute-done.3.refs_5_), channel_id=1, source_target_pairs={{0,8},{8,0},{16,24},{24,16},{32,40},{40,32},{48,56},{56,48},{64,72... | collective-permute-start | bytes 1572872 | tf_op jit(solution)/shard_map/ppermute | solution.py:325
  56.3 39.3 %collective-permute-start.6 = (bf16[1024,256]{1,0:T(8,128)(2,1)S(1)}, bf16[1024,256]{1,0:T(8,128)(2,1)}, u32[]{:S(2)}, u32[]{:S(2)}) collective-permute-start(bf16[1024,256]{1,0:T(8,128)(2,1)S(1)} %collective-permute-done.5.refs_3_), channel_id=1, source_target_pairs={{0,8},{16,24},{32,40},{48,56},{64,72},{80,88},{96,104},{112,120},{... | collective-permute-start | bytes 1572872 | tf_op jit(solution)/shard_map/ppermute | solution.py:325
  57.5 38.0 %collective-permute-start.8 = (bf16[1024,256]{1,0:T(8,128)(2,1)S(1)}, bf16[1024,256]{1,0:T(8,128)(2,1)}, u32[]{:S(2)}, u32[]{:S(2)}) collective-permute-start(bf16[1024,256]{1,0:T(8,128)(2,1)S(1)} %collective-permute-done.7.refs_5_), channel_id=1, source_target_pairs={{0,8},{8,0},{16,24},{24,16},{32,40},{40,32},{48,56},{56,48},{64,72... | collective-permute-start | bytes 1572872 | tf_op jit(solution)/shard_map/ppermute | solution.py:325
  60.8 50.7 %collective-permute-start.10 = (bf16[1024,256]{1,0:T(8,128)(2,1)}, bf16[1024,256]{1,0:T(8,128)(2,1)}, u32[]{:S(2)}, u32[]{:S(2)}) collective-permute-start(bf16[1024,256]{1,0:T(8,128)(2,1)} %collective-permute-done.9.refs_3_), channel_id=1, source_target_pairs={{0,8},{16,24},{32,40},{48,56},{64,72},{80,88},{96,104},{112,120},{... | collective-permute-start | bytes 1572872 | tf_op jit(solution)/shard_map/ppermute | solution.py:325
  62.1 3.1 copy-start.3
  62.1 295.2 %collective-permute-start.19 = (f32[776,128]{1,0:T(8,128)}, f32[776,128]{1,0:T(8,128)}, u32[]{:S(2)}, u32[]{:S(2)}) collective-permute-start(f32[776,128]{1,0:T(8,128)} %collective-permute-done.16), channel_id=1, source_target_pairs={{0,8},{16,24},{32,40},{48,56},{64,72},{80,88},{96,104},{112,120},{... | collective-permute-start | bytes 1191944 | tf_op jit(solution)/shard_map/ppermute | solution.py:325
  65.2 0.8 copy-start.2
  66.0 291.3 %collective-permute-start.18 = (f32[776,128]{1,0:T(8,128)}, f32[776,128]{1,0:T(8,128)}, u32[]{:S(2)}, u32[]{:S(2)}) collective-permute-start(f32[776,128]{1,0:T(8,128)} %broadcast_select_fusion.5), channel_id=1, source_target_pairs={{0,8},{8,0},{16,24},{24,16},{32,40},{40,32},{48,56},{56,48},{64,72... | collective-permute-start | bytes 1191944 | tf_op jit(solution)/shard_map/ppermute | solution.py:325
  122.1 231.7 %copy-start.8 = (f32[768]{0:T(1024)S(1)}, f32[768]{0:T(1024)}, u32[]{:S(2)}) copy-start(f32[768]{0:T(1024)} %param.23) | copy-start | bytes 9220
  122.1 232.3 %copy-start.9 = (f32[768]{0:T(1024)S(1)}, f32[768]{0:T(1024)}, u32[]{:S(2)}) copy-start(f32[768]{0:T(1024)} %param.22) | copy-start | bytes 9220
  122.1 245.0 %copy-start.6 = (bf16[512,768]{1,0:T(8,128)(2,1)S(1)}, bf16[512,768]{1,0:T(8,128)(2,1)}, u32[]{:S(2)}) copy-start(bf16[512,768]{1,0:T(8,128)(2,1)} %get-tuple-element.577.attention_ref) | copy-start | bytes 2359300
  122.1 229.2 %collective-permute-start.11 = (f32[8,512]{1,0:T(8,128)S(1)}, f32[8,512]{1,0:T(8,128)S(1)}, u32[]{:S(2)}, u32[]{:S(2)}) collective-permute-start(f32[8,512]{1,0:T(8,128)S(1)} %get-tuple-element.326), channel_id=1, source_target_pairs={{0,1},{1,0},{2,3},{3,2},{4,5},{5,4},{6,7},{7,6},{8,9},{9,8},{10,11... | collective-permute-start | bytes 49160 | tf_op jit(solution)/shard_map/ppermute | solution.py:447
  351.3 3.7 %collective-permute-start.12 = (f32[8,512]{1,0:T(8,128)S(1)}, f32[8,512]{1,0:T(8,128)S(1)}, u32[]{:S(2)}, u32[]{:S(2)}) collective-permute-start(f32[8,512]{1,0:T(8,128)S(1)} %add.101), channel_id=1, source_target_pairs={{0,2},{1,3},{2,0},{3,1},{4,6},{5,7},{6,4},{7,5},{8,10},{9,11},{10,... | collective-permute-start | bytes 49160 | tf_op jit(solution)/shard_map/ppermute | solution.py:447
  355.0 11.5 %collective-permute-start.13 = (f32[8,512]{1,0:T(8,128)S(1)}, f32[8,512]{1,0:T(8,128)S(1)}, u32[]{:S(2)}, u32[]{:S(2)}) collective-permute-start(f32[8,512]{1,0:T(8,128)S(1)} %add.102), channel_id=1, source_target_pairs={{0,4},{1,5},{2,6},{3,7},{4,0},{5,1},{6,2},{7,3},{8,12},{9,13},{10,... | collective-permute-start | bytes 49160 | tf_op jit(solution)/shard_map/ppermute | solution.py:447

commit v2 on v1

v2 whole, which is shorter than its diff:
```python
import functools
import math

import jax
import jax.numpy as jnp
from jax import lax
from jax.experimental import pallas as pl
from jax.experimental.pallas import tpu as pltpu
from jax.sharding import PartitionSpec as P

HD = 128
ROWS = 512
HEADS = 6
TILE = 256
EPS = 1e-06
MASKED = -1e30
LOG2E = math.log2(math.e)
SCORE_SCALE = LOG2E / math.sqrt(HD)
SAFE_EXPONENT = 100.0
STATE_ROWS = HEADS * HD + 8
NEVER = 1 << 20

VMEM = pl.BlockSpec(memory_space=pltpu.VMEM)
SMEM = pl.BlockSpec(memory_space=pltpu.SMEM)
f32 = jnp.float32
bf16 = jnp.bfloat16
highest = lax.Precision.HIGHEST


def dot(a, b, contract=((1,), (0,)), precision=None):
    return lax.dot_general(a, b, (contract, ((), ())), precision=precision, preferred_element_type=f32)


def params():
    return pltpu.CompilerParams(vmem_limit_bytes=56 << 20)


def cost(us):
    return pl.CostEstimate(flops=int(us * 1e9), bytes_accessed=int(us * 1e6), transcendentals=int(us * 1e6))


def head(h):
    return slice(h * HD, (h + 1) * HD)


def recur_kernel(q_ref, k_ref, v_ref, step_ref, local_ref, grow_ref, message_ref, padded):
    padded[...] = jnp.full((ROWS, HD), 0.5, f32)
    padded[:, :HEADS] = step_ref[...]
    step = jnp.transpose(padded[...])[:8, :]
    rate = step / (1.0 + step)
    log_decay = -jnp.log(1.0 + step) * LOG2E
    earlier = lax.broadcasted_iota(jnp.int32, (ROWS, ROWS), 0)
    later = lax.broadcasted_iota(jnp.int32, (ROWS, ROWS), 1)
    upper = jnp.where(earlier <= later, 1.0, 0.0).astype(f32)
    total = dot(log_decay, upper, precision=highest)
    source = jnp.log(rate) * LOG2E - total
    end = total[:, ROWS - 1 : ROWS]
    tail = jnp.exp2(end + source)
    rows = jnp.concatenate([total, tail, jnp.zeros((HD - 16, ROWS), f32)], 0)
    columns = jnp.transpose(rows)
    grow_ref[...] = jnp.exp2(columns)
    message_ref[HEADS * HD :, :] = jnp.broadcast_to(end, (8, HD))
    at_row = lax.broadcasted_iota(jnp.int32, (TILE, TILE), 0)
    at_column = lax.broadcasted_iota(jnp.int32, (TILE, TILE), 1)
    seen = at_column <= at_row
    for h in range(HEADS):
        keys = k_ref[:, head(h)].astype(f32)
        keys = keys * lax.rsqrt(jnp.sum(keys * keys, -1, keepdims=True) + EPS)
        unit = keys.astype(bf16)
        values = v_ref[:, head(h)]
        for a in range(0, ROWS, TILE):
            result = None
            for b in range(0, a + TILE, TILE):
                scores = dot(q_ref[a : a + TILE, head(h)], unit[b : b + TILE], ((1,), (1,)))
                decay = jnp.exp2(columns[a : a + TILE, h : h + 1] + source[h : h + 1, b : b + TILE])
                weights = scores * decay
                if a == b:
                    weights = jnp.where(seen, weights, 0.0)
                part = dot(weights.astype(bf16), values[b : b + TILE])
                result = part if result is None else result + part
            local_ref[a : a + TILE, head(h)] = result
        tailed = (values.astype(f32) * columns[:, 8 + h : 9 + h]).astype(bf16)
        message_ref[head(h), :] = dot(unit, tailed, ((0,), (0,)))


def recur(lh_query, lh_key, lh_value, lh_step):
    return pl.pallas_call(
        recur_kernel,
        out_shape=(
            jax.ShapeDtypeStruct((ROWS, HEADS * HD), f32),
            jax.ShapeDtypeStruct((ROWS, HD), f32),
            jax.ShapeDtypeStruct((STATE_ROWS, HD), f32),
        ),
        in_specs=[VMEM] * 4,
        out_specs=(VMEM,) * 3,
        scratch_shapes=[pltpu.VMEM((ROWS, HD), f32)],
        compiler_params=params(),
        cost_estimate=cost(2.5),
        name="recur",
    )(lh_query, lh_key, lh_value, lh_step)


def follow(early, late):
    logs = early[1] + late[1]
    states = [jnp.exp2(late[1][h : h + 1, :]) * early[0][h] + late[0][h] for h in range(HEADS)]
    return states, logs


def state_of(ref, wanted=None):
    states = [ref[head(h), :] for h in range(HEADS)]
    logs = ref[HEADS * HD :, :]
    if wanted is None:
        return states, logs
    return [jnp.where(wanted, state, 0.0) for state in states], jnp.where(wanted, logs, 0.0)


def put_state(ref, value):
    for h in range(HEADS):
        ref[head(h), :] = value[0][h]
    ref[HEADS * HD :, :] = value[1]


def join_kernel(bit, mine_ref, own_ref, other_ref, out_ref):
    own_first = (mine_ref[0] // bit) % 2 == 0
    own, other = state_of(own_ref), state_of(other_ref)

    def pick(one, two):
        return [jnp.where(own_first, a, b) for a, b in zip(one[0], two[0])], jnp.where(own_first, one[1], two[1])

    put_state(out_ref, follow(pick(own, other), pick(other, own)))


def join(bit, mine, own, other):
    return pl.pallas_call(
        functools.partial(join_kernel, bit),
        out_shape=jax.ShapeDtypeStruct((STATE_ROWS, HD), f32),
        in_specs=[SMEM, VMEM, VMEM],
        out_specs=VMEM,
        compiler_params=params(),
        cost_estimate=cost(1.0),
        name="join",
    )(mine, own, other)


def hand_kernel(mine_ref, behind_ref, beyond_ref, out_ref):
    plane, core = mine_ref[0] // 4, mine_ref[0] % 2
    behind = state_of(behind_ref, (plane == 3) | (core == 0))
    beyond = state_of(beyond_ref, (plane >= 2) & (core == 1))
    put_state(out_ref, follow(behind, beyond))


def hand(mine, behind, beyond):
    return pl.pallas_call(
        hand_kernel,
        out_shape=jax.ShapeDtypeStruct((STATE_ROWS, HD), f32),
        in_specs=[SMEM, VMEM, VMEM],
        out_specs=VMEM,
        compiler_params=params(),
        cost_estimate=cost(1.0),
        name="hand",
    )(mine, behind, beyond)


def attend_kernel(first, numbers_of, buffers, mine_ref, *refs):
    mine = mine_ref[0]
    refs = list(refs)
    query_ref = refs.pop(0)
    own_ref = refs.pop(0) if first else None
    carry_ref, count_ref, top_in_ref = (None,) * 3 if first else (refs.pop(0) for _ in range(3))
    block_refs = [refs.pop(0) for _ in range(buffers)]
    if first:
        numerator_ref, counted_ref, top_ref, sums, scaled, keys, values = refs
    else:
        out_ref, square_ref, safe_ref, sums, scaled, keys, values, top_ref = refs
    ones = jnp.ones((HD, HD), bf16)

    def norm(part):
        part = part.astype(f32)
        lengths = dot((part * part).astype(bf16), ones)
        return jnp.max(lengths.reshape(-1, 8, HD), 0)

    for h in range(HEADS):
        scaled[h * ROWS : (h + 1) * ROWS, :] = (query_ref[:, head(h)].astype(f32) * SCORE_SCALE).astype(bf16)
    if first:
        sums[...] = jnp.zeros_like(sums)
        top_ref[0:8, :] = norm(scaled[...])
        top_ref[8:16, :] = norm(own_ref[:, :HD])
    else:
        for h in range(HEADS):
            sums[h, :, :HD] = carry_ref[:, head(h)]
            sums[h, :, HD:] = jnp.broadcast_to(count_ref[:, h : h + 1], (ROWS, HD))
        top_ref[...] = top_in_ref[...]
    values[:, HD:] = jnp.ones((values.shape[0], HD), bf16)

    filled = jnp.int32(0)
    for block, number in zip(block_refs, numbers_of(mine)):
        rows = block.shape[0]
        takes = number < mine
        place = filled

        @pl.when(takes)
        def _():
            at = pl.ds(pl.multiple_of(place * ROWS, ROWS), rows)
            keys[at, :] = block[:, :HD]
            values[at, :HD] = block[:, HD:]
            top_ref[8:16, :] = jnp.maximum(top_ref[8:16, :], norm(block[:, :HD]))

        filled = filled + jnp.where(takes, rows // ROWS, 0)

    def visit(start, count):
        at = pl.ds(pl.multiple_of(start, ROWS), count)
        block_keys = keys[at, :]
        block_values = values[at, :]
        for h in range(HEADS):
            for a in range(0, ROWS, TILE):
                query = scaled[h * ROWS + a : h * ROWS + a + TILE, :]
                weights = jnp.exp2(dot(query, block_keys, ((1,), (1,)))).astype(bf16)
                sums[h, a : a + TILE, :] += dot(weights, block_values)

    def pair(n, _):
        visit(n * 2 * ROWS, 2 * ROWS)
        return 0

    lax.fori_loop(0, filled // 2, pair, 0)

    if first:

        @pl.when(filled % 2 == 1)
        def _():
            visit((filled - 1) * ROWS, ROWS)

        at_row = lax.broadcasted_iota(jnp.int32, (TILE, TILE), 0)
        at_column = lax.broadcasted_iota(jnp.int32, (TILE, TILE), 1)
        seen = at_column <= at_row
        values[:ROWS, :HD] = own_ref[:, HD:]
        for h in range(HEADS):
            for a in range(0, ROWS, TILE):
                query = scaled[h * ROWS + a : h * ROWS + a + TILE, :]
                for b in range(0, a + TILE, TILE):
                    weights = jnp.exp2(dot(query, own_ref[b : b + TILE, :HD], ((1,), (1,))))
                    if a == b:
                        weights = jnp.where(seen, weights, 0.0)
                    sums[h, a : a + TILE, :] += dot(weights.astype(bf16), values[b : b + TILE, :])
            numerator_ref[:, head(h)] = sums[h, :, :HD]
            counted_ref[:, h : h + 1] = sums[h, :, HD : HD + 1]
    else:
        squares = jnp.zeros((8, ROWS), f32)
        for h in range(HEADS):
            result = (sums[h, :, :HD] / sums[h, :, HD:]).astype(bf16)
            out_ref[:, head(h)] = result
            result = result.astype(f32)
            squares = squares + dot(jnp.ones((8, HD), bf16), (result * result).astype(bf16), ((1,), (1,)))
        square_ref[...] = squares
        bound = jnp.max(top_ref[:8, :]) * jnp.max(top_ref[8:, :])
        safe_ref[0] = jnp.where(bound * 1.05 <= SAFE_EXPONENT * SAFE_EXPONENT, 1, 0)


def attend(mine, query, own, carry, blocks, numbers_of):
    first = carry is None
    size = sum(block.shape[0] for block in blocks)
    operands = [query] + ([own] if first else list(carry)) + list(blocks)
    top = (16, HD)
    scratch = [
        pltpu.VMEM((HEADS, ROWS, 2 * HD), f32),
        pltpu.VMEM((HEADS * ROWS, HD), bf16),
        pltpu.VMEM((size, HD), bf16),
        pltpu.VMEM((size, 2 * HD), bf16),
    ]
    if first:
        out_shape = (
            jax.ShapeDtypeStruct((ROWS, HEADS * HD), f32),
            jax.ShapeDtypeStruct((ROWS, HD), f32),
            jax.ShapeDtypeStruct(top, f32),
        )
        out_specs = (VMEM,) * 3
    else:
        out_shape = (
            jax.ShapeDtypeStruct((ROWS, HEADS * HD), bf16),
            jax.ShapeDtypeStruct((8, ROWS), f32),
            jax.ShapeDtypeStruct((1,), jnp.int32),
        )
        out_specs = (VMEM, VMEM, SMEM)
        scratch.append(pltpu.VMEM(top, f32))
    return pl.pallas_call(
        functools.partial(attend_kernel, first, numbers_of, len(blocks)),
        out_shape=out_shape,
        in_specs=[SMEM] + [VMEM] * len(operands),
        out_specs=out_specs,
        scratch_shapes=scratch,
        compiler_params=params(),
        cost_estimate=cost(14.0),
        name="attend_near" if first else "attend_far",
    )(mine, *operands)


def attend_shifted(mine, query, pieces, numbers):
    grouped = query.reshape(ROWS, HEADS, HD)
    stacked = jnp.concatenate(pieces, 0)
    count = stacked.shape[0] // ROWS
    table = jnp.stack(numbers).astype(jnp.int32)
    scale = 1.0 / math.sqrt(HD)
    positions = mine * ROWS + jnp.arange(ROWS, dtype=jnp.int32)
    initial = (
        jnp.full((HEADS, ROWS), MASKED, f32),
        jnp.zeros((HEADS, ROWS), f32),
        jnp.zeros((HEADS, ROWS, HD), f32),
    )

    def step(n, running):
        def visit(current):
            top, totals, numerator = current
            block = lax.dynamic_slice_in_dim(stacked, n * ROWS, ROWS, 0)
            scores = jnp.einsum("rgd,sd->grs", grouped, block[:, :HD], preferred_element_type=f32) * scale
            places = table[n] * ROWS + jnp.arange(ROWS, dtype=jnp.int32)
            visible = places[None, :] <= positions[:, None]
            scores = jnp.where(visible, scores, MASKED)
            new_top = jnp.maximum(top, jnp.max(scores, -1))
            rescale = jnp.exp(top - new_top)
            weights = jnp.where(visible, jnp.exp(scores - new_top[..., None]), 0.0)
            numerator = numerator * rescale[..., None] + jnp.einsum(
                "grs,sd->grd", weights.astype(bf16), block[:, HD:], preferred_element_type=f32
            )
            return (new_top, totals * rescale + jnp.sum(weights, -1), numerator)

        return lax.cond(table[n] <= mine, visit, lambda current: current, running)

    _, totals, numerator = lax.fori_loop(0, count, step, initial)
    result = (numerator / totals[..., None]).astype(bf16)
    result = jnp.transpose(result, (1, 0, 2)).reshape(ROWS, HEADS * HD)
    wide = result.astype(f32)
    return result, jnp.broadcast_to(jnp.sum(wide * wide, -1)[None], (8, ROWS))


def carry_kernel(
    mine_ref, query_ref, local_ref, grow_ref, kept_ref, handed_ref, chip_ref, core_ref, gain_ref, out_ref
):
    mine = mine_ref[0]
    plane, side, core = mine // 4, (mine // 2) % 2, mine % 2
    kept, handed = state_of(kept_ref), state_of(handed_ref)

    def pick(one, two, wanted):
        states = [jnp.where(wanted, jnp.where(core == 0, a, b), 0.0) for a, b in zip(one[0], two[0])]
        return states, jnp.where(wanted, jnp.where(core == 0, one[1], two[1]), 0.0)

    entering = pick(handed, kept, plane >= 2)
    entering = follow(entering, pick(kept, handed, plane >= 1))
    entering = follow(entering, state_of(chip_ref, side == 1))
    entering = follow(entering, state_of(core_ref, core == 1))
    grow = grow_ref[...]
    for h in range(HEADS):
        state = entering[0][h]
        upper = state.astype(bf16)
        lower = (state - upper.astype(f32)).astype(bf16)
        both = dot(query_ref[:, head(h)], jnp.concatenate([upper, lower], 1))
        entered = both[:, :HD] + both[:, HD:]
        result = local_ref[:, head(h)] + entered * grow[:, h : h + 1]
        square = jnp.mean(result * result, -1, keepdims=True)
        out_ref[:, head(h)] = result * lax.rsqrt(square + EPS) * gain_ref[head(h)][None, :]


def finish_kernel(features, attention_ref, square_ref, other_ref, linear_ref, gain_ref, out_ref):
    factor = lax.rsqrt((square_ref[...] + other_ref[...]) / features + EPS)
    factor = dot(factor, jnp.full((8, HD), 0.125, f32), ((0,), (0,)), highest)
    for h in range(HEADS):
        part = attention_ref[:, head(h)].astype(f32) * factor * gain_ref[head(h)][None, :]
        out_ref[:, head(h)] = (part + linear_ref[:, head(h)]).astype(bf16)


def simple(kernel, dtype, name, scalar, *operands):
    return pl.pallas_call(
        kernel,
        out_shape=jax.ShapeDtypeStruct((ROWS, HEADS * HD), dtype),
        in_specs=[SMEM] * len(scalar) + [VMEM] * len(operands),
        out_specs=VMEM,
        compiler_params=params(),
        cost_estimate=cost(2.0),
        name=name,
    )(*scalar, *operands)


def body(att_query, att_key, att_value, lh_query, lh_key, lh_value, lh_step, att_gain, lh_gain):
    mine = lax.axis_index("ctx")
    place = mine.reshape(1).astype(jnp.int32)

    def move(value, pairs):
        return lax.ppermute(value, "ctx", pairs)

    every = range(16)
    sibling = [(i, i ^ 1) for i in every]
    sideways = [(i, i ^ 2) for i in every]
    last_plane = [(i, i + 4) for i in every if i % 2 == 0 and i < 12] + [(i, i + 12) for i in (1, 3)]
    plane_before = [(i, i + 8) for i in every if i % 2 == 1 and i < 8]

    own = jnp.concatenate([att_key, att_value], 1)
    across = move(own, [(i, i ^ 2) for i in every if i < 4 or i % 4 < 2])
    near = move(own, sibling)
    chip = jnp.concatenate([own, near], 0)
    behind = move(chip, last_plane)
    beyond = move(chip, plane_before)

    local, grow, message = recur(lh_query, lh_key, lh_value, lh_step)
    other = move(message, sibling)
    of_chip = join(1, place, message, other)
    other_chip = move(of_chip, sideways)

    across_near = move(across, sibling)
    behind_near = move(behind, sibling)
    level = move(behind, [(i, j) for i, j in sideways if (i % 2 == 0 and i >= 4) or i >= 12])
    level_beyond = move(beyond, [(i, j) for i, j in sideways if i % 2 == 1 and i >= 8])

    def where(number, wanted):
        return jnp.where(wanted, number, NEVER)

    def parts(mine):
        return mine // 4, (mine // 2) % 2, mine % 2, mine - mine % 2

    def columns(number):
        return number + 2 - 4 * ((number // 2) % 2)

    def brought(mine, core):
        plane, _, _, even = parts(mine)
        if core == 0:
            return where(even - 4, plane >= 1)
        return where(even - 12, plane == 3)

    def near_numbers(mine):
        plane, side, core, even = parts(mine)
        siding = side == 1
        own_bring = jnp.where(core == 0, brought(mine, 0), brought(mine, 1))
        other_bring = jnp.where(core == 0, brought(mine, 1), brought(mine, 0))
        return [where(mine - 1, core == 1), where(even - 2, siding), where(even - 2, siding), own_bring, other_bring]

    def far_numbers(mine):
        plane, side, core, even = parts(mine)
        beyond_at = where(even - 8, plane >= 2)
        own_bring = jnp.where(core == 0, brought(mine, 0), brought(mine, 1))
        other_bring = jnp.where(core == 0, brought(mine, 1), brought(mine, 0))
        return [
            where(beyond_at, core == 1),
            where(beyond_at, core == 0),
            own_bring,
            other_bring,
            where(beyond_at, core == 1),
            where(beyond_at, core == 0),
        ]

    near_blocks = [near, across, across_near, behind, behind_near]
    carry = attend(place, att_query, own, None, near_blocks, near_numbers)

    of_plane = join(2, place, of_chip, other_chip)
    state_behind = move(of_plane, last_plane)
    state_beyond = move(of_plane, plane_before)

    beyond_near = move(beyond, sibling)
    level_near = move(level, sibling)
    level_beyond_near = move(level_beyond, sibling)
    far_blocks = [beyond, beyond_near, level, level_near, level_beyond, level_beyond_near]
    attention, squares, safe = attend(place, att_query, None, carry, far_blocks, far_numbers)

    def shifted():
        _, side, core, even = parts(mine)
        pieces = [own] + near_blocks + far_blocks
        firsts = [mine] + near_numbers(mine) + far_numbers(mine)
        flip = [False, False] + [False] * 2 + [True] * 2 + [True] * 6
        numbers = []
        for n, (piece, number) in enumerate(zip(pieces, firsts)):
            numbers += [number] if piece.shape[0] == ROWS else [number, number + 1]
        return attend_shifted(mine, att_query, pieces, numbers)

    attention, squares = lax.cond(safe[0] > 0, lambda: (attention, squares), shifted)

    kept = hand(place, state_behind, state_beyond)
    handed = move(kept, sibling)
    linear = simple(
        carry_kernel, f32, "carry", [place], lh_query, local, grow, kept, handed, other_chip, other, lh_gain
    )

    def over(value, bit):
        return lax.ppermute(value, "tp", [(i, i ^ bit) for i in range(8)])

    squares = squares + over(squares, 1)
    squares = squares + over(squares, 2)
    features = HEADS * HD * lax.axis_size("tp")
    return simple(
        functools.partial(finish_kernel, float(features)),
        bf16,
        "finish",
        [],
        attention,
        squares,
        over(squares, 4),
        linear,
        att_gain,
    )


def solution(mesh):
    placed = (P("ctx", "tp"),) * 7 + (P("tp"), P("tp"))
    return jax.shard_map(body, mesh=mesh, in_specs=placed, out_specs=P("ctx", "tp"), check_vma=False)
```

time: 372 us -> 345 us (0.927)
  starting transfers between devices: 255 us -> 21.8 us
  matrix products: 0 us -> 100 us
  local copies, waits for them, and re-layouts: 7.07 us -> 81.5 us
  loops' own time: 0.02 us -> 26.9 us
  other arithmetic: 13.9 us -> 30 us
  Pallas kernels: 67 us -> 58.5 us
    ppermute x3, starting transfers between devices: 232 us -> 5.68 us  [over(): return lax.ppermute(value, 'tp', [(i, i ^ bit) for i in range(8)])]
    dot_general x0 -> x32, matrix products: none -> 100 us  [the longest x16 67 us: visit(): jnp.einsum('grs,sd->grd', weights.astype(bf16), block[:, HD:], preferred_...]
    cond x1 -> x63, local copies, waits for them, and re-layouts: 0.01 us -> 50.2 us
    another operation x1 -> x22, loops' own time: 0.02 us -> 26.9 us  [the longest x1 14.2 us: attend_shifted(): _, totals, numerator = lax.fori_loop(0, count, step, initial)]
    reduce_sum x0 -> x17, other arithmetic: none -> 26.1 us  [the longest x16 24.4 us: visit(): return (new_top, totals * rescale + jnp.sum(weights, -1), numerator)]
    dynamic_slice x0 -> x36, local copies, waits for them, and re-layouts: none -> 23.4 us  [the longest x20 13 us: step(): return lax.cond(table[n] <= mine, visit, lambda current: current, running)]
    select_n x5 -> x0, other arithmetic: 9.26 us -> none  [the longest x1 2.34 us: body(): jnp.where(core == 0, one_back, swapped_one)]
    pallas_call x7 -> x5, Pallas kernels: 52.9 us -> 44.7 us  [the longest x2 38.9 us: attend(): pl.pallas_call(functools.partial(attend_kernel, first, numbers_of, len(bl...]
  transfers between devices with their start and end apart: 20 -> 19, of which waited for: 4 -> 7; matrix products, arithmetic and copies ran while one was open for 5% -> 48% of each run, Pallas kernels for 17% -> 14%
where the time goes in v2:
time: 345 us; the launch traced here: 343 us
  matrix products  100 us (29%)
  local copies, waits for them, and re-layouts  81.5 us (24%)
  Pallas kernels  58.5 us (17%)
  other arithmetic  30 us (9%)
  loops' own time  26.9 us (8%)
  waiting for transfers between devices  22.9 us (7%)
  starting transfers between devices  21.8 us (6%)
    dot_general x16, matrix products, visit(): jnp.einsum('grs,sd->grd', weights.astype(bf16), block[:, HD:], preferred_...  67 us
    cond x62, local copies, waits for them, and re-layouts  49.1 us
    pallas_call x2, Pallas kernels, attend(): pl.pallas_call(functools.partial(attend_kernel, first, numbers_of, len(bl...  38.9 us
    dot_general x16, matrix products, visit(): jnp.einsum('rgd,sd->grs', grouped, block[:, :HD], preferred_element_type=...  33.4 us
    reduce_sum x16, other arithmetic, visit(): return (new_top, totals * rescale + jnp.sum(weights, -1), numerator)  24.4 us
    ppermute x16, waiting for transfers between devices, move(): return lax.ppermute(value, 'ctx', pairs)  20.4 us
    ppermute x16, starting transfers between devices, move(): return lax.ppermute(value, 'ctx', pairs)  16.2 us
    another operation x1, loops' own time, attend_shifted(): _, totals, numerator = lax.fori_loop(0, count, step, initial)  14.2 us
  transfers between devices with their start and end apart: 19, of which 7 were waited for; matrix products, arithmetic and copies ran while one was open for 48% of the time, Pallas kernels for 14%

profile of v2, /device:TPU:101, one launch (start us, length us, event | category | flops | bytes accessed | tf_op | source)
XLA Modules:
  0.0 342.8 jit_solution(14467893608258561727)
XLA Ops:
  1.6 6.2 %recur.1 = (f32[512,768]{1,0:T(8,128)}, f32[512,128]{1,0:T(8,128)}, f32[776,128]{1,0:T(8,128)}) custom-call(bf16[512,768]{1,0:T(8,128)(2,1)} %query_ref.1, bf16[512,768]{1,0:T(8,128)(2,1)} %k_ref.1, bf16[512,768]{1,0:T(8,128)(2,1)} %v_ref.1, f32[512,6]{1,0:T(8,128)} %copy.18.step_ref), custom_call_target="tpu_custom_call" | custom-call | flops 2500000000 | bytes 2500000 | tf_op jit(solution)/shard_map/recur/pallas_call | solution.py:87
  17.0 8.0 %collective-permute-done.15.other_ref.chip_ref = f32[776,128]{1,0:T(8,128)S(1)} collective-permute-done((f32[776,128]{1,0:T(8,128)}, f32[776,128]{1,0:T(8,128)S(1)}, u32[]{:S(2)}, u32[]{:S(2)}) %collective-permute-start.15) | collective-permute-done | bytes 397344 | tf_op jit(solution)/shard_map/ppermute | solution.py:386
  30.0 4.5 %collective-permute-start.7 = (bf16[1024,256]{1,0:T(8,128)(2,1)S(1)}, bf16[1024,256]{1,0:T(8,128)(2,1)S(1)}, u32[]{:S(2)}, u32[]{:S(2)}) collective-permute-start(bf16[1024,256]{1,0:T(8,128)(2,1)S(1)} %collective-permute-done.3.refs_5_), channel_id=1, source_target_pairs={{32,48},{48,32},{64,80},{80,64},{96,112},{104,120},{112,96},{120,1... | collective-permute-start | bytes 1572872 | tf_op jit(solution)/shard_map/ppermute | solution.py:386
  34.5 2.3 collective-permute-start.9
  39.6 7.6 %collective-permute-done.17.beyond_ref = f32[776,128]{1,0:T(8,128)S(1)} collective-permute-done((f32[776,128]{1,0:T(8,128)}, f32[776,128]{1,0:T(8,128)S(1)}, u32[]{:S(2)}, u32[]{:S(2)}) %collective-permute-start.17) | collective-permute-done | bytes 397344 | tf_op jit(solution)/shard_map/ppermute | solution.py:386
  50.4 2.4 collective-permute-done.9.refs_8_
  52.8 18.9 %attend_near.1 = (f32[512,768]{1,0:T(8,128)}, f32[512,128]{1,0:T(8,128)}, f32[16,128]{1,0:T(8,128)}) custom-call(s32[1]{0:T(128)} %bitcast.18.mine_ref, bf16[512,768]{1,0:T(8,128)(2,1)S(1)} %copy-done.1, bf16[512,256]{1,0:T(8,128)(2,1)S(1)} %constant_dynamic-update-slice_fusion.12.refs_1_, bf16[512,256]{1,0:T(8,128)(2,1)S(1)} %collective-permute-done.refs_2_, ...), custom_call_target="tpu_custom_call" | custom-call | flops 14000000000 | bytes 14000000 | tf_op jit(solution)/shard_map/attend_near/pallas_call | solution.py:284
  71.7 20.0 %attend_far.1 = (bf16[512,768]{1,0:T(8,128)(2,1)}, f32[8,512]{1,0:T(8,128)S(1)}, s32[1]{0:T(128)}) custom-call(s32[1]{0:T(128)} %bitcast.18.mine_ref, bf16[512,768]{1,0:T(8,128)(2,1)S(1)} %copy-done.1, f32[512,768]{1,0:T(8,128)} %get-tuple-element.256.refs_1_, f32[512,128]{1,0:T(8,128)} %get-tuple-element.257.refs_2_, f32[16,128]{1,0:T(8,128)} %get-tuple-element.258.refs_3_, ...), custom_call_target="tpu_custom_call" | custom-call | flops 14000000000 | bytes 14000000 | tf_op jit(solution)/shard_map/attend_far/pallas_call | solution.py:284
  92.3 234.2 %conditional.2 = (f32[8,512]{1,0:T(8,128)S(1)}, bf16[512,768]{1,0:T(8,128)(2,1)}) conditional(s32[]{:T(128)} %bitcast.19, (s32[]{:T(128)}, bf16[512,256]{1,0:T(8,128)(2,1)S(1)}, bf16[512,256]{1,0:T(8,128)(2,1)S(1)}, bf16[512,256]{1,0:T(8,128)(2,1)S(1)}, bf16[512,256]{1,0:T(8,128)(2,1)S(1)}, /*index=5*/bf16[1024,256]{1,0:T(8,128)(2,1)S(1)}, ...), branch_computations={%region_0.8_spmd, %region_8.9_spmd} | conditional | flops 828774976 | bytes 92804496 | solution.py:470
  98.1 2.3 copy-done.2
  101.3 220.8 %while.17 = (s32[]{:T(128)}, f32[6,512]{1,0:T(8,128)S(1)}, f32[6,512]{1,0:T(8,128)S(1)}, f32[6,512,128]{2,1,0:T(8,128)S(1)}, s32[20]{0:T(128)S(1)}, /*index=5*/s...) while((s32[]{:T(128)}, f32[6,512]{1,0:T(8,128)S(1)}, ...), condition=%wide.region_6.6_spmd.clone, body=%wide.region_1.5_spmd.clone.sunk | while | flops 826809344 | bytes 49492392 | solution.py:327
  102.6 12.1 %conditional.5 = ((f32[6,512]{1,0:T(8,128)S(1)}, f32[6,512]{1,0:T(8,128)S(1)}, f32[6,512,128]{2,1,0:T(8,128)S(1)})) conditional(s32[]{:T(128)} %convert_element_type.35, (f32[6,512]{1,0:T(8,128)S(1)}, f32[6,512]{1,0:T(8,128)S(1)}, f32[6,512,128]{2,1,0:T(8,128)S(1)}) %tuple.59, (s32[]{:T(128)}, s32[20]{0:T(128)S(1)}, s32[]{:T(128)}, ...), branch_computations={%region_2.1_spmd, %region_3.4_spmd} | conditional | flops 826809344 | bytes 49490116 | solution.py:325
  106.3 2.6 copy-done
  110.5 4.2 %multiply_add_fusion = f32[6,512,128]{2,1,0:T(8,128)S(1)} fusion(f32[6,512,128]{2,1,0:T(8,128)S(1)} %get-tuple-element.215, f32[512,512,6]{1,0,2:T(8,128)} %copy-done, f32[6,512]{1,0:T(8,128)S(1)} %max.2, pred[512,512]{0,1:T(8,128)(4,1)S(1)} %broadcast_compare_fusion, f32[6,512]{1,0:T(8,128)S(1)} %get-tuple-element.339, ...), kind=kOutput, calls=%fused_computation.8 | convolution fusion | flops 411303936 | bytes 9854984 | tf_op jit(solution)/shard_map/cond/branch_0_fun/while/body/eval_jaxpr/cond/branch_1_fun/grs,sd->grd/dot_general | solution.py:320
  116.1 12.1 %conditional.5 = ((f32[6,512]{1,0:T(8,128)S(1)}, f32[6,512]{1,0:T(8,128)S(1)}, f32[6,512,128]{2,1,0:T(8,128)S(1)})) conditional(s32[]{:T(128)} %convert_element_type.35, (f32[6,512]{1,0:T(8,128)S(1)}, f32[6,512]{1,0:T(8,128)S(1)}, f32[6,512,128]{2,1,0:T(8,128)S(1)}) %tuple.59, (s32[]{:T(128)}, s32[20]{0:T(128)S(1)}, s32[]{:T(128)}, ...), branch_computations={%region_2.1_spmd, %region_3.4_spmd} | conditional | flops 826809344 | bytes 49490116 | solution.py:325
  119.8 2.6 copy-done
  123.9 4.2 %multiply_add_fusion = f32[6,512,128]{2,1,0:T(8,128)S(1)} fusion(f32[6,512,128]{2,1,0:T(8,128)S(1)} %get-tuple-element.215, f32[512,512,6]{1,0,2:T(8,128)} %copy-done, f32[6,512]{1,0:T(8,128)S(1)} %max.2, pred[512,512]{0,1:T(8,128)(4,1)S(1)} %broadcast_compare_fusion, f32[6,512]{1,0:T(8,128)S(1)} %get-tuple-element.339, ...), kind=kOutput, calls=%fused_computation.8 | convolution fusion | flops 411303936 | bytes 9854984 | tf_op jit(solution)/shard_map/cond/branch_0_fun/while/body/eval_jaxpr/cond/branch_1_fun/grs,sd->grd/dot_general | solution.py:320
  129.5 12.1 %conditional.5 = ((f32[6,512]{1,0:T(8,128)S(1)}, f32[6,512]{1,0:T(8,128)S(1)}, f32[6,512,128]{2,1,0:T(8,128)S(1)})) conditional(s32[]{:T(128)} %convert_element_type.35, (f32[6,512]{1,0:T(8,128)S(1)}, f32[6,512]{1,0:T(8,128)S(1)}, f32[6,512,128]{2,1,0:T(8,128)S(1)}) %tuple.59, (s32[]{:T(128)}, s32[20]{0:T(128)S(1)}, s32[]{:T(128)}, ...), branch_computations={%region_2.1_spmd, %region_3.4_spmd} | conditional | flops 826809344 | bytes 49490116 | solution.py:325
  133.2 2.6 copy-done
  137.4 4.2 %multiply_add_fusion = f32[6,512,128]{2,1,0:T(8,128)S(1)} fusion(f32[6,512,128]{2,1,0:T(8,128)S(1)} %get-tuple-element.215, f32[512,512,6]{1,0,2:T(8,128)} %copy-done, f32[6,512]{1,0:T(8,128)S(1)} %max.2, pred[512,512]{0,1:T(8,128)(4,1)S(1)} %broadcast_compare_fusion, f32[6,512]{1,0:T(8,128)S(1)} %get-tuple-element.339, ...), kind=kOutput, calls=%fused_computation.8 | convolution fusion | flops 411303936 | bytes 9854984 | tf_op jit(solution)/shard_map/cond/branch_0_fun/while/body/eval_jaxpr/cond/branch_1_fun/grs,sd->grd/dot_general | solution.py:320
  143.0 12.1 %conditional.5 = ((f32[6,512]{1,0:T(8,128)S(1)}, f32[6,512]{1,0:T(8,128)S(1)}, f32[6,512,128]{2,1,0:T(8,128)S(1)})) conditional(s32[]{:T(128)} %convert_element_type.35, (f32[6,512]{1,0:T(8,128)S(1)}, f32[6,512]{1,0:T(8,128)S(1)}, f32[6,512,128]{2,1,0:T(8,128)S(1)}) %tuple.59, (s32[]{:T(128)}, s32[20]{0:T(128)S(1)}, s32[]{:T(128)}, ...), branch_computations={%region_2.1_spmd, %region_3.4_spmd} | conditional | flops 826809344 | bytes 49490116 | solution.py:325
  146.7 2.6 copy-done
  150.8 4.2 %multiply_add_fusion = f32[6,512,128]{2,1,0:T(8,128)S(1)} fusion(f32[6,512,128]{2,1,0:T(8,128)S(1)} %get-tuple-element.215, f32[512,512,6]{1,0,2:T(8,128)} %copy-done, f32[6,512]{1,0:T(8,128)S(1)} %max.2, pred[512,512]{0,1:T(8,128)(4,1)S(1)} %broadcast_compare_fusion, f32[6,512]{1,0:T(8,128)S(1)} %get-tuple-element.339, ...), kind=kOutput, calls=%fused_computation.8 | convolution fusion | flops 411303936 | bytes 9854984 | tf_op jit(solution)/shard_map/cond/branch_0_fun/while/body/eval_jaxpr/cond/branch_1_fun/grs,sd->grd/dot_general | solution.py:320
  156.4 12.1 %conditional.5 = ((f32[6,512]{1,0:T(8,128)S(1)}, f32[6,512]{1,0:T(8,128)S(1)}, f32[6,512,128]{2,1,0:T(8,128)S(1)})) conditional(s32[]{:T(128)} %convert_element_type.35, (f32[6,512]{1,0:T(8,128)S(1)}, f32[6,512]{1,0:T(8,128)S(1)}, f32[6,512,128]{2,1,0:T(8,128)S(1)}) %tuple.59, (s32[]{:T(128)}, s32[20]{0:T(128)S(1)}, s32[]{:T(128)}, ...), branch_computations={%region_2.1_spmd, %region_3.4_spmd} | conditional | flops 826809344 | bytes 49490116 | solution.py:325
  160.1 2.6 copy-done
  164.3 4.2 %multiply_add_fusion = f32[6,512,128]{2,1,0:T(8,128)S(1)} fusion(f32[6,512,128]{2,1,0:T(8,128)S(1)} %get-tuple-element.215, f32[512,512,6]{1,0,2:T(8,128)} %copy-done, f32[6,512]{1,0:T(8,128)S(1)} %max.2, pred[512,512]{0,1:T(8,128)(4,1)S(1)} %broadcast_compare_fusion, f32[6,512]{1,0:T(8,128)S(1)} %get-tuple-element.339, ...), kind=kOutput, calls=%fused_computation.8 | convolution fusion | flops 411303936 | bytes 9854984 | tf_op jit(solution)/shard_map/cond/branch_0_fun/while/body/eval_jaxpr/cond/branch_1_fun/grs,sd->grd/dot_general | solution.py:320
  169.8 12.1 %conditional.5 = ((f32[6,512]{1,0:T(8,128)S(1)}, f32[6,512]{1,0:T(8,128)S(1)}, f32[6,512,128]{2,1,0:T(8,128)S(1)})) conditional(s32[]{:T(128)} %convert_element_type.35, (f32[6,512]{1,0:T(8,128)S(1)}, f32[6,512]{1,0:T(8,128)S(1)}, f32[6,512,128]{2,1,0:T(8,128)S(1)}) %tuple.59, (s32[]{:T(128)}, s32[20]{0:T(128)S(1)}, s32[]{:T(128)}, ...), branch_computations={%region_2.1_spmd, %region_3.4_spmd} | conditional | flops 826809344 | bytes 49490116 | solution.py:325
  173.6 2.6 copy-done
  177.7 4.2 %multiply_add_fusion = f32[6,512,128]{2,1,0:T(8,128)S(1)} fusion(f32[6,512,128]{2,1,0:T(8,128)S(1)} %get-tuple-element.215, f32[512,512,6]{1,0,2:T(8,128)} %copy-done, f32[6,512]{1,0:T(8,128)S(1)} %max.2, pred[512,512]{0,1:T(8,128)(4,1)S(1)} %broadcast_compare_fusion, f32[6,512]{1,0:T(8,128)S(1)} %get-tuple-element.339, ...), kind=kOutput, calls=%fused_computation.8 | convolution fusion | flops 411303936 | bytes 9854984 | tf_op jit(solution)/shard_map/cond/branch_0_fun/while/body/eval_jaxpr/cond/branch_1_fun/grs,sd->grd/dot_general | solution.py:320
  183.3 12.1 %conditional.5 = ((f32[6,512]{1,0:T(8,128)S(1)}, f32[6,512]{1,0:T(8,128)S(1)}, f32[6,512,128]{2,1,0:T(8,128)S(1)})) conditional(s32[]{:T(128)} %convert_element_type.35, (f32[6,512]{1,0:T(8,128)S(1)}, f32[6,512]{1,0:T(8,128)S(1)}, f32[6,512,128]{2,1,0:T(8,128)S(1)}) %tuple.59, (s32[]{:T(128)}, s32[20]{0:T(128)S(1)}, s32[]{:T(128)}, ...), branch_computations={%region_2.1_spmd, %region_3.4_spmd} | conditional | flops 826809344 | bytes 49490116 | solution.py:325
  184.9 2.1 fusion.2
  187.0 2.6 copy-done
  191.2 4.2 %multiply_add_fusion = f32[6,512,128]{2,1,0:T(8,128)S(1)} fusion(f32[6,512,128]{2,1,0:T(8,128)S(1)} %get-tuple-element.215, f32[512,512,6]{1,0,2:T(8,128)} %copy-done, f32[6,512]{1,0:T(8,128)S(1)} %max.2, pred[512,512]{0,1:T(8,128)(4,1)S(1)} %broadcast_compare_fusion, f32[6,512]{1,0:T(8,128)S(1)} %get-tuple-element.339, ...), kind=kOutput, calls=%fused_computation.8 | convolution fusion | flops 411303936 | bytes 9854984 | tf_op jit(solution)/shard_map/cond/branch_0_fun/while/body/eval_jaxpr/cond/branch_1_fun/grs,sd->grd/dot_general | solution.py:320
  196.8 12.1 %conditional.5 = ((f32[6,512]{1,0:T(8,128)S(1)}, f32[6,512]{1,0:T(8,128)S(1)}, f32[6,512,128]{2,1,0:T(8,128)S(1)})) conditional(s32[]{:T(128)} %convert_element_type.35, (f32[6,512]{1,0:T(8,128)S(1)}, f32[6,512]{1,0:T(8,128)S(1)}, f32[6,512,128]{2,1,0:T(8,128)S(1)}) %tuple.59, (s32[]{:T(128)}, s32[20]{0:T(128)S(1)}, s32[]{:T(128)}, ...), branch_computations={%region_2.1_spmd, %region_3.4_spmd} | conditional | flops 826809344 | bytes 49490116 | solution.py:325
  198.4 2.1 fusion.2
  200.5 2.6 copy-done
  204.7 4.2 %multiply_add_fusion = f32[6,512,128]{2,1,0:T(8,128)S(1)} fusion(f32[6,512,128]{2,1,0:T(8,128)S(1)} %get-tuple-element.215, f32[512,512,6]{1,0,2:T(8,128)} %copy-done, f32[6,512]{1,0:T(8,128)S(1)} %max.2, pred[512,512]{0,1:T(8,128)(4,1)S(1)} %broadcast_compare_fusion, f32[6,512]{1,0:T(8,128)S(1)} %get-tuple-element.339, ...), kind=kOutput, calls=%fused_computation.8 | convolution fusion | flops 411303936 | bytes 9854984 | tf_op jit(solution)/shard_map/cond/branch_0_fun/while/body/eval_jaxpr/cond/branch_1_fun/grs,sd->grd/dot_general | solution.py:320
  210.2 12.1 %conditional.5 = ((f32[6,512]{1,0:T(8,128)S(1)}, f32[6,512]{1,0:T(8,128)S(1)}, f32[6,512,128]{2,1,0:T(8,128)S(1)})) conditional(s32[]{:T(128)} %convert_element_type.35, (f32[6,512]{1,0:T(8,128)S(1)}, f32[6,512]{1,0:T(8,128)S(1)}, f32[6,512,128]{2,1,0:T(8,128)S(1)}) %tuple.59, (s32[]{:T(128)}, s32[20]{0:T(128)S(1)}, s32[]{:T(128)}, ...), branch_computations={%region_2.1_spmd, %region_3.4_spmd} | conditional | flops 826809344 | bytes 49490116 | solution.py:325
  214.0 2.6 copy-done
  218.1 4.2 %multiply_add_fusion = f32[6,512,128]{2,1,0:T(8,128)S(1)} fusion(f32[6,512,128]{2,1,0:T(8,128)S(1)} %get-tuple-element.215, f32[512,512,6]{1,0,2:T(8,128)} %copy-done, f32[6,512]{1,0:T(8,128)S(1)} %max.2, pred[512,512]{0,1:T(8,128)(4,1)S(1)} %broadcast_compare_fusion, f32[6,512]{1,0:T(8,128)S(1)} %get-tuple-element.339, ...), kind=kOutput, calls=%fused_computation.8 | convolution fusion | flops 411303936 | bytes 9854984 | tf_op jit(solution)/shard_map/cond/branch_0_fun/while/body/eval_jaxpr/cond/branch_1_fun/grs,sd->grd/dot_general | solution.py:320
  223.7 12.1 %conditional.5 = ((f32[6,512]{1,0:T(8,128)S(1)}, f32[6,512]{1,0:T(8,128)S(1)}, f32[6,512,128]{2,1,0:T(8,128)S(1)})) conditional(s32[]{:T(128)} %convert_element_type.35, (f32[6,512]{1,0:T(8,128)S(1)}, f32[6,512]{1,0:T(8,128)S(1)}, f32[6,512,128]{2,1,0:T(8,128)S(1)}) %tuple.59, (s32[]{:T(128)}, s32[20]{0:T(128)S(1)}, s32[]{:T(128)}, ...), branch_computations={%region_2.1_spmd, %region_3.4_spmd} | conditional | flops 826809344 | bytes 49490116 | solution.py:325
  227.4 2.6 copy-done
  231.6 4.2 %multiply_add_fusion = f32[6,512,128]{2,1,0:T(8,128)S(1)} fusion(f32[6,512,128]{2,1,0:T(8,128)S(1)} %get-tuple-element.215, f32[512,512,6]{1,0,2:T(8,128)} %copy-done, f32[6,512]{1,0:T(8,128)S(1)} %max.2, pred[512,512]{0,1:T(8,128)(4,1)S(1)} %broadcast_compare_fusion, f32[6,512]{1,0:T(8,128)S(1)} %get-tuple-element.339, ...), kind=kOutput, calls=%fused_computation.8 | convolution fusion | flops 411303936 | bytes 9854984 | tf_op jit(solution)/shard_map/cond/branch_0_fun/while/body/eval_jaxpr/cond/branch_1_fun/grs,sd->grd/dot_general | solution.py:320
  239.9 12.1 %conditional.5 = ((f32[6,512]{1,0:T(8,128)S(1)}, f32[6,512]{1,0:T(8,128)S(1)}, f32[6,512,128]{2,1,0:T(8,128)S(1)})) conditional(s32[]{:T(128)} %convert_element_type.35, (f32[6,512]{1,0:T(8,128)S(1)}, f32[6,512]{1,0:T(8,128)S(1)}, f32[6,512,128]{2,1,0:T(8,128)S(1)}) %tuple.59, (s32[]{:T(128)}, s32[20]{0:T(128)S(1)}, s32[]{:T(128)}, ...), branch_computations={%region_2.1_spmd, %region_3.4_spmd} | conditional | flops 826809344 | bytes 49490116 | solution.py:325
  243.6 2.6 copy-done
  247.8 4.2 %multiply_add_fusion = f32[6,512,128]{2,1,0:T(8,128)S(1)} fusion(f32[6,512,128]{2,1,0:T(8,128)S(1)} %get-tuple-element.215, f32[512,512,6]{1,0,2:T(8,128)} %copy-done, f32[6,512]{1,0:T(8,128)S(1)} %max.2, pred[512,512]{0,1:T(8,128)(4,1)S(1)} %broadcast_compare_fusion, f32[6,512]{1,0:T(8,128)S(1)} %get-tuple-element.339, ...), kind=kOutput, calls=%fused_computation.8 | convolution fusion | flops 411303936 | bytes 9854984 | tf_op jit(solution)/shard_map/cond/branch_0_fun/while/body/eval_jaxpr/cond/branch_1_fun/grs,sd->grd/dot_general | solution.py:320
  253.4 12.1 %conditional.5 = ((f32[6,512]{1,0:T(8,128)S(1)}, f32[6,512]{1,0:T(8,128)S(1)}, f32[6,512,128]{2,1,0:T(8,128)S(1)})) conditional(s32[]{:T(128)} %convert_element_type.35, (f32[6,512]{1,0:T(8,128)S(1)}, f32[6,512]{1,0:T(8,128)S(1)}, f32[6,512,128]{2,1,0:T(8,128)S(1)}) %tuple.59, (s32[]{:T(128)}, s32[20]{0:T(128)S(1)}, s32[]{:T(128)}, ...), branch_computations={%region_2.1_spmd, %region_3.4_spmd} | conditional | flops 826809344 | bytes 49490116 | solution.py:325
  257.1 2.6 copy-done
  261.3 4.2 %multiply_add_fusion = f32[6,512,128]{2,1,0:T(8,128)S(1)} fusion(f32[6,512,128]{2,1,0:T(8,128)S(1)} %get-tuple-element.215, f32[512,512,6]{1,0,2:T(8,128)} %copy-done, f32[6,512]{1,0:T(8,128)S(1)} %max.2, pred[512,512]{0,1:T(8,128)(4,1)S(1)} %broadcast_compare_fusion, f32[6,512]{1,0:T(8,128)S(1)} %get-tuple-element.339, ...), kind=kOutput, calls=%fused_computation.8 | convolution fusion | flops 411303936 | bytes 9854984 | tf_op jit(solution)/shard_map/cond/branch_0_fun/while/body/eval_jaxpr/cond/branch_1_fun/grs,sd->grd/dot_general | solution.py:320
  266.8 12.1 %conditional.5 = ((f32[6,512]{1,0:T(8,128)S(1)}, f32[6,512]{1,0:T(8,128)S(1)}, f32[6,512,128]{2,1,0:T(8,128)S(1)})) conditional(s32[]{:T(128)} %convert_element_type.35, (f32[6,512]{1,0:T(8,128)S(1)}, f32[6,512]{1,0:T(8,128)S(1)}, f32[6,512,128]{2,1,0:T(8,128)S(1)}) %tuple.59, (s32[]{:T(128)}, s32[20]{0:T(128)S(1)}, s32[]{:T(128)}, ...), branch_computations={%region_2.1_spmd, %region_3.4_spmd} | conditional | flops 826809344 | bytes 49490116 | solution.py:325
  270.5 2.6 copy-done
  274.7 4.2 %multiply_add_fusion = f32[6,512,128]{2,1,0:T(8,128)S(1)} fusion(f32[6,512,128]{2,1,0:T(8,128)S(1)} %get-tuple-element.215, f32[512,512,6]{1,0,2:T(8,128)} %copy-done, f32[6,512]{1,0:T(8,128)S(1)} %max.2, pred[512,512]{0,1:T(8,128)(4,1)S(1)} %broadcast_compare_fusion, f32[6,512]{1,0:T(8,128)S(1)} %get-tuple-element.339, ...), kind=kOutput, calls=%fused_computation.8 | convolution fusion | flops 411303936 | bytes 9854984 | tf_op jit(solution)/shard_map/cond/branch_0_fun/while/body/eval_jaxpr/cond/branch_1_fun/grs,sd->grd/dot_general | solution.py:320
  280.3 12.1 %conditional.5 = ((f32[6,512]{1,0:T(8,128)S(1)}, f32[6,512]{1,0:T(8,128)S(1)}, f32[6,512,128]{2,1,0:T(8,128)S(1)})) conditional(s32[]{:T(128)} %convert_element_type.35, (f32[6,512]{1,0:T(8,128)S(1)}, f32[6,512]{1,0:T(8,128)S(1)}, f32[6,512,128]{2,1,0:T(8,128)S(1)}) %tuple.59, (s32[]{:T(128)}, s32[20]{0:T(128)S(1)}, s32[]{:T(128)}, ...), branch_computations={%region_2.1_spmd, %region_3.4_spmd} | conditional | flops 826809344 | bytes 49490116 | solution.py:325
  284.0 2.6 copy-done
  288.2 4.2 %multiply_add_fusion = f32[6,512,128]{2,1,0:T(8,128)S(1)} fusion(f32[6,512,128]{2,1,0:T(8,128)S(1)} %get-tuple-element.215, f32[512,512,6]{1,0,2:T(8,128)} %copy-done, f32[6,512]{1,0:T(8,128)S(1)} %max.2, pred[512,512]{0,1:T(8,128)(4,1)S(1)} %broadcast_compare_fusion, f32[6,512]{1,0:T(8,128)S(1)} %get-tuple-element.339, ...), kind=kOutput, calls=%fused_computation.8 | convolution fusion | flops 411303936 | bytes 9854984 | tf_op jit(solution)/shard_map/cond/branch_0_fun/while/body/eval_jaxpr/cond/branch_1_fun/grs,sd->grd/dot_general | solution.py:320
  293.7 12.1 %conditional.5 = ((f32[6,512]{1,0:T(8,128)S(1)}, f32[6,512]{1,0:T(8,128)S(1)}, f32[6,512,128]{2,1,0:T(8,128)S(1)})) conditional(s32[]{:T(128)} %convert_element_type.35, (f32[6,512]{1,0:T(8,128)S(1)}, f32[6,512]{1,0:T(8,128)S(1)}, f32[6,512,128]{2,1,0:T(8,128)S(1)}) %tuple.59, (s32[]{:T(128)}, s32[20]{0:T(128)S(1)}, s32[]{:T(128)}, ...), branch_computations={%region_2.1_spmd, %region_3.4_spmd} | conditional | flops 826809344 | bytes 49490116 | solution.py:325
  297.4 2.6 copy-done
  301.6 4.2 %multiply_add_fusion = f32[6,512,128]{2,1,0:T(8,128)S(1)} fusion(f32[6,512,128]{2,1,0:T(8,128)S(1)} %get-tuple-element.215, f32[512,512,6]{1,0,2:T(8,128)} %copy-done, f32[6,512]{1,0:T(8,128)S(1)} %max.2, pred[512,512]{0,1:T(8,128)(4,1)S(1)} %broadcast_compare_fusion, f32[6,512]{1,0:T(8,128)S(1)} %get-tuple-element.339, ...), kind=kOutput, calls=%fused_computation.8 | convolution fusion | flops 411303936 | bytes 9854984 | tf_op jit(solution)/shard_map/cond/branch_0_fun/while/body/eval_jaxpr/cond/branch_1_fun/grs,sd->grd/dot_general | solution.py:320
  307.2 12.1 %conditional.5 = ((f32[6,512]{1,0:T(8,128)S(1)}, f32[6,512]{1,0:T(8,128)S(1)}, f32[6,512,128]{2,1,0:T(8,128)S(1)})) conditional(s32[]{:T(128)} %convert_element_type.35, (f32[6,512]{1,0:T(8,128)S(1)}, f32[6,512]{1,0:T(8,128)S(1)}, f32[6,512,128]{2,1,0:T(8,128)S(1)}) %tuple.59, (s32[]{:T(128)}, s32[20]{0:T(128)S(1)}, s32[]{:T(128)}, ...), branch_computations={%region_2.1_spmd, %region_3.4_spmd} | conditional | flops 826809344 | bytes 49490116 | solution.py:325
  310.9 2.6 copy-done
  315.1 4.2 %multiply_add_fusion = f32[6,512,128]{2,1,0:T(8,128)S(1)} fusion(f32[6,512,128]{2,1,0:T(8,128)S(1)} %get-tuple-element.215, f32[512,512,6]{1,0,2:T(8,128)} %copy-done, f32[6,512]{1,0:T(8,128)S(1)} %max.2, pred[512,512]{0,1:T(8,128)(4,1)S(1)} %broadcast_compare_fusion, f32[6,512]{1,0:T(8,128)S(1)} %get-tuple-element.339, ...), kind=kOutput, calls=%fused_computation.8 | convolution fusion | flops 411303936 | bytes 9854984 | tf_op jit(solution)/shard_map/cond/branch_0_fun/while/body/eval_jaxpr/cond/branch_1_fun/grs,sd->grd/dot_general | solution.py:320
  332.2 2.4 collective-permute-start.13
  334.6 4.6 %carry.1.linear_ref = f32[512,768]{1,0:T(8,128)} custom-call(s32[1]{0:T(128)} %bitcast.18.mine_ref, bf16[512,768]{1,0:T(8,128)(2,1)} %query_ref.1, f32[512,768]{1,0:T(8,128)} %get-tuple-element.264.local_ref, f32[512,128]{1,0:T(8,128)} %get-tuple-element.265.grow_ref, f32[776,128]{1,0:T(8,128)} %hand.1.kept_ref, ...), custom_call_target="tpu_custom_call" | custom-call | flops 2000000000 | bytes 2000000 | tf_op jit(solution)/shard_map/carry/pallas_call | solution.py:370
  339.9 3.0 finish.1
  (270 shorter events, 120.0 us)
Async XLA Ops:
  0.0 8.5 %copy-start.3 = (bf16[512,128]{1,0:T(8,128)(2,1)S(1)}, bf16[512,128]{1,0:T(8,128)(2,1)}, u32[]{:S(2)}) copy-start(bf16[512,128]{1,0:T(8,128)(2,1)} %param.16) | copy-start | bytes 393220
  0.0 8.6 %copy-start.4 = (bf16[512,128]{1,0:T(8,128)(2,1)S(1)}, bf16[512,128]{1,0:T(8,128)(2,1)}, u32[]{:S(2)}) copy-start(bf16[512,128]{1,0:T(8,128)(2,1)} %param.17) | copy-start | bytes 393220
  7.8 2.2 collective-permute-start.14
  8.6 4.5 %collective-permute-start = (bf16[512,256]{1,0:T(8,128)(2,1)S(1)}, bf16[512,256]{1,0:T(8,128)(2,1)S(1)}, u32[]{:S(2)}, u32[]{:S(2)}) collective-permute-start(bf16[512,256]{1,0:T(8,128)(2,1)S(1)} %constant_dynamic-update-slice_fusion.12.refs_1_), channel_id=1, source_target_pairs={{0,8},{8,0},{16,24},{24,16},{32,40},{40,32},{48,56},{56,48},{64,72... | collective-permute-start | bytes 786440 | tf_op jit(solution)/shard_map/ppermute | solution.py:386
  10.1 0.8 copy-start.6
  10.9 41.9 %copy-start.1 = (bf16[512,768]{1,0:T(8,128)(2,1)S(1)}, bf16[512,768]{1,0:T(8,128)(2,1)}, u32[]{:S(2)}) copy-start(bf16[512,768]{1,0:T(8,128)(2,1)} %refs_0_.3) | copy-start | bytes 2359300
  12.9 12.1 %collective-permute-start.15 = (f32[776,128]{1,0:T(8,128)}, f32[776,128]{1,0:T(8,128)S(1)}, u32[]{:S(2)}, u32[]{:S(2)}) collective-permute-start(f32[776,128]{1,0:T(8,128)} %join.2.own_ref), channel_id=1, source_target_pairs={{0,16},{8,24},{16,0},{24,8},{32,48},{40,56},{48,32},{56,40},{64,80... | collective-permute-start | bytes 1191944 | tf_op jit(solution)/shard_map/ppermute | solution.py:386
  13.1 16.9 %collective-permute-start.3 = (bf16[1024,256]{1,0:T(8,128)(2,1)S(1)}, bf16[1024,256]{1,0:T(8,128)(2,1)S(1)}, u32[]{:S(2)}, u32[]{:S(2)}) collective-permute-start(bf16[1024,256]{1,0:T(8,128)(2,1)S(1)} %pad_maximum_fusion), channel_id=1, source_target_pairs={{0,32},{16,48},{32,64},{48,80},{64,96},{80,112},{8,104},{24,120},{... | collective-permute-start | bytes 1572872 | tf_op jit(solution)/shard_map/ppermute | solution.py:386
  14.4 20.1 %collective-permute-start.5 = (bf16[1024,256]{1,0:T(8,128)(2,1)S(1)}, bf16[1024,256]{1,0:T(8,128)(2,1)S(1)}, u32[]{:S(2)}, u32[]{:S(2)}) collective-permute-start(bf16[1024,256]{1,0:T(8,128)(2,1)S(1)} %pad_maximum_fusion), channel_id=1, source_target_pairs={{8,72},{24,88},{40,104},{56,120},{9,73},{25,89},{41,105},{57,121},... | collective-permute-start | bytes 1572872 | tf_op jit(solution)/shard_map/ppermute | solution.py:386
  15.7 21.2 %collective-permute-start.1 = (bf16[512,256]{1,0:T(8,128)(2,1)S(1)}, bf16[512,256]{1,0:T(8,128)(2,1)S(1)}, u32[]{:S(2)}, u32[]{:S(2)}) collective-permute-start(bf16[512,256]{1,0:T(8,128)(2,1)S(1)} %constant_dynamic-update-slice_fusion.12.refs_1_), channel_id=1, source_target_pairs={{0,16},{8,24},{16,0},{24,8},{32,48},{40,56},{64,80},{72,88},{96,11... | collective-permute-start | bytes 786440 | tf_op jit(solution)/shard_map/ppermute | solution.py:386
  25.0 0.7 copy-start.7
  27.7 10.6 %collective-permute-start.16 = (f32[776,128]{1,0:T(8,128)}, f32[776,128]{1,0:T(8,128)S(1)}, u32[]{:S(2)}, u32[]{:S(2)}) collective-permute-start(f32[776,128]{1,0:T(8,128)} %join.3), channel_id=1, source_target_pairs={{0,32},{16,48},{32,64},{48,80},{64,96},{80,112},{8,104},{24,120},{... | collective-permute-start | bytes 1191944 | tf_op jit(solution)/shard_map/ppermute | solution.py:386
  30.0 19.9 %collective-permute-start.7 = (bf16[1024,256]{1,0:T(8,128)(2,1)S(1)}, bf16[1024,256]{1,0:T(8,128)(2,1)S(1)}, u32[]{:S(2)}, u32[]{:S(2)}) collective-permute-start(bf16[1024,256]{1,0:T(8,128)(2,1)S(1)} %collective-permute-done.3.refs_5_), channel_id=1, source_target_pairs={{32,48},{48,32},{64,80},{80,64},{96,112},{104,120},{112,96},{120,1... | collective-permute-start | bytes 1572872 | tf_op jit(solution)/shard_map/ppermute | solution.py:386
  34.5 18.2 %collective-permute-start.9 = (bf16[1024,256]{1,0:T(8,128)(2,1)S(1)}, bf16[1024,256]{1,0:T(8,128)(2,1)}, u32[]{:S(2)}, u32[]{:S(2)}) collective-permute-start(bf16[1024,256]{1,0:T(8,128)(2,1)S(1)} %collective-permute-done.5.refs_4_), channel_id=1, source_target_pairs={{72,88},{88,72},{104,120},{120,104},{73,89},{89,73},{105,121},{121... | collective-permute-start | bytes 1572872 | tf_op jit(solution)/shard_map/ppermute | solution.py:386
  36.8 16.0 %collective-permute-start.4 = (bf16[1024,256]{1,0:T(8,128)(2,1)S(1)}, bf16[1024,256]{1,0:T(8,128)(2,1)}, u32[]{:S(2)}, u32[]{:S(2)}) collective-permute-start(bf16[1024,256]{1,0:T(8,128)(2,1)S(1)} %collective-permute-done.3.refs_5_), channel_id=1, source_target_pairs={{0,8},{8,0},{16,24},{24,16},{32,40},{40,32},{48,56},{56,48},{64,72... | collective-permute-start | bytes 1572872 | tf_op jit(solution)/shard_map/ppermute | solution.py:386
  36.9 10.3 %collective-permute-start.17 = (f32[776,128]{1,0:T(8,128)}, f32[776,128]{1,0:T(8,128)S(1)}, u32[]{:S(2)}, u32[]{:S(2)}) collective-permute-start(f32[776,128]{1,0:T(8,128)} %join.3), channel_id=1, source_target_pairs={{8,72},{24,88},{40,104},{56,120},{9,73},{25,89},{41,105},{57,121},... | collective-permute-start | bytes 1191944 | tf_op jit(solution)/shard_map/ppermute | solution.py:386
  38.2 9.0 %copy-start.8 = (f32[776,128]{1,0:T(8,128)}, f32[776,128]{1,0:T(8,128)S(1)}, u32[]{:S(2)}) copy-start(f32[776,128]{1,0:T(8,128)S(1)} %collective-permute-done.16.behind_ref) | copy-start | bytes 1191940
  38.2 11.6 %collective-permute-start.2 = (bf16[512,256]{1,0:T(8,128)(2,1)S(1)}, bf16[512,256]{1,0:T(8,128)(2,1)S(1)}, u32[]{:S(2)}, u32[]{:S(2)}) collective-permute-start(bf16[512,256]{1,0:T(8,128)(2,1)S(1)} %collective-permute-done.1.refs_3_), channel_id=1, source_target_pairs={{0,8},{8,0},{16,24},{24,16},{32,40},{40,32},{48,56},{56,48},{64,72... | collective-permute-start | bytes 786440 | tf_op jit(solution)/shard_map/ppermute | solution.py:386
  47.2 0.7 copy-start.9
  47.2 24.5 %collective-permute-start.6 = (bf16[1024,256]{1,0:T(8,128)(2,1)S(1)}, bf16[1024,256]{1,0:T(8,128)(2,1)}, u32[]{:S(2)}, u32[]{:S(2)}) collective-permute-start(bf16[1024,256]{1,0:T(8,128)(2,1)S(1)} %collective-permute-done.5.refs_4_), channel_id=1, source_target_pairs={{0,8},{8,0},{16,24},{24,16},{32,40},{40,32},{48,56},{56,48},{64,72... | collective-permute-start | bytes 1572872 | tf_op jit(solution)/shard_map/ppermute | solution.py:386
  49.9 284.8 %collective-permute-start.18 = (f32[776,128]{1,0:T(8,128)}, f32[776,128]{1,0:T(8,128)}, u32[]{:S(2)}, u32[]{:S(2)}) collective-permute-start(f32[776,128]{1,0:T(8,128)} %hand.1.kept_ref), channel_id=1, source_target_pairs={{0,8},{8,0},{16,24},{24,16},{32,40},{40,32},{48,56},{56,48},{64,72... | collective-permute-start | bytes 1191944 | tf_op jit(solution)/shard_map/ppermute | solution.py:386
  49.9 21.8 %collective-permute-start.8 = (bf16[1024,256]{1,0:T(8,128)(2,1)S(1)}, bf16[1024,256]{1,0:T(8,128)(2,1)}, u32[]{:S(2)}, u32[]{:S(2)}) collective-permute-start(bf16[1024,256]{1,0:T(8,128)(2,1)S(1)} %collective-permute-done.7.refs_6_), channel_id=1, source_target_pairs={{0,8},{8,0},{16,24},{24,16},{32,40},{40,32},{48,56},{56,48},{64,72... | collective-permute-start | bytes 1572872 | tf_op jit(solution)/shard_map/ppermute | solution.py:386
  52.8 18.9 %collective-permute-start.10 = (bf16[1024,256]{1,0:T(8,128)(2,1)}, bf16[1024,256]{1,0:T(8,128)(2,1)}, u32[]{:S(2)}, u32[]{:S(2)}) collective-permute-start(bf16[1024,256]{1,0:T(8,128)(2,1)} %collective-permute-done.9.refs_8_), channel_id=1, source_target_pairs={{0,8},{8,0},{16,24},{24,16},{32,40},{40,32},{48,56},{56,48},{64,72... | collective-permute-start | bytes 1572872 | tf_op jit(solution)/shard_map/ppermute | solution.py:386
  98.1 2.3 copy-start.2
  106.3 2.6 copy-start
  119.7 2.6 copy-start
  133.2 2.6 copy-start
  146.6 2.6 copy-start
  160.1 2.6 copy-start
  173.5 2.6 copy-start
  187.0 2.6 copy-start
  200.5 2.6 copy-start
  213.9 2.6 copy-start
  227.4 2.6 copy-start
  243.6 2.6 copy-start
  257.1 2.6 copy-start
  270.5 2.6 copy-start
  284.0 2.6 copy-start
  297.4 2.6 copy-start
  310.9 2.6 copy-start
  326.5 13.3 %copy-start.11 = (bf16[512,768]{1,0:T(8,128)(2,1)S(1)}, bf16[512,768]{1,0:T(8,128)(2,1)}, u32[]{:S(2)}) copy-start(bf16[512,768]{1,0:T(8,128)(2,1)} %get-tuple-element.319.attention_ref) | copy-start | bytes 2359300
  326.5 3.1 collective-permute-start.11
  329.6 2.6 collective-permute-start.12
  332.2 7.0 %copy-start.5 = (f32[8,512]{1,0:T(8,128)}, f32[8,512]{1,0:T(8,128)S(1)}, u32[]{:S(2)}) copy-start(f32[8,512]{1,0:T(8,128)S(1)} %add.97.square_ref) | copy-start | bytes 49156
  332.2 7.0 %collective-permute-start.13 = (f32[8,512]{1,0:T(8,128)S(1)}, f32[8,512]{1,0:T(8,128)S(1)}, u32[]{:S(2)}, u32[]{:S(2)}) collective-permute-start(f32[8,512]{1,0:T(8,128)S(1)} %add.97.square_ref), channel_id=1, source_target_pairs={{0,4},{1,5},{2,6},{3,7},{4,0},{5,1},{6,2},{7,3},{8,12},{9,13},{10,... | collective-permute-start | bytes 49160 | tf_op jit(solution)/shard_map/ppermute | solution.py:479
  339.3 0.6 copy-start.10

commit v3 on v2

--- a/solution.py
+++ b/solution.py
@@ -31,8 +31,8 @@
     return lax.dot_general(a, b, (contract, ((), ())), precision=precision, preferred_element_type=f32)
 
 
-def params():
-    return pltpu.CompilerParams(vmem_limit_bytes=56 << 20)
+def params(megabytes):
+    return pltpu.CompilerParams(vmem_limit_bytes=megabytes << 20)
 
 
 def cost(us):
@@ -44,15 +44,16 @@
 
 
 def recur_kernel(q_ref, k_ref, v_ref, step_ref, local_ref, grow_ref, message_ref, padded):
-    padded[...] = jnp.full((ROWS, HD), 0.5, f32)
-    padded[:, :HEADS] = step_ref[...]
-    step = jnp.transpose(padded[...])[:8, :]
+    padded[...] = jnp.full((8, ROWS), 0.5, f32)
+    padded[:HEADS, :] = step_ref[...]
+    step = padded[...]
     rate = step / (1.0 + step)
-    log_decay = -jnp.log(1.0 + step) * LOG2E
-    earlier = lax.broadcasted_iota(jnp.int32, (ROWS, ROWS), 0)
-    later = lax.broadcasted_iota(jnp.int32, (ROWS, ROWS), 1)
-    upper = jnp.where(earlier <= later, 1.0, 0.0).astype(f32)
-    total = dot(log_decay, upper, precision=highest)
+    total = -jnp.log(1.0 + step) * LOG2E
+    place = lax.broadcasted_iota(jnp.int32, (8, ROWS), 1)
+    reach = 1
+    while reach < ROWS:
+        total = total + jnp.where(place >= reach, pltpu.roll(total, reach, 1), 0.0)
+        reach *= 2
     source = jnp.log(rate) * LOG2E - total
     end = total[:, ROWS - 1 : ROWS]
     tail = jnp.exp2(end + source)
@@ -93,11 +94,11 @@
         ),
         in_specs=[VMEM] * 4,
         out_specs=(VMEM,) * 3,
-        scratch_shapes=[pltpu.VMEM((ROWS, HD), f32)],
-        compiler_params=params(),
+        scratch_shapes=[pltpu.VMEM((8, ROWS), f32)],
+        compiler_params=params(16),
         cost_estimate=cost(2.5),
         name="recur",
-    )(lh_query, lh_key, lh_value, lh_step)
+    )(lh_query, lh_key, lh_value, lh_step.T)
 
 
 def follow(early, late):
@@ -136,7 +137,7 @@
         out_shape=jax.ShapeDtypeStruct((STATE_ROWS, HD), f32),
         in_specs=[SMEM, VMEM, VMEM],
         out_specs=VMEM,
-        compiler_params=params(),
+        compiler_params=params(14),
         cost_estimate=cost(1.0),
         name="join",
     )(mine, own, other)
@@ -155,7 +156,7 @@
         out_shape=jax.ShapeDtypeStruct((STATE_ROWS, HD), f32),
         in_specs=[SMEM, VMEM, VMEM],
         out_specs=VMEM,
-        compiler_params=params(),
+        compiler_params=params(14),
         cost_estimate=cost(1.0),
         name="hand",
     )(mine, behind, beyond)
@@ -181,14 +182,11 @@
 
     for h in range(HEADS):
         scaled[h * ROWS : (h + 1) * ROWS, :] = (query_ref[:, head(h)].astype(f32) * SCORE_SCALE).astype(bf16)
+    sums[...] = jnp.zeros_like(sums)
     if first:
-        sums[...] = jnp.zeros_like(sums)
         top_ref[0:8, :] = norm(scaled[...])
         top_ref[8:16, :] = norm(own_ref[:, :HD])
     else:
-        for h in range(HEADS):
-            sums[h, :, :HD] = carry_ref[:, head(h)]
-            sums[h, :, HD:] = jnp.broadcast_to(count_ref[:, h : h + 1], (ROWS, HD))
         top_ref[...] = top_in_ref[...]
     values[:, HD:] = jnp.ones((values.shape[0], HD), bf16)
 
@@ -244,13 +242,14 @@
             numerator_ref[:, head(h)] = sums[h, :, :HD]
             counted_ref[:, h : h + 1] = sums[h, :, HD : HD + 1]
     else:
-        squares = jnp.zeros((8, ROWS), f32)
+        squares = jnp.zeros((ROWS, HD), f32)
         for h in range(HEADS):
-            result = (sums[h, :, :HD] / sums[h, :, HD:]).astype(bf16)
+            count = sums[h, :, HD:] + count_ref[:, h : h + 1]
+            result = ((sums[h, :, :HD] + carry_ref[:, head(h)]) / count).astype(bf16)
             out_ref[:, head(h)] = result
             result = result.astype(f32)
-            squares = squares + dot(jnp.ones((8, HD), bf16), (result * result).astype(bf16), ((1,), (1,)))
-        square_ref[...] = squares
+            squares = squares + result * result
+        square_ref[...] = dot(jnp.ones((8, HD), f32), squares, ((1,), (1,)), highest)
         bound = jnp.max(top_ref[:8, :]) * jnp.max(top_ref[8:, :])
         safe_ref[0] = jnp.where(bound * 1.05 <= SAFE_EXPONENT * SAFE_EXPONENT, 1, 0)
 
@@ -287,7 +286,7 @@
         in_specs=[SMEM] + [VMEM] * len(operands),
         out_specs=out_specs,
         scratch_shapes=scratch,
-        compiler_params=params(),
+        compiler_params=params(26),
         cost_estimate=cost(14.0),
         name="attend_near" if first else "attend_far",
     )(mine, *operands)
@@ -372,7 +371,7 @@
         out_shape=jax.ShapeDtypeStruct((ROWS, HEADS * HD), dtype),
         in_specs=[SMEM] * len(scalar) + [VMEM] * len(operands),
         out_specs=VMEM,
-        compiler_params=params(),
+        compiler_params=params(14),
         cost_estimate=cost(2.0),
         name=name,
     )(*scalar, *operands)
@@ -395,6 +394,7 @@
     across = move(own, [(i, i ^ 2) for i in every if i < 4 or i % 4 < 2])
     near = move(own, sibling)
     chip = jnp.concatenate([own, near], 0)
+    chip, lh_step = lax.optimization_barrier((chip, lh_step))
     behind = move(chip, last_plane)
     beyond = move(chip, plane_before)
 
@@ -445,7 +445,11 @@
         ]
 
     near_blocks = [near, across, across_near, behind, behind_near]
+    near_blocks, of_chip = lax.optimization_barrier((near_blocks, of_chip))
     carry = attend(place, att_query, own, None, near_blocks, near_numbers)
+    carry, other_chip, beyond, level, level_beyond = lax.optimization_barrier(
+        (carry, other_chip, beyond, level, level_beyond)
+    )
 
     of_plane = join(2, place, of_chip, other_chip)
     state_behind = move(of_plane, last_plane)
@@ -455,7 +459,9 @@
     level_near = move(level, sibling)
     level_beyond_near = move(level_beyond, sibling)
     far_blocks = [beyond, beyond_near, level, level_near, level_beyond, level_beyond_near]
+    far_blocks, of_plane = lax.optimization_barrier((far_blocks, of_plane))
     attention, squares, safe = attend(place, att_query, None, carry, far_blocks, far_numbers)
+    safe, state_behind, state_beyond = lax.optimization_barrier((safe, state_behind, state_beyond))
 
     def shifted():
         _, side, core, even = parts(mine)

time: 345 us -> 381 us (1.10)
  matrix products: 100 us -> 143 us
  Pallas kernels: 58.5 us -> 44 us
  local copies, waits for them, and re-layouts: 81.5 us -> 91.9 us
    dot_general x16, matrix products: 67 us -> 105 us  [visit(): jnp.einsum('grs,sd->grd', weights.astype(bf16), block[:, HD:], preferred_...]
    dot_general x16, matrix products: 33.4 us -> 38.2 us  [visit(): jnp.einsum('rgd,sd->grs', grouped, block[:, :HD], preferred_element_type=...]
    pallas_call x2, Pallas kernels: 7.58 us -> 2.84 us  [simple(): pl.pallas_call(kernel, out_shape=jax.ShapeDtypeStruct((ROWS, HEADS * HD),...]
    cond x62 -> x64, local copies, waits for them, and re-layouts: 49.1 us -> 53 us
    unnamed x22 -> x29, local copies, waits for them, and re-layouts: 4.49 us -> 7.88 us
  transfers between devices with their start and end apart: 19 -> 19, of which waited for: 7 -> 7; matrix products, arithmetic and copies ran while one was open for 48% -> 56% of each run, Pallas kernels for 14% -> 11%
where the time goes in v3:
time: 381 us; the launch traced here: 379 us
  matrix products  143 us (38%)
  local copies, waits for them, and re-layouts  91.9 us (24%)
  Pallas kernels  44 us (12%)
  other arithmetic  30.7 us (8%)
  loops' own time  25 us (7%)
  waiting for transfers between devices  23.5 us (6%)
  starting transfers between devices  20.5 us (5%)
    dot_general x16, matrix products, visit(): jnp.einsum('grs,sd->grd', weights.astype(bf16), block[:, HD:], preferred_...  105 us
    cond x64, local copies, waits for them, and re-layouts  53 us
    dot_general x16, matrix products, visit(): jnp.einsum('rgd,sd->grs', grouped, block[:, :HD], preferred_element_type=...  38.2 us
    pallas_call x2, Pallas kernels, attend(): pl.pallas_call(functools.partial(attend_kernel, first, numbers_of, len(bl...  37.5 us
    reduce_sum x16, other arithmetic, visit(): return (new_top, totals * rescale + jnp.sum(weights, -1), numerator)  24.3 us
    ppermute x16, waiting for transfers between devices, move(): return lax.ppermute(value, 'ctx', pairs)  20.5 us
    ppermute x16, starting transfers between devices, move(): return lax.ppermute(value, 'ctx', pairs)  15.3 us
    another operation x1, loops' own time, attend_shifted(): _, totals, numerator = lax.fori_loop(0, count, step, initial)  13 us
  transfers between devices with their start and end apart: 19, of which 7 were waited for; matrix products, arithmetic and copies ran while one was open for 56% of the time, Pallas kernels for 11%

profile of v3, /device:TPU:101, one launch (start us, length us, event | category | flops | bytes accessed | tf_op | source)
XLA Modules:
  0.0 379.3 jit_solution(2143663619600129250)
XLA Ops:
  8.5 13.1 %collective-permute-done.3.refs_5_ = bf16[1024,256]{1,0:T(8,128)(2,1)S(1)} collective-permute-done((bf16[1024,256]{1,0:T(8,128)(2,1)}, bf16[1024,256]{1,0:T(8,128)(2,1)S(1)}, u32[]{:S(2)}, u32[]{:S(2)}) %collective-permute-start.3) | collective-permute-done | bytes 524320 | tf_op jit(solution)/shard_map/ppermute | solution.py:385
  25.9 3.5 recur.1
  32.5 4.9 %collective-permute-start.8 = (bf16[1024,256]{1,0:T(8,128)(2,1)S(1)}, bf16[1024,256]{1,0:T(8,128)(2,1)}, u32[]{:S(2)}, u32[]{:S(2)}) collective-permute-start(bf16[1024,256]{1,0:T(8,128)(2,1)S(1)} %collective-permute-done.3.refs_5_), channel_id=1, source_target_pairs={{32,48},{48,32},{64,80},{80,64},{96,112},{104,120},{112,96},{120,1... | collective-permute-start | bytes 1572872 | tf_op jit(solution)/shard_map/ppermute | solution.py:385
  39.3 18.0 %attend_near.1 = (f32[512,768]{1,0:T(8,128)S(1)}, f32[512,128]{1,0:T(8,128)S(1)}, f32[16,128]{1,0:T(8,128)S(1)}) custom-call(s32[1]{0:T(128)} %bitcast.18.mine_ref, bf16[512,768]{1,0:T(8,128)(2,1)S(1)} %copy-done.10, bf16[512,256]{1,0:T(8,128)(2,1)S(1)} %constant_dynamic-update-slice_fusion.12.refs_1_, bf16[512,256]{1,0:T(8,128)(2,1)S(1)} %collective-permute-done.refs_2_, ...), custom_call_target="tpu_custom_call" | custom-call | flops 14000000000 | bytes 14000000 | tf_op jit(solution)/shard_map/attend_near/pallas_call | solution.py:283
  57.4 4.5 %collective-permute-done.9.refs_8_ = bf16[1024,256]{1,0:T(8,128)(2,1)} collective-permute-done((bf16[1024,256]{1,0:T(8,128)(2,1)}, bf16[1024,256]{1,0:T(8,128)(2,1)}, u32[]{:S(2)}, u32[]{:S(2)}) %collective-permute-start.9) | collective-permute-done | bytes 524320 | tf_op jit(solution)/shard_map/ppermute | solution.py:385
  65.6 19.5 %attend_far.1 = (bf16[512,768]{1,0:T(8,128)(2,1)}, f32[8,512]{1,0:T(8,128)S(1)}, s32[1]{0:T(128)}) custom-call(s32[1]{0:T(128)} %bitcast.18.mine_ref, bf16[512,768]{1,0:T(8,128)(2,1)S(1)} %copy-done.10, f32[512,768]{1,0:T(8,128)S(1)} %get-tuple-element.291.refs_1_, f32[512,128]{1,0:T(8,128)S(1)} %get-tuple-element.292.refs_2_, ...), custom_call_target="tpu_custom_call" | custom-call | flops 14000000000 | bytes 14000000 | tf_op jit(solution)/shard_map/attend_far/pallas_call | solution.py:283
  86.2 280.7 %conditional.2 = (f32[8,512]{1,0:T(8,128)S(1)}, bf16[512,768]{1,0:T(8,128)(2,1)}) conditional(s32[]{:T(128)} %bitcast.20, (s32[]{:T(128)}, bf16[512,256]{1,0:T(8,128)(2,1)S(1)}, bf16[512,256]{1,0:T(8,128)(2,1)S(1)}, bf16[512,256]{1,0:T(8,128)(2,1)S(1)}, bf16[512,256]{1,0:T(8,128)(2,1)}, /*index=5*/bf16[1024,256]{1,0:T(8,128)(2,1)}, ...), branch_computations={%region_0.8_spmd, %region_8.9_spmd} | conditional | flops 828774976 | bytes 94901680 | solution.py:476
  101.5 259.4 %while.17 = (s32[]{:T(128)}, f32[6,512]{1,0:T(8,128)S(1)}, f32[6,512]{1,0:T(8,128)S(1)}, f32[6,512,128]{2,1,0:T(8,128)}, s32[20]{0:T(128)S(1)}, /*index=5*/s32[]...) while((s32[]{:T(128)}, f32[6,512]{1,0:T(8,128)S(1)}, ...), condition=%wide.region_6.6_spmd.clone, body=%wide.region_1.5_spmd.clone.sunk | while | flops 826809344 | bytes 49492384 | solution.py:326
  102.8 14.6 %conditional.5 = ((f32[6,512]{1,0:T(8,128)S(1)}, f32[6,512]{1,0:T(8,128)S(1)}, f32[6,512,128]{2,1,0:T(8,128)})) conditional(s32[]{:T(128)} %convert_element_type.35, (f32[6,512]{1,0:T(8,128)S(1)}, f32[6,512]{1,0:T(8,128)S(1)}, f32[6,512,128]{2,1,0:T(8,128)}) %tuple.69, (s32[]{:T(128)}, s32[20]{0:T(128)S(1)}, s32[]{:T(128)}, ...), branch_computations={%region_2.1_spmd, %region_3.4_spmd} | conditional | flops 826809344 | bytes 49490116 | solution.py:324
  106.7 2.6 copy-done.9
  110.9 6.5 %multiply_add_fusion = f32[6,512,128]{2,1,0:T(8,128)} fusion(f32[6,512,128]{2,1,0:T(8,128)} %get-tuple-element.215, f32[512,512,6]{1,0,2:T(8,128)} %copy-done.9, f32[6,512]{1,0:T(8,128)S(1)} %max.2, pred[512,512]{0,1:T(8,128)(4,1)S(1)} %broadcast_compare_fusion, f32[6,512]{1,0:T(8,128)S(1)} %get-tuple-element.387, ...), kind=kOutput, calls=%fused_computation.8 | convolution fusion | flops 411303936 | bytes 9854984 | tf_op jit(solution)/shard_map/cond/branch_0_fun/while/body/eval_jaxpr/cond/branch_1_fun/grs,sd->grd/dot_general | solution.py:319
  118.7 14.6 %conditional.5 = ((f32[6,512]{1,0:T(8,128)S(1)}, f32[6,512]{1,0:T(8,128)S(1)}, f32[6,512,128]{2,1,0:T(8,128)})) conditional(s32[]{:T(128)} %convert_element_type.35, (f32[6,512]{1,0:T(8,128)S(1)}, f32[6,512]{1,0:T(8,128)S(1)}, f32[6,512,128]{2,1,0:T(8,128)}) %tuple.69, (s32[]{:T(128)}, s32[20]{0:T(128)S(1)}, s32[]{:T(128)}, ...), branch_computations={%region_2.1_spmd, %region_3.4_spmd} | conditional | flops 826809344 | bytes 49490116 | solution.py:324
  122.6 2.6 copy-done.9
  126.8 6.5 %multiply_add_fusion = f32[6,512,128]{2,1,0:T(8,128)} fusion(f32[6,512,128]{2,1,0:T(8,128)} %get-tuple-element.215, f32[512,512,6]{1,0,2:T(8,128)} %copy-done.9, f32[6,512]{1,0:T(8,128)S(1)} %max.2, pred[512,512]{0,1:T(8,128)(4,1)S(1)} %broadcast_compare_fusion, f32[6,512]{1,0:T(8,128)S(1)} %get-tuple-element.387, ...), kind=kOutput, calls=%fused_computation.8 | convolution fusion | flops 411303936 | bytes 9854984 | tf_op jit(solution)/shard_map/cond/branch_0_fun/while/body/eval_jaxpr/cond/branch_1_fun/grs,sd->grd/dot_general | solution.py:319
  134.6 14.6 %conditional.5 = ((f32[6,512]{1,0:T(8,128)S(1)}, f32[6,512]{1,0:T(8,128)S(1)}, f32[6,512,128]{2,1,0:T(8,128)})) conditional(s32[]{:T(128)} %convert_element_type.35, (f32[6,512]{1,0:T(8,128)S(1)}, f32[6,512]{1,0:T(8,128)S(1)}, f32[6,512,128]{2,1,0:T(8,128)}) %tuple.69, (s32[]{:T(128)}, s32[20]{0:T(128)S(1)}, s32[]{:T(128)}, ...), branch_computations={%region_2.1_spmd, %region_3.4_spmd} | conditional | flops 826809344 | bytes 49490116 | solution.py:324
  138.5 2.6 copy-done.9
  142.7 6.5 %multiply_add_fusion = f32[6,512,128]{2,1,0:T(8,128)} fusion(f32[6,512,128]{2,1,0:T(8,128)} %get-tuple-element.215, f32[512,512,6]{1,0,2:T(8,128)} %copy-done.9, f32[6,512]{1,0:T(8,128)S(1)} %max.2, pred[512,512]{0,1:T(8,128)(4,1)S(1)} %broadcast_compare_fusion, f32[6,512]{1,0:T(8,128)S(1)} %get-tuple-element.387, ...), kind=kOutput, calls=%fused_computation.8 | convolution fusion | flops 411303936 | bytes 9854984 | tf_op jit(solution)/shard_map/cond/branch_0_fun/while/body/eval_jaxpr/cond/branch_1_fun/grs,sd->grd/dot_general | solution.py:319
  150.5 14.6 %conditional.5 = ((f32[6,512]{1,0:T(8,128)S(1)}, f32[6,512]{1,0:T(8,128)S(1)}, f32[6,512,128]{2,1,0:T(8,128)})) conditional(s32[]{:T(128)} %convert_element_type.35, (f32[6,512]{1,0:T(8,128)S(1)}, f32[6,512]{1,0:T(8,128)S(1)}, f32[6,512,128]{2,1,0:T(8,128)}) %tuple.69, (s32[]{:T(128)}, s32[20]{0:T(128)S(1)}, s32[]{:T(128)}, ...), branch_computations={%region_2.1_spmd, %region_3.4_spmd} | conditional | flops 826809344 | bytes 49490116 | solution.py:324
  152.0 2.4 fusion.2
  154.4 2.6 copy-done.9
  158.6 6.5 %multiply_add_fusion = f32[6,512,128]{2,1,0:T(8,128)} fusion(f32[6,512,128]{2,1,0:T(8,128)} %get-tuple-element.215, f32[512,512,6]{1,0,2:T(8,128)} %copy-done.9, f32[6,512]{1,0:T(8,128)S(1)} %max.2, pred[512,512]{0,1:T(8,128)(4,1)S(1)} %broadcast_compare_fusion, f32[6,512]{1,0:T(8,128)S(1)} %get-tuple-element.387, ...), kind=kOutput, calls=%fused_computation.8 | convolution fusion | flops 411303936 | bytes 9854984 | tf_op jit(solution)/shard_map/cond/branch_0_fun/while/body/eval_jaxpr/cond/branch_1_fun/grs,sd->grd/dot_general | solution.py:319
  166.3 14.6 %conditional.5 = ((f32[6,512]{1,0:T(8,128)S(1)}, f32[6,512]{1,0:T(8,128)S(1)}, f32[6,512,128]{2,1,0:T(8,128)})) conditional(s32[]{:T(128)} %convert_element_type.35, (f32[6,512]{1,0:T(8,128)S(1)}, f32[6,512]{1,0:T(8,128)S(1)}, f32[6,512,128]{2,1,0:T(8,128)}) %tuple.69, (s32[]{:T(128)}, s32[20]{0:T(128)S(1)}, s32[]{:T(128)}, ...), branch_computations={%region_2.1_spmd, %region_3.4_spmd} | conditional | flops 826809344 | bytes 49490116 | solution.py:324
  167.9 2.4 fusion.2
  170.3 2.6 copy-done.9
  174.4 6.5 %multiply_add_fusion = f32[6,512,128]{2,1,0:T(8,128)} fusion(f32[6,512,128]{2,1,0:T(8,128)} %get-tuple-element.215, f32[512,512,6]{1,0,2:T(8,128)} %copy-done.9, f32[6,512]{1,0:T(8,128)S(1)} %max.2, pred[512,512]{0,1:T(8,128)(4,1)S(1)} %broadcast_compare_fusion, f32[6,512]{1,0:T(8,128)S(1)} %get-tuple-element.387, ...), kind=kOutput, calls=%fused_computation.8 | convolution fusion | flops 411303936 | bytes 9854984 | tf_op jit(solution)/shard_map/cond/branch_0_fun/while/body/eval_jaxpr/cond/branch_1_fun/grs,sd->grd/dot_general | solution.py:319
  182.2 14.6 %conditional.5 = ((f32[6,512]{1,0:T(8,128)S(1)}, f32[6,512]{1,0:T(8,128)S(1)}, f32[6,512,128]{2,1,0:T(8,128)})) conditional(s32[]{:T(128)} %convert_element_type.35, (f32[6,512]{1,0:T(8,128)S(1)}, f32[6,512]{1,0:T(8,128)S(1)}, f32[6,512,128]{2,1,0:T(8,128)}) %tuple.69, (s32[]{:T(128)}, s32[20]{0:T(128)S(1)}, s32[]{:T(128)}, ...), branch_computations={%region_2.1_spmd, %region_3.4_spmd} | conditional | flops 826809344 | bytes 49490116 | solution.py:324
  183.8 2.4 fusion.2
  186.2 2.6 copy-done.9
  190.3 6.5 %multiply_add_fusion = f32[6,512,128]{2,1,0:T(8,128)} fusion(f32[6,512,128]{2,1,0:T(8,128)} %get-tuple-element.215, f32[512,512,6]{1,0,2:T(8,128)} %copy-done.9, f32[6,512]{1,0:T(8,128)S(1)} %max.2, pred[512,512]{0,1:T(8,128)(4,1)S(1)} %broadcast_compare_fusion, f32[6,512]{1,0:T(8,128)S(1)} %get-tuple-element.387, ...), kind=kOutput, calls=%fused_computation.8 | convolution fusion | flops 411303936 | bytes 9854984 | tf_op jit(solution)/shard_map/cond/branch_0_fun/while/body/eval_jaxpr/cond/branch_1_fun/grs,sd->grd/dot_general | solution.py:319
  198.1 14.6 %conditional.5 = ((f32[6,512]{1,0:T(8,128)S(1)}, f32[6,512]{1,0:T(8,128)S(1)}, f32[6,512,128]{2,1,0:T(8,128)})) conditional(s32[]{:T(128)} %convert_element_type.35, (f32[6,512]{1,0:T(8,128)S(1)}, f32[6,512]{1,0:T(8,128)S(1)}, f32[6,512,128]{2,1,0:T(8,128)}) %tuple.69, (s32[]{:T(128)}, s32[20]{0:T(128)S(1)}, s32[]{:T(128)}, ...), branch_computations={%region_2.1_spmd, %region_3.4_spmd} | conditional | flops 826809344 | bytes 49490116 | solution.py:324
  199.6 2.4 fusion.2
  202.1 2.6 copy-done.9
  206.2 6.5 %multiply_add_fusion = f32[6,512,128]{2,1,0:T(8,128)} fusion(f32[6,512,128]{2,1,0:T(8,128)} %get-tuple-element.215, f32[512,512,6]{1,0,2:T(8,128)} %copy-done.9, f32[6,512]{1,0:T(8,128)S(1)} %max.2, pred[512,512]{0,1:T(8,128)(4,1)S(1)} %broadcast_compare_fusion, f32[6,512]{1,0:T(8,128)S(1)} %get-tuple-element.387, ...), kind=kOutput, calls=%fused_computation.8 | convolution fusion | flops 411303936 | bytes 9854984 | tf_op jit(solution)/shard_map/cond/branch_0_fun/while/body/eval_jaxpr/cond/branch_1_fun/grs,sd->grd/dot_general | solution.py:319
  214.0 14.6 %conditional.5 = ((f32[6,512]{1,0:T(8,128)S(1)}, f32[6,512]{1,0:T(8,128)S(1)}, f32[6,512,128]{2,1,0:T(8,128)})) conditional(s32[]{:T(128)} %convert_element_type.35, (f32[6,512]{1,0:T(8,128)S(1)}, f32[6,512]{1,0:T(8,128)S(1)}, f32[6,512,128]{2,1,0:T(8,128)}) %tuple.69, (s32[]{:T(128)}, s32[20]{0:T(128)S(1)}, s32[]{:T(128)}, ...), branch_computations={%region_2.1_spmd, %region_3.4_spmd} | conditional | flops 826809344 | bytes 49490116 | solution.py:324
  215.5 2.4 fusion.2
  218.0 2.6 copy-done.9
  222.1 6.5 %multiply_add_fusion = f32[6,512,128]{2,1,0:T(8,128)} fusion(f32[6,512,128]{2,1,0:T(8,128)} %get-tuple-element.215, f32[512,512,6]{1,0,2:T(8,128)} %copy-done.9, f32[6,512]{1,0:T(8,128)S(1)} %max.2, pred[512,512]{0,1:T(8,128)(4,1)S(1)} %broadcast_compare_fusion, f32[6,512]{1,0:T(8,128)S(1)} %get-tuple-element.387, ...), kind=kOutput, calls=%fused_computation.8 | convolution fusion | flops 411303936 | bytes 9854984 | tf_op jit(solution)/shard_map/cond/branch_0_fun/while/body/eval_jaxpr/cond/branch_1_fun/grs,sd->grd/dot_general | solution.py:319
  229.9 14.6 %conditional.5 = ((f32[6,512]{1,0:T(8,128)S(1)}, f32[6,512]{1,0:T(8,128)S(1)}, f32[6,512,128]{2,1,0:T(8,128)})) conditional(s32[]{:T(128)} %convert_element_type.35, (f32[6,512]{1,0:T(8,128)S(1)}, f32[6,512]{1,0:T(8,128)S(1)}, f32[6,512,128]{2,1,0:T(8,128)}) %tuple.69, (s32[]{:T(128)}, s32[20]{0:T(128)S(1)}, s32[]{:T(128)}, ...), branch_computations={%region_2.1_spmd, %region_3.4_spmd} | conditional | flops 826809344 | bytes 49490116 | solution.py:324
  233.8 2.6 copy-done.9
  238.0 6.5 %multiply_add_fusion = f32[6,512,128]{2,1,0:T(8,128)} fusion(f32[6,512,128]{2,1,0:T(8,128)} %get-tuple-element.215, f32[512,512,6]{1,0,2:T(8,128)} %copy-done.9, f32[6,512]{1,0:T(8,128)S(1)} %max.2, pred[512,512]{0,1:T(8,128)(4,1)S(1)} %broadcast_compare_fusion, f32[6,512]{1,0:T(8,128)S(1)} %get-tuple-element.387, ...), kind=kOutput, calls=%fused_computation.8 | convolution fusion | flops 411303936 | bytes 9854984 | tf_op jit(solution)/shard_map/cond/branch_0_fun/while/body/eval_jaxpr/cond/branch_1_fun/grs,sd->grd/dot_general | solution.py:319
  245.8 14.6 %conditional.5 = ((f32[6,512]{1,0:T(8,128)S(1)}, f32[6,512]{1,0:T(8,128)S(1)}, f32[6,512,128]{2,1,0:T(8,128)})) conditional(s32[]{:T(128)} %convert_element_type.35, (f32[6,512]{1,0:T(8,128)S(1)}, f32[6,512]{1,0:T(8,128)S(1)}, f32[6,512,128]{2,1,0:T(8,128)}) %tuple.69, (s32[]{:T(128)}, s32[20]{0:T(128)S(1)}, s32[]{:T(128)}, ...), branch_computations={%region_2.1_spmd, %region_3.4_spmd} | conditional | flops 826809344 | bytes 49490116 | solution.py:324
  249.7 2.6 copy-done.9
  253.9 6.5 %multiply_add_fusion = f32[6,512,128]{2,1,0:T(8,128)} fusion(f32[6,512,128]{2,1,0:T(8,128)} %get-tuple-element.215, f32[512,512,6]{1,0,2:T(8,128)} %copy-done.9, f32[6,512]{1,0:T(8,128)S(1)} %max.2, pred[512,512]{0,1:T(8,128)(4,1)S(1)} %broadcast_compare_fusion, f32[6,512]{1,0:T(8,128)S(1)} %get-tuple-element.387, ...), kind=kOutput, calls=%fused_computation.8 | convolution fusion | flops 411303936 | bytes 9854984 | tf_op jit(solution)/shard_map/cond/branch_0_fun/while/body/eval_jaxpr/cond/branch_1_fun/grs,sd->grd/dot_general | solution.py:319
  264.3 14.6 %conditional.5 = ((f32[6,512]{1,0:T(8,128)S(1)}, f32[6,512]{1,0:T(8,128)S(1)}, f32[6,512,128]{2,1,0:T(8,128)})) conditional(s32[]{:T(128)} %convert_element_type.35, (f32[6,512]{1,0:T(8,128)S(1)}, f32[6,512]{1,0:T(8,128)S(1)}, f32[6,512,128]{2,1,0:T(8,128)}) %tuple.69, (s32[]{:T(128)}, s32[20]{0:T(128)S(1)}, s32[]{:T(128)}, ...), branch_computations={%region_2.1_spmd, %region_3.4_spmd} | conditional | flops 826809344 | bytes 49490116 | solution.py:324
  268.2 2.6 copy-done.9
  272.4 6.5 %multiply_add_fusion = f32[6,512,128]{2,1,0:T(8,128)} fusion(f32[6,512,128]{2,1,0:T(8,128)} %get-tuple-element.215, f32[512,512,6]{1,0,2:T(8,128)} %copy-done.9, f32[6,512]{1,0:T(8,128)S(1)} %max.2, pred[512,512]{0,1:T(8,128)(4,1)S(1)} %broadcast_compare_fusion, f32[6,512]{1,0:T(8,128)S(1)} %get-tuple-element.387, ...), kind=kOutput, calls=%fused_computation.8 | convolution fusion | flops 411303936 | bytes 9854984 | tf_op jit(solution)/shard_map/cond/branch_0_fun/while/body/eval_jaxpr/cond/branch_1_fun/grs,sd->grd/dot_general | solution.py:319
  280.2 14.6 %conditional.5 = ((f32[6,512]{1,0:T(8,128)S(1)}, f32[6,512]{1,0:T(8,128)S(1)}, f32[6,512,128]{2,1,0:T(8,128)})) conditional(s32[]{:T(128)} %convert_element_type.35, (f32[6,512]{1,0:T(8,128)S(1)}, f32[6,512]{1,0:T(8,128)S(1)}, f32[6,512,128]{2,1,0:T(8,128)}) %tuple.69, (s32[]{:T(128)}, s32[20]{0:T(128)S(1)}, s32[]{:T(128)}, ...), branch_computations={%region_2.1_spmd, %region_3.4_spmd} | conditional | flops 826809344 | bytes 49490116 | solution.py:324
  281.7 2.4 fusion.2
  284.1 2.6 copy-done.9
  288.3 6.5 %multiply_add_fusion = f32[6,512,128]{2,1,0:T(8,128)} fusion(f32[6,512,128]{2,1,0:T(8,128)} %get-tuple-element.215, f32[512,512,6]{1,0,2:T(8,128)} %copy-done.9, f32[6,512]{1,0:T(8,128)S(1)} %max.2, pred[512,512]{0,1:T(8,128)(4,1)S(1)} %broadcast_compare_fusion, f32[6,512]{1,0:T(8,128)S(1)} %get-tuple-element.387, ...), kind=kOutput, calls=%fused_computation.8 | convolution fusion | flops 411303936 | bytes 9854984 | tf_op jit(solution)/shard_map/cond/branch_0_fun/while/body/eval_jaxpr/cond/branch_1_fun/grs,sd->grd/dot_general | solution.py:319
  296.1 14.6 %conditional.5 = ((f32[6,512]{1,0:T(8,128)S(1)}, f32[6,512]{1,0:T(8,128)S(1)}, f32[6,512,128]{2,1,0:T(8,128)})) conditional(s32[]{:T(128)} %convert_element_type.35, (f32[6,512]{1,0:T(8,128)S(1)}, f32[6,512]{1,0:T(8,128)S(1)}, f32[6,512,128]{2,1,0:T(8,128)}) %tuple.69, (s32[]{:T(128)}, s32[20]{0:T(128)S(1)}, s32[]{:T(128)}, ...), branch_computations={%region_2.1_spmd, %region_3.4_spmd} | conditional | flops 826809344 | bytes 49490116 | solution.py:324
  300.0 2.6 copy-done.9
  304.2 6.5 %multiply_add_fusion = f32[6,512,128]{2,1,0:T(8,128)} fusion(f32[6,512,128]{2,1,0:T(8,128)} %get-tuple-element.215, f32[512,512,6]{1,0,2:T(8,128)} %copy-done.9, f32[6,512]{1,0:T(8,128)S(1)} %max.2, pred[512,512]{0,1:T(8,128)(4,1)S(1)} %broadcast_compare_fusion, f32[6,512]{1,0:T(8,128)S(1)} %get-tuple-element.387, ...), kind=kOutput, calls=%fused_computation.8 | convolution fusion | flops 411303936 | bytes 9854984 | tf_op jit(solution)/shard_map/cond/branch_0_fun/while/body/eval_jaxpr/cond/branch_1_fun/grs,sd->grd/dot_general | solution.py:319
  312.0 14.6 %conditional.5 = ((f32[6,512]{1,0:T(8,128)S(1)}, f32[6,512]{1,0:T(8,128)S(1)}, f32[6,512,128]{2,1,0:T(8,128)})) conditional(s32[]{:T(128)} %convert_element_type.35, (f32[6,512]{1,0:T(8,128)S(1)}, f32[6,512]{1,0:T(8,128)S(1)}, f32[6,512,128]{2,1,0:T(8,128)}) %tuple.69, (s32[]{:T(128)}, s32[20]{0:T(128)S(1)}, s32[]{:T(128)}, ...), branch_computations={%region_2.1_spmd, %region_3.4_spmd} | conditional | flops 826809344 | bytes 49490116 | solution.py:324
  315.9 2.6 copy-done.9
  320.1 6.5 %multiply_add_fusion = f32[6,512,128]{2,1,0:T(8,128)} fusion(f32[6,512,128]{2,1,0:T(8,128)} %get-tuple-element.215, f32[512,512,6]{1,0,2:T(8,128)} %copy-done.9, f32[6,512]{1,0:T(8,128)S(1)} %max.2, pred[512,512]{0,1:T(8,128)(4,1)S(1)} %broadcast_compare_fusion, f32[6,512]{1,0:T(8,128)S(1)} %get-tuple-element.387, ...), kind=kOutput, calls=%fused_computation.8 | convolution fusion | flops 411303936 | bytes 9854984 | tf_op jit(solution)/shard_map/cond/branch_0_fun/while/body/eval_jaxpr/cond/branch_1_fun/grs,sd->grd/dot_general | solution.py:319
  327.9 14.6 %conditional.5 = ((f32[6,512]{1,0:T(8,128)S(1)}, f32[6,512]{1,0:T(8,128)S(1)}, f32[6,512,128]{2,1,0:T(8,128)})) conditional(s32[]{:T(128)} %convert_element_type.35, (f32[6,512]{1,0:T(8,128)S(1)}, f32[6,512]{1,0:T(8,128)S(1)}, f32[6,512,128]{2,1,0:T(8,128)}) %tuple.69, (s32[]{:T(128)}, s32[20]{0:T(128)S(1)}, s32[]{:T(128)}, ...), branch_computations={%region_2.1_spmd, %region_3.4_spmd} | conditional | flops 826809344 | bytes 49490116 | solution.py:324
  331.8 2.6 copy-done.9
  336.0 6.5 %multiply_add_fusion = f32[6,512,128]{2,1,0:T(8,128)} fusion(f32[6,512,128]{2,1,0:T(8,128)} %get-tuple-element.215, f32[512,512,6]{1,0,2:T(8,128)} %copy-done.9, f32[6,512]{1,0:T(8,128)S(1)} %max.2, pred[512,512]{0,1:T(8,128)(4,1)S(1)} %broadcast_compare_fusion, f32[6,512]{1,0:T(8,128)S(1)} %get-tuple-element.387, ...), kind=kOutput, calls=%fused_computation.8 | convolution fusion | flops 411303936 | bytes 9854984 | tf_op jit(solution)/shard_map/cond/branch_0_fun/while/body/eval_jaxpr/cond/branch_1_fun/grs,sd->grd/dot_general | solution.py:319
  343.8 14.6 %conditional.5 = ((f32[6,512]{1,0:T(8,128)S(1)}, f32[6,512]{1,0:T(8,128)S(1)}, f32[6,512,128]{2,1,0:T(8,128)})) conditional(s32[]{:T(128)} %convert_element_type.35, (f32[6,512]{1,0:T(8,128)S(1)}, f32[6,512]{1,0:T(8,128)S(1)}, f32[6,512,128]{2,1,0:T(8,128)}) %tuple.69, (s32[]{:T(128)}, s32[20]{0:T(128)S(1)}, s32[]{:T(128)}, ...), branch_computations={%region_2.1_spmd, %region_3.4_spmd} | conditional | flops 826809344 | bytes 49490116 | solution.py:324
  347.7 2.6 copy-done.9
  351.8 6.5 %multiply_add_fusion = f32[6,512,128]{2,1,0:T(8,128)} fusion(f32[6,512,128]{2,1,0:T(8,128)} %get-tuple-element.215, f32[512,512,6]{1,0,2:T(8,128)} %copy-done.9, f32[6,512]{1,0:T(8,128)S(1)} %max.2, pred[512,512]{0,1:T(8,128)(4,1)S(1)} %broadcast_compare_fusion, f32[6,512]{1,0:T(8,128)S(1)} %get-tuple-element.387, ...), kind=kOutput, calls=%fused_computation.8 | convolution fusion | flops 411303936 | bytes 9854984 | tf_op jit(solution)/shard_map/cond/branch_0_fun/while/body/eval_jaxpr/cond/branch_1_fun/grs,sd->grd/dot_general | solution.py:319
  361.0 3.1 copy.14
  372.1 2.9 collective-permute-start.17
  (279 shorter events, 123.3 us)
Async XLA Ops:
  1.9 1.9 collective-permute-start
  4.6 17.0 %collective-permute-start.3 = (bf16[1024,256]{1,0:T(8,128)(2,1)}, bf16[1024,256]{1,0:T(8,128)(2,1)S(1)}, u32[]{:S(2)}, u32[]{:S(2)}) collective-permute-start(bf16[1024,256]{1,0:T(8,128)(2,1)} %pad_maximum_fusion), channel_id=1, source_target_pairs={{0,32},{16,48},{32,64},{48,80},{64,96},{80,112},{8,104},{24,120},{... | collective-permute-start | bytes 1572872 | tf_op jit(solution)/shard_map/ppermute | solution.py:385
  5.9 25.0 %collective-permute-start.1 = (bf16[512,256]{1,0:T(8,128)(2,1)S(1)}, bf16[512,256]{1,0:T(8,128)(2,1)S(1)}, u32[]{:S(2)}, u32[]{:S(2)}) collective-permute-start(bf16[512,256]{1,0:T(8,128)(2,1)S(1)} %constant_dynamic-update-slice_fusion.12.refs_1_), channel_id=1, source_target_pairs={{0,16},{8,24},{16,0},{24,8},{32,48},{40,56},{64,80},{72,88},{96,11... | collective-permute-start | bytes 786440 | tf_op jit(solution)/shard_map/ppermute | solution.py:385
  7.2 30.1 %collective-permute-start.7 = (bf16[1024,256]{1,0:T(8,128)(2,1)}, bf16[1024,256]{1,0:T(8,128)(2,1)}, u32[]{:S(2)}, u32[]{:S(2)}) collective-permute-start(bf16[1024,256]{1,0:T(8,128)(2,1)} %pad_maximum_fusion), channel_id=1, source_target_pairs={{8,72},{24,88},{40,104},{56,120},{9,73},{25,89},{41,105},{57,121},... | collective-permute-start | bytes 1572872 | tf_op jit(solution)/shard_map/ppermute | solution.py:385
  21.6 17.8 %copy-start.11 = (bf16[1024,256]{1,0:T(8,128)(2,1)}, bf16[1024,256]{1,0:T(8,128)(2,1)S(1)}, u32[]{:S(2)}) copy-start(bf16[1024,256]{1,0:T(8,128)(2,1)S(1)} %collective-permute-done.3.refs_5_) | copy-start | bytes 1572868
  21.6 17.7 %collective-permute-start.4 = (bf16[1024,256]{1,0:T(8,128)(2,1)S(1)}, bf16[1024,256]{1,0:T(8,128)(2,1)}, u32[]{:S(2)}, u32[]{:S(2)}) collective-permute-start(bf16[1024,256]{1,0:T(8,128)(2,1)S(1)} %collective-permute-done.3.refs_5_), channel_id=1, source_target_pairs={{0,8},{8,0},{16,24},{24,16},{32,40},{40,32},{48,56},{56,48},{64,72... | collective-permute-start | bytes 1572872 | tf_op jit(solution)/shard_map/ppermute | solution.py:385
  21.6 1.3 copy-start
  22.9 1.1 copy-start.1
  24.0 1.1 copy-start.2
  25.2 0.7 copy-start.4
  25.9 13.5 %copy-start.10 = (bf16[512,768]{1,0:T(8,128)(2,1)S(1)}, bf16[512,768]{1,0:T(8,128)(2,1)}, u32[]{:S(2)}) copy-start(bf16[512,768]{1,0:T(8,128)(2,1)} %refs_0_.3) | copy-start | bytes 2359300
  29.4 1.2 copy-start.7
  30.6 1.7 collective-permute-start.5
  30.9 8.4 %collective-permute-start.2 = (bf16[512,256]{1,0:T(8,128)(2,1)S(1)}, bf16[512,256]{1,0:T(8,128)(2,1)S(1)}, u32[]{:S(2)}, u32[]{:S(2)}) collective-permute-start(bf16[512,256]{1,0:T(8,128)(2,1)S(1)} %collective-permute-done.1.refs_3_), channel_id=1, source_target_pairs={{0,8},{8,0},{16,24},{24,16},{32,40},{40,32},{48,56},{56,48},{64,72... | collective-permute-start | bytes 786440 | tf_op jit(solution)/shard_map/ppermute | solution.py:385
  32.4 25.0 %collective-permute-start.6 = (f32[776,128]{1,0:T(8,128)S(1)}, f32[776,128]{1,0:T(8,128)S(1)}, u32[]{:S(2)}, u32[]{:S(2)}) collective-permute-start(f32[776,128]{1,0:T(8,128)S(1)} %join.2.own_ref), channel_id=1, source_target_pairs={{0,16},{8,24},{16,0},{24,8},{32,48},{40,56},{48,32},{56,40},{64,80... | collective-permute-start | bytes 1191944 | tf_op jit(solution)/shard_map/ppermute | solution.py:385
  32.5 24.9 %collective-permute-start.8 = (bf16[1024,256]{1,0:T(8,128)(2,1)S(1)}, bf16[1024,256]{1,0:T(8,128)(2,1)}, u32[]{:S(2)}, u32[]{:S(2)}) collective-permute-start(bf16[1024,256]{1,0:T(8,128)(2,1)S(1)} %collective-permute-done.3.refs_5_), channel_id=1, source_target_pairs={{32,48},{48,32},{64,80},{80,64},{96,112},{104,120},{112,96},{120,1... | collective-permute-start | bytes 1572872 | tf_op jit(solution)/shard_map/ppermute | solution.py:385
  37.3 24.5 %collective-permute-start.9 = (bf16[1024,256]{1,0:T(8,128)(2,1)}, bf16[1024,256]{1,0:T(8,128)(2,1)}, u32[]{:S(2)}, u32[]{:S(2)}) collective-permute-start(bf16[1024,256]{1,0:T(8,128)(2,1)} %collective-permute-done.7.refs_4_), channel_id=1, source_target_pairs={{72,88},{88,72},{104,120},{120,104},{73,89},{89,73},{105,121},{121... | collective-permute-start | bytes 1572872 | tf_op jit(solution)/shard_map/ppermute | solution.py:385
  39.3 18.0 %copy-start.14 = (bf16[512,256]{1,0:T(8,128)(2,1)}, bf16[512,256]{1,0:T(8,128)(2,1)S(1)}, u32[]{:S(2)}) copy-start(bf16[512,256]{1,0:T(8,128)(2,1)S(1)} %collective-permute-done.2.refs_4_) | copy-start | bytes 786436
  61.9 3.2 collective-permute-start.10
  61.9 3.2 collective-permute-start.11
  62.4 3.2 collective-permute-start.12
  62.4 22.7 %collective-permute-start.13 = (f32[776,128]{1,0:T(8,128)S(1)}, f32[776,128]{1,0:T(8,128)S(1)}, u32[]{:S(2)}, u32[]{:S(2)}) collective-permute-start(f32[776,128]{1,0:T(8,128)S(1)} %join.3), channel_id=1, source_target_pairs={{0,32},{16,48},{32,64},{48,80},{64,96},{80,112},{8,104},{24,120},{... | collective-permute-start | bytes 1191944 | tf_op jit(solution)/shard_map/ppermute | solution.py:385
  63.7 21.4 %collective-permute-start.14 = (f32[776,128]{1,0:T(8,128)S(1)}, f32[776,128]{1,0:T(8,128)S(1)}, u32[]{:S(2)}, u32[]{:S(2)}) collective-permute-start(f32[776,128]{1,0:T(8,128)S(1)} %join.3), channel_id=1, source_target_pairs={{8,72},{24,88},{40,104},{56,120},{9,73},{25,89},{41,105},{57,121},... | collective-permute-start | bytes 1191944 | tf_op jit(solution)/shard_map/ppermute | solution.py:385
  65.1 20.1 %copy-start.12 = (bf16[1024,256]{1,0:T(8,128)(2,1)}, bf16[1024,256]{1,0:T(8,128)(2,1)S(1)}, u32[]{:S(2)}) copy-start(bf16[1024,256]{1,0:T(8,128)(2,1)S(1)} %collective-permute-done.10.refs_5_) | copy-start | bytes 1572868
  85.2 289.7 %collective-permute-start.18 = (f32[776,128]{1,0:T(8,128)S(1)}, f32[776,128]{1,0:T(8,128)S(1)}, u32[]{:S(2)}, u32[]{:S(2)}) collective-permute-start(f32[776,128]{1,0:T(8,128)S(1)} %hand.1.kept_ref), channel_id=1, source_target_pairs={{0,8},{8,0},{16,24},{24,16},{32,40},{40,32},{48,56},{56,48},{64,72... | collective-permute-start | bytes 1191944 | tf_op jit(solution)/shard_map/ppermute | solution.py:385
  86.2 288.8 %copy-start.3 = (bf16[512,768]{1,0:T(8,128)(2,1)S(1)}, bf16[512,768]{1,0:T(8,128)(2,1)}, u32[]{:S(2)}) copy-start(bf16[512,768]{1,0:T(8,128)(2,1)} %query_ref.1) | copy-start | bytes 2359300
  86.2 288.8 %copy-start.5 = (f32[768]{0:T(1024)S(1)}, f32[768]{0:T(1024)}, u32[]{:S(2)}) copy-start(f32[768]{0:T(1024)} %gain_ref.2) | copy-start | bytes 9220
  86.6 4.4 %copy-start.13 = (bf16[1024,256]{1,0:T(8,128)(2,1)S(1)}, bf16[1024,256]{1,0:T(8,128)(2,1)}, u32[]{:S(2)}) copy-start(bf16[1024,256]{1,0:T(8,128)(2,1)} %get-tuple-element.237) | copy-start | bytes 1572868 | tf_op jit(solution)/shard_map/cond
  95.3 2.3 copy-start.15
  106.7 2.6 copy-start.9
  122.6 2.6 copy-start.9
  138.5 2.6 copy-start.9
  154.4 2.6 copy-start.9
  170.3 2.6 copy-start.9
  186.2 2.6 copy-start.9
  202.0 2.6 copy-start.9
  217.9 2.6 copy-start.9
  233.8 2.6 copy-start.9
  249.7 2.6 copy-start.9
  268.2 2.6 copy-start.9
  284.1 2.6 copy-start.9
  300.0 2.6 copy-start.9
  315.9 2.6 copy-start.9
  331.8 2.6 copy-start.9
  347.7 2.6 copy-start.9
  366.9 10.9 %copy-start.6 = (f32[768]{0:T(1024)S(1)}, f32[768]{0:T(1024)}, u32[]{:S(2)}) copy-start(f32[768]{0:T(1024)} %gain_ref.3) | copy-start | bytes 9220
  366.9 2.6 collective-permute-start.15
  369.5 2.6 collective-permute-start.16
  372.1 5.7 %collective-permute-start.17 = (f32[8,512]{1,0:T(8,128)S(1)}, f32[8,512]{1,0:T(8,128)S(1)}, u32[]{:S(2)}, u32[]{:S(2)}) collective-permute-start(f32[8,512]{1,0:T(8,128)S(1)} %add.97.square_ref), channel_id=1, source_target_pairs={{0,4},{1,5},{2,6},{3,7},{4,0},{5,1},{6,2},{7,3},{8,12},{9,13},{10,... | collective-permute-start | bytes 49160 | tf_op jit(solution)/shard_map/ppermute | solution.py:485
  375.0 1.4 copy-start.8
  376.4 1.3 copy-start.16
